TPU v7x, 256 devices: a whole 4x4x8 slice. The times are simulated.
256 devices in a mesh: sub: 2 (over z_hi), row: 8 (over x, core), col: 16 (over z_lo, y).
Axes of the slice: x: 4, y: 4, z: 8 (z_hi: 2, z_lo: 4; z = z_hi * 4 + z_lo), core: 2. Of those that a mesh axis runs over, the one named last changes fastest.
Arguments:
- panel: float32 [65536, 512], P(('sub', 'row', 'col')), as said below
- trailing: float32 [65536, 4096], P(('sub', 'row'), 'col'), may hold values from -6 to 6
- child: float32 [2, 16384, 4096], P('sub', 'row', 'col'), may hold values from -6 to 6
- child_map: int32 [2, 64], P('sub', 'row'), may hold values from 0 to 31, as said below
- pattern: int32 [256, 16], P(('sub', 'row'), 'col'), may hold values from 0 to 1
Outputs:
- factor: float32 [65536, 512], P(('sub', 'row', 'col'))
- updated: float32 [65536, 4096], P(('sub', 'row'), 'col')
Inputs may be any that keep to these rules, and one draw needn't show every extreme that they name: `child_map`: the child block rows held by one index of row map to distinct slots; slot v means half v // 16 of sub and block v % 16 of that row index's block rows. The last entry of each such run of 8 is 16 * 2 - 1. `panel`: rows 0 to 511 form a symmetric positive definite block.
All inputs are finite; a program needn't handle non-finite values.
Results may differ from a plain program's by a relative error of at most 0.00007.
Values sent between devices are 32-bit elements; how exact they have to be, the bound alone decides.
No kernel may reach another device: no remote copies, remote signals or barrier semaphores. Data moves between devices by JAX's collectives and lax.ppermute only.
A program may use at most 128 MiB of HBM per device.

v0:
```python
import jax
import jax.numpy as jnp
from jax import lax
from jax.sharding import PartitionSpec as P


def from_root(x, axis, root):
    mine = lax.axis_index(axis) == root
    return lax.psum(jnp.where(mine, x, jnp.zeros_like(x)), axis)


def local(panel, trailing, child, child_map, pattern):
    shard_rows = panel.shape[0]
    panel_width = panel.shape[1]
    block_size = trailing.shape[1]
    pieces = max(1, panel_width // shard_rows)
    pivot_pieces = []
    for number in range(pieces):
        pivot_pieces.append(from_root(panel, ("sub", "row", "col"), number))
    pivot_top = jnp.concatenate(pivot_pieces, axis=0)
    lower_factor = jnp.linalg.cholesky(pivot_top)
    identity = jnp.eye(panel_width, dtype=jnp.float32)
    inverse = jax.scipy.linalg.solve_triangular(lower_factor, identity, lower=True)
    inverse_t = inverse.T
    col_index = lax.axis_index("col")
    group_rows = jnp.dot(
        lax.all_gather(panel, "col", axis=0, tiled=True),
        inverse_t,
        precision=lax.Precision.HIGHEST,
        preferred_element_type=jnp.float32,
    )
    own_rows = lax.dynamic_slice_in_dim(group_rows, col_index * shard_rows, shard_rows, 0)
    group_count = group_rows.shape[0]
    row_blocks = group_count // block_size
    first_row = panel_width + col_index * block_size
    owner = first_row // group_count
    in_owner = first_row % group_count
    candidate = lax.dynamic_slice_in_dim(group_rows, in_owner, block_size, 0)
    window = from_root(candidate, ("sub", "row"), owner)
    window_t = window.T
    sub_count = lax.axis_size("sub")
    child_blocks = child_map.shape[1]
    all_child, all_map = (
        lax.all_gather(child, "sub", axis=0, tiled=True),
        lax.all_gather(child_map, "sub", axis=0, tiled=True),
    )
    sub_index = lax.axis_index("sub")
    own_slots = sub_index * row_blocks + jnp.arange(row_blocks, dtype=jnp.int32)
    onehot = (own_slots[:, None] == all_map.reshape(1, sub_count * child_blocks)).astype(
        jnp.float32
    )
    child_flat = all_child.reshape(sub_count * child_blocks, block_size * block_size)
    extend = jnp.dot(
        onehot, child_flat, precision=lax.Precision.HIGHEST, preferred_element_type=jnp.float32
    )
    extend = extend.reshape(row_blocks * block_size, block_size)
    assembled = trailing + extend
    update = jnp.dot(
        group_rows, window_t, precision=lax.Precision.HIGHEST, preferred_element_type=jnp.float32
    )
    present = pattern[:, 0].astype(jnp.float32)
    masked = (update.reshape(row_blocks, block_size, block_size) * present[:, None, None]).reshape(
        group_count, block_size
    )
    updated = assembled - masked
    return (own_rows, updated)


def solution(mesh):
    return jax.shard_map(
        local,
        mesh=mesh,
        in_specs=(
            P(("sub", "row", "col"), None),
            P(("sub", "row"), "col"),
            P("sub", "row", "col"),
            P("sub", "row"),
            P(("sub", "row"), "col"),
        ),
        out_specs=(P(("sub", "row", "col"), None), P(("sub", "row"), "col")),
        check_vma=False,
    )
```

profile of v0, /device:TPU:1, one launch (start us, length us, event | category | flops | bytes accessed | tf_op | source)
XLA Modules:
  0.0 691.0 jit_solution(3431088338734765414)
XLA Ops:
  7.2 1.2 copy.11
  11.3 9.3 %all-gather = s32[2,1,8]{2,1,0:T(1,128)S(1)} all-gather(s32[1,1,8]{2,1,0:T(1,128)S(1)} %bitcast.63), channel_id=1, replica_groups=mesh['sub'=2,'row'=8,'col'=16] {'sub'}, dimensions={0}, use_global_device_ids=true | all-gather | bytes 96 | tf_op jit(solution)/shard_map/all_gather | solution.py:45
  21.9 250.8 %all-reduce.7.cloned.1.call-done = (f32[256,512]{0,1:T(8,128)}, f32[256,512]{0,1:T(8,128)}) async-done(((f32[256,512]{0,1:T(8,128)}, f32[256,512]{0,1:T(8,128)}), (f32[256,512]{0,1:T(8,128)}, f32[256,512]{0,1:T(8,128)})) %all-reduce.7.cloned.1.call-update) | async-done | bytes 1048592 | tf_op jit(solution)/shard_map/psum | solution.py:9
  272.7 1.1 constant_dynamic-update-slice_fusion.1
  273.8 1.1 constant_dynamic-update-slice_fusion
  276.5 11.7 %cholesky.104 = f32[128,128]{1,0:T(8,128)S(1)} custom-call(f32[128,128]{1,0:T(8,128)S(1)} %cholesky.266), custom_call_target="Cholesky" | custom-call | tf_op jit(solution)/shard_map/jit(cholesky)/cholesky | solution.py:21
  288.4 9.8 %custom-call.31 = f32[1,128,128]{1,2,0:T(8,128)S(1)} custom-call(f32[1,128,128]{2,1,0:T(8,128)S(1)} %get-tuple-element.39), custom_call_target="InvertDiagBlocksLowerTriangular" | custom-call | tf_op jit(solution)/shard_map/jit(cholesky)/cholesky | solution.py:21
  298.2 1.2 constant_dynamic-update-slice_fusion.4
  299.4 1.3 convolution_subtract_fusion.3
  300.7 11.7 %cholesky.217 = f32[128,128]{1,0:T(8,128)S(1)} custom-call(f32[128,128]{1,0:T(8,128)S(1)} %cholesky.270), custom_call_target="Cholesky" | custom-call | tf_op jit(solution)/shard_map/jit(cholesky)/cholesky | solution.py:21
  312.5 10.0 %custom-call.32 = f32[1,128,128]{1,2,0:T(8,128)S(1)} custom-call(f32[1,128,128]{2,1,0:T(8,128)S(1)} %get-tuple-element.36), custom_call_target="InvertDiagBlocksLowerTriangular" | custom-call | tf_op jit(solution)/shard_map/jit(cholesky)/cholesky | solution.py:21
  322.7 1.3 convolution_subtract_fusion.4
  324.0 11.7 %cholesky.238 = f32[128,128]{1,0:T(8,128)S(1)} custom-call(f32[128,128]{1,0:T(8,128)S(1)} %cholesky.275), custom_call_target="Cholesky" | custom-call | tf_op jit(solution)/shard_map/jit(cholesky)/cholesky | solution.py:21
  336.4 9.8 %custom-call.33 = f32[1,128,128]{1,2,0:T(8,128)S(1)} custom-call(f32[1,128,128]{2,1,0:T(8,128)S(1)} %get-tuple-element.33), custom_call_target="InvertDiagBlocksLowerTriangular" | custom-call | tf_op jit(solution)/shard_map/jit(cholesky)/cholesky | solution.py:21
  346.4 1.2 convolution_subtract_fusion.5
  347.7 11.7 %cholesky.255 = f32[128,128]{1,0:T(8,128)S(1)} custom-call(f32[128,128]{1,0:T(8,128)S(1)} %convolution_subtract_fusion.5), custom_call_target="Cholesky" | custom-call | tf_op jit(solution)/shard_map/jit(cholesky)/cholesky | solution.py:21
  363.6 10.4 %while.1 = (s32[]{:T(128)}, f32[512,512]{1,0:T(8,128)S(1)}, s32[4,2]{0,1:T(2,128)S(1)}, f32[4,128,128]{2,1,0:T(8,128)}, s32[]{:T(128)}) while((s32[]{:T(128)}, f32[512,512]{1,0:T(8,128)S(1)}, s32[4,2]{0,1:T(2,128)S(1)}, f32[4,128,128]{2,1,0:T(8,128)}, s32[]{:T(128)}) %tuple.35), condition=%wide.while_cond, body=%wide.while_body.sunk | while | flops 2 | bytes 132705 | solution.py:23
  364.2 2.0 bitcast_dynamic-update-slice_fusion.2
  366.8 2.0 bitcast_dynamic-update-slice_fusion.2
  369.4 2.0 bitcast_dynamic-update-slice_fusion.2
  372.0 2.0 bitcast_dynamic-update-slice_fusion.2
  374.0 40.1 %custom-call.34 = f32[4,128,128]{1,2,0:T(8,128)S(1)} custom-call(f32[4,128,128]{2,1,0:T(8,128)} %get-tuple-element.9), custom_call_target="InvertDiagBlocksLowerTriangular" | custom-call | tf_op jit(solution)/shard_map/jit(_solve_triangular)/triangular_solve | solution.py:23
  415.7 1.3 fusion.30
  417.6 1.3 fusion.29
  418.9 16.7 %fusion.1 = f32[512,4096]{1,0:T(8,128)S(1)} fusion(f32[4096,512]{1,0:T(8,128)} %all-gather.4.cloned.1.call-done, f32[128,512]{1,0:T(8,128)S(1)} %fusion.29, f32[128,512]{1,0:T(8,128)S(1)} %fusion.30, f32[128,512]{1,0:T(8,128)S(1)} %fusion.32, f32[128,512]{1,0:T(8,128)S(1)} %fusion.20), kind=kOutput, calls=%fused_computation.13 | convolution fusion | flops 12885688320 | bytes 17825792 | tf_op jit(solution)/shard_map/dot_general | solution.py:26
  435.7 3.2 copy-done
  439.9 48.6 %all-gather.6.cloned.1.call-done = f32[2,2048,256]{2,1,0:T(8,128)} async-done(((f32[1,2048,256]{2,1,0:T(8,128)}), f32[2,2048,256]{2,1,0:T(8,128)}) %all-gather.6.cloned.1.call-update) | async-done | bytes 4194320 | tf_op jit(solution)/shard_map/all_gather | solution.py:44
  488.5 4.0 reshape.64
  492.5 6.3 fusion.38
  498.8 3.9 reshape.65
  503.7 160.9 %all-reduce.5.cloned.1.call-done = f32[256,512]{0,1:T(8,128)} async-done(((f32[256,512]{0,1:T(8,128)}), f32[256,512]{0,1:T(8,128)}) %all-reduce.5.cloned.1.call-update) | async-done | bytes 524304 | tf_op jit(solution)/shard_map/psum | solution.py:9
  664.6 19.4 %fusion = f32[4096,256]{1,0:T(8,128)} fusion(f32[512,4096]{1,0:T(8,128)} %copy-done, f32[256,512]{0,1:T(8,128)} %all-reduce.5.cloned.1.call-done, f32[4096,256]{1,0:T(8,128)} %param.6, f32[4096,256]{1,0:T(8,128)} %reshape.65, f32[4096]{0:T(1024)S(1)} %bitcast.62), kind=kOutput, calls=%fused_computation.3 | convolution fusion | flops 6445596672 | bytes 21512192 | tf_op jit(solution)/shard_map/dot_general | solution.py:58
  (62 shorter events, 15.1 us)
Async XLA Ops:
  7.2 4.2 copy-start.3
  7.2 14.6 %copy-start.4 = (s32[16,1]{0,1:T(1,128)S(1)}, s32[16,1]{0,1:T(1,128)}, u32[]{:S(2)}) copy-start(s32[16,1]{0,1:T(1,128)} %param.9) | copy-start | bytes 196
  7.2 265.5 %all-reduce.7.cloned.1.call-start = ((), (), s32[]{:S(2)}) async-start(), calls=%async_computation.3 | async-start | bytes 2097152 | tf_op jit(solution)/shard_map/psum | solution.py:9
  9.6 409.4 %all-gather.4.cloned.1.call-start = ((), (), s32[]{:S(2)}) async-start(), calls=%async_computation | async-start | bytes 8912896 | tf_op jit(solution)/shard_map/all_gather | solution.py:27
  10.3 478.2 %all-gather.6.cloned.1.call-start = ((), (), s32[]{:S(2)}) async-start(), calls=%async_computation.1 | async-start | bytes 6291456 | tf_op jit(solution)/shard_map/all_gather | solution.py:44
  11.0 653.6 %all-reduce.5.cloned.1.call-start = ((), (), s32[]{:S(2)}) async-start(), calls=%async_computation.2 | async-start | bytes 1048576 | tf_op jit(solution)/shard_map/psum | solution.py:9
  275.5 1.0 copy-start.1
  414.1 0.7 copy-start.2
  435.7 3.2 copy-start
Sparse Core Ops, SparseCore 0:
  14.2 258.4 all-reduce.6
  274.6 102.7 all-gather.3
  379.3 109.1 all-gather.5
  491.1 173.4 all-reduce.4
where the time goes:
time: 701 us; the launch traced here: 691 us
  waiting for transfers between devices  462 us (66%)
  other arithmetic  122 us (17%)
  matrix products  52.6 us (8%)
  local copies, waits for them, and re-layouts  28.1 us (4%)
  between operations  17.1 us (2%)
  blocking collectives  9.32 us (1%)
    psum x2, waiting for transfers between devices, from_root(): return lax.psum(jnp.where(mine, x, jnp.zeros_like(x)), axis)  412 us
    another operation x14, other arithmetic, local(): lower_factor = jnp.linalg.cholesky(pivot_top)  78.7 us
    all_gather x1, waiting for transfers between devices, local(): lax.all_gather(child, 'sub', axis=0, tiled=True)  48.6 us
    another operation x3, other arithmetic, local(): jax.scipy.linalg.solve_triangular(lower_factor, identity, lower=True)  40.3 us
    dot_general x1, matrix products, local(): jnp.dot(group_rows, window_t, precision=lax.Precision.HIGHEST, preferred_...  19.4 us
    dot_general x1, matrix products, local(): jnp.dot(lax.all_gather(panel, 'col', axis=0, tiled=True), inverse_t, prec...  16.7 us
  transfers between devices with their start and end apart: 4, of which 3 were waited for; matrix products, arithmetic and copies ran while one was open for 26% of the time, Pallas kernels for 0%

commit v1 on v0

v1 whole, which is shorter than its diff:
```python
import jax
import jax.numpy as jnp
from jax import lax
from jax.experimental import pallas as pl
from jax.experimental.pallas import tpu as pltpu
from jax.sharding import PartitionSpec as P

HI = lax.Precision.HIGHEST
ALL = ("sub", "row", "col")
SB = 128
NX, NY, NZ = 4, 4, 8


def linear(x, core, y, z):
    return (z // 4) * 128 + (x * 2 + core) * 16 + (z % 4) * 4 + y


def pairs_of(move):
    pairs = []
    for x in range(NX):
        for core in range(2):
            for y in range(NY):
                for z in range(NZ):
                    to = move(x, core, y, z)
                    if to is not None:
                        pairs.append((linear(x, core, y, z), linear(*to)))
    return pairs


def send(value, move):
    return lax.ppermute(value, ALL, pairs_of(move))


def contract(a, b, dim_a, dim_b):
    return lax.dot_general(
        a, b, (((dim_a,), (dim_b,)), ((), ())), precision=HI, preferred_element_type=jnp.float32
    )


def block_inverse(strips, group):
    lane = lax.broadcasted_iota(jnp.int32, (8, SB), 1)
    sublane = lax.broadcasted_iota(jnp.int32, (8, SB), 0)
    held = list(strips)
    count = len(held)
    for first in range(0, SB, group):
        own = first // 8
        columns = {}
        for t in range(own, count):
            columns[t] = [
                jnp.broadcast_to(held[t][:, first + m : first + m + 1], (8, SB)) for m in range(group)
            ]
        for m in range(group):
            r = first % 8 + m
            col = first + m
            tops = [jnp.broadcast_to(columns[own][k][r : r + 1, :], (8, SB)) for k in range(m, group)]
            inverse = 1.0 / tops[0]
            row = jnp.broadcast_to(held[own][r : r + 1, :], (8, SB))
            row = jnp.where(lane == col, 1.0, row)
            for t in range(own, count):
                scale = columns[t][m] * inverse
                if t == own:
                    if r == 7:
                        continue
                    scale = jnp.where(sublane > r, scale, 0.0)
                    held[t] = jnp.where((lane == col) & (sublane > r), -scale, held[t] - scale * row)
                else:
                    held[t] = jnp.where(lane == col, 0.0, held[t]) - scale * row
                for k in range(m + 1, group):
                    columns[t][k] = columns[t][k] - scale * tops[k - m]
    out = []
    for t in range(count):
        rows = sublane + 8 * t
        diagonal = jnp.sum(jnp.where(lane == rows, held[t], 0.0), axis=1, keepdims=True)
        unit = jnp.where(lane < rows, held[t], jnp.where(lane == rows, 1.0, 0.0))
        out.append(unit * lax.rsqrt(diagonal))
    return out


def pivot_kernel(parts_ref, inverse_ref, work, lower, diag):
    width = work.shape[0]
    half = width // 2
    left = parts_ref[0]
    right = parts_ref[1]
    work[...] = jnp.zeros_like(work)
    work[0:half, 0:half] = left[:, 0:half]
    work[half : half + SB, 0:half] = left[:, half : half + SB].T
    work[half:, half:] = right[:, 0:half]
    work[half + SB :, 0:SB] = right[0:SB, half:]
    work[half + SB :, SB:half] = right[SB:, half:]
    lower[...] = jnp.zeros_like(lower)
    inverse_ref[...] = jnp.zeros_like(inverse_ref)

    def step(k, carry):
        off = pl.multiple_of(k * SB, SB)
        strips = [work[pl.ds(off + 8 * t, 8), pl.ds(off, SB)] for t in range(SB // 8)]
        done = block_inverse(strips, 8)
        for t in range(SB // 8):
            diag[8 * t : 8 * t + 8, :] = done[t]
        inv = diag[...]
        below = contract(work[:, pl.ds(off, SB)], inv, 1, 1)
        rows = lax.broadcasted_iota(jnp.int32, (width, SB), 0)
        below = jnp.where(rows >= off + SB, below, 0.0)
        lower[:, pl.ds(off, SB)] = below
        work[...] = work[...] - contract(below, below, 1, 1)
        before = contract(lower[pl.ds(off, SB), :], inverse_ref[...], 1, 0)
        inverse_ref[pl.ds(off, SB), :] = -contract(inv, before, 1, 0)
        inverse_ref[pl.ds(off, SB), pl.ds(off, SB)] = inv
        return carry

    lax.fori_loop(0, width // SB, step, 0)


def pivot_inverse(parts):
    width = 2 * parts.shape[1]
    return pl.pallas_call(
        pivot_kernel,
        out_shape=jax.ShapeDtypeStruct((width, width), jnp.float32),
        scratch_shapes=[
            pltpu.VMEM((width, width), jnp.float32),
            pltpu.VMEM((width, width), jnp.float32),
            pltpu.VMEM((SB, SB), jnp.float32),
        ],
        compiler_params=pltpu.CompilerParams(vmem_limit_bytes=32 << 20),
    )(parts)


def solve_kernel(inverse_ref, panel_ref, window_ref, factor_ref, weight_ref):
    inverse = inverse_ref[...]
    factor_ref[...] = contract(panel_ref[...], inverse, 1, 1)
    weight_ref[...] = contract(contract(window_ref[...], inverse, 1, 1), inverse, 1, 0)


def solve(inverse, panel, window):
    shape = jax.ShapeDtypeStruct(panel.shape, jnp.float32)
    return pl.pallas_call(
        solve_kernel,
        out_shape=(shape, jax.ShapeDtypeStruct(window.shape, jnp.float32)),
        compiler_params=pltpu.CompilerParams(vmem_limit_bytes=32 << 20),
    )(inverse, panel, window)


def final_kernel(table, group_ref, weight_ref, trailing_ref, own_ref, other_ref, out_ref):
    i = pl.program_id(0)
    out_ref[...] = trailing_ref[...]

    @pl.when(table[1, i] == 1)
    def _():
        out_ref[...] += own_ref[...]

    @pl.when(table[3, i] == 1)
    def _():
        out_ref[...] += other_ref[...]

    @pl.when(table[5, i] == 1)
    def _():
        out_ref[...] -= contract(group_ref[...], weight_ref[...], 1, 1)


def final(table, group, weight, trailing, own, other):
    size = weight.shape[0]
    width = weight.shape[1]
    blocks = trailing.shape[0] // size
    square = lambda pick: pl.BlockSpec((size, size), pick)
    return pl.pallas_call(
        final_kernel,
        grid_spec=pltpu.PrefetchScalarGridSpec(
            num_scalar_prefetch=1,
            grid=(blocks,),
            in_specs=[
                pl.BlockSpec((size, width), lambda i, t: (t[4, i], 0)),
                pl.BlockSpec((size, width), lambda i, t: (0, 0)),
                square(lambda i, t: (i, 0)),
                square(lambda i, t: (t[0, i], 0)),
                square(lambda i, t: (t[2, i], 0)),
            ],
            out_specs=square(lambda i, t: (i, 0)),
        ),
        out_shape=jax.ShapeDtypeStruct(trailing.shape, jnp.float32),
        compiler_params=pltpu.CompilerParams(vmem_limit_bytes=32 << 20),
    )(table, group, weight, trailing, own, other)


def kept(has, index):
    blocks = has.shape[0]
    coded = jnp.where(has, jnp.arange(blocks, dtype=jnp.int32) * blocks + index, -1)
    place = jnp.arange(blocks)
    latest = jnp.max(jnp.where(place[None, :] <= place[:, None], coded[None, :], -1), axis=1)
    return jnp.where(latest >= 0, latest % blocks, 0)


def lookup(slots, base, blocks):
    match = slots[None, :] == base + jnp.arange(blocks, dtype=jnp.int32)[:, None]
    has = jnp.any(match, axis=1)
    index = jnp.argmax(match, axis=1).astype(jnp.int32)
    return kept(has, index), has.astype(jnp.int32)


def pivot_parts(panel, x, core, y, z):
    half = panel.shape[1] // 2
    packed = jnp.concatenate([panel[SB:, 0:SB], panel[SB:, SB:half]], axis=0)
    from_left = panel[:, : half + SB]
    from_right = jnp.concatenate([panel[:, half:], packed], axis=1)
    whole = jnp.where(y == 0, from_left, from_right)
    split = send(
        whole[SB:], lambda x, c, y, z: (x, 1, y, z) if x == 0 and c == 0 and z == 0 and y < 2 else None
    )
    held = jnp.where(core == 0, whole[:SB], split)

    orders = (
        (("z", 4), ("z", 2), ("z", 1), ("x", 2), ("x", 1), ("y", 2)),
        (("x", 2), ("x", 1), ("y", 2), ("z", 4), ("z", 2), ("z", 1)),
    )
    have = {(0, c, y, 0) for c in range(2) for y in range(2)}
    for number in range(len(orders[0])):
        targets = {}
        for place in sorted(have):
            axis, stride = orders[place[1]][number]
            where = "xcyz".index(axis)
            to = list(place)
            to[where] += stride
            targets[place] = tuple(to)
        got = send(held, lambda x, c, y, z: targets.get((x, c, y, z)))
        receives = False
        for c in range(2):
            axis, stride = orders[c][number]
            coordinate = {"x": x, "y": y, "z": z}[axis]
            receives = receives | ((core == c) & ((coordinate // stride) % 2 == 1))
        held = jnp.where(receives, got, held)
        have = have | set(targets.values())
    other = send(held, lambda x, c, y, z: (x, c, y ^ 1, z))
    left = jnp.where(y % 2 == 0, held, other)
    right = jnp.where(y % 2 == 0, other, held)
    mine = jnp.stack([left, right])
    theirs = send(mine, lambda x, c, y, z: (x, 1 - c, y, z))
    top = jnp.where(core == 0, mine, theirs)
    bottom = jnp.where(core == 0, theirs, mine)
    return jnp.concatenate([top, bottom], axis=1)


def window_rows(panel, x, core, z):
    place = {}
    for col in range(16):
        block = 2 + col
        place[(block // 16) * 16 + block % 16] = col
    held = lax.ppermute(panel, ALL, sorted(place.items()))
    got = send(held, lambda x, c, y, z: (x, c, y, z + 4) if x == 0 and c == 0 and z < 4 else None)
    held = jnp.where(z >= 4, got, held)
    got = send(held, lambda x, c, y, z: (2, c, y, z) if x == 0 and c == 0 else None)
    held = jnp.where(x == 2, got, held)
    got = send(held, lambda x, c, y, z: (x + 1, c, y, z) if x % 2 == 0 and c == 0 else None)
    held = jnp.where(x % 2 == 1, got, held)
    got = send(held, lambda x, c, y, z: (x, 1, y, z) if c == 0 else None)
    return jnp.where(core == 1, got, held)


def local(panel, trailing, child, child_map, pattern):
    size = trailing.shape[1]
    blocks = trailing.shape[0] // size
    sub = lax.axis_index("sub")
    row = lax.axis_index("row")
    col = lax.axis_index("col")
    x, core, y, z = row // 2, row % 2, col % NY, sub * 4 + col // NY
    swap = lambda x, c, y, z: (x, c, y, (z + 4) % NZ)
    parts = pivot_parts(panel, x, core, y, z)
    other_child = send(child[0], swap)
    other_map = send(child_map, swap)
    group = lax.all_gather(panel, "col", axis=0, tiled=True)
    window = window_rows(panel, x, core, z)
    base = sub * blocks
    own_index, own_has = lookup(child_map[0], base, blocks)
    other_index, other_has = lookup(other_map[0], base, blocks)
    present = pattern[:, 0] == 1
    rows_index = kept(present, jnp.arange(blocks, dtype=jnp.int32))
    table = jnp.stack(
        [own_index, own_has, other_index, other_has, rows_index, present.astype(jnp.int32)]
    )
    inverse = pivot_inverse(parts)
    factor, weight = solve(inverse, panel, window)
    updated = final(table, group, weight, trailing, child[0], other_child)
    return (factor, updated)


def solution(mesh):
    return jax.shard_map(
        local,
        mesh=mesh,
        in_specs=(
            P(("sub", "row", "col"), None),
            P(("sub", "row"), "col"),
            P("sub", "row", "col"),
            P("sub", "row"),
            P(("sub", "row"), "col"),
        ),
        out_specs=(P(("sub", "row", "col"), None), P(("sub", "row"), "col")),
        check_vma=False,
    )
```

time: 701 us -> 306 us (0.44)
  the two profiles are of different devices: /device:TPU:1 before, /device:TPU:122 now
where the time goes in v1:
time: 306 us; the launch traced here: 304 us
  waiting for transfers between devices  128 us (42%)
  starting transfers between devices  103 us (34%)
  Pallas kernels  43.5 us (14%)
  between operations  14.5 us (5%)
  local copies, waits for them, and re-layouts  7.47 us (2%)
  other arithmetic  7.28 us (2%)
    ppermute x15, waiting for transfers between devices, send(): return lax.ppermute(value, ALL, pairs_of(move))  127 us
    ppermute x15, starting transfers between devices, send(): return lax.ppermute(value, ALL, pairs_of(move))  102 us
    pallas_call x1, Pallas kernels, pivot_inverse(): pl.pallas_call(pivot_kernel, out_shape=jax.ShapeDtypeStruct((width, width...  26.9 us
    pallas_call x1, Pallas kernels, final(): pl.pallas_call(final_kernel, grid_spec=pltpu.PrefetchScalarGridSpec(num_s...  13.7 us
  transfers between devices with their start and end apart: 17, of which 3 were waited for; matrix products, arithmetic and copies ran while one was open for 3% of the time, Pallas kernels for 10%

profile of v1, /device:TPU:122, one launch (start us, length us, event | category | flops | bytes accessed | tf_op | source)
XLA Modules:
  0.0 303.6 jit_solution(3591456476426188560)
XLA Ops:
  7.2 0.7 all-gather.2.cloned.1.call-update
  7.9 0.7 collective-permute-start.9
  8.6 4.6 %collective-permute-start.14 = (s32[1,8]{1,0:T(1,128)}, s32[1,8]{1,0:T(1,128)S(1)}, u32[]{:S(2)}, u32[]{:S(2)}) collective-permute-start(s32[1,8]{1,0:T(1,128)} %param.8), channel_id=1, source_target_pairs={{0,128},{4,132},{8,136},{12,140},{128,0},{132,4},{136,8},{140,12},... | collective-permute-start | bytes 104 | tf_op jit(solution)/shard_map/ppermute | solution.py:31
  13.2 1.0 slice.19
  14.2 0.9 fusion.4
  15.1 1.0 maximum_select_fusion
  16.1 0.7 collective-permute-start
  16.8 1.5 collective-permute-start.15
  18.3 0.7 bitcast_select_fusion
  19.1 1.3 compare_reduce_fusion.2
  20.4 0.7 collective-permute-start.1
  21.1 0.7 fusion
  21.8 0.7 collective-permute-start.2
  22.8 0.7 collective-permute-start.3
  24.1 0.7 collective-permute-start.10
  24.8 0.7 collective-permute-start.4
  25.7 0.7 collective-permute-start.5
  26.4 0.7 collective-permute-start.11
  27.2 1.3 collective-permute-start.6
  28.5 118.2 %collective-permute-done.6 = f32[128,384]{1,0:T(8,128)S(1)} collective-permute-done((f32[128,384]{1,0:T(8,128)S(1)}, f32[128,384]{1,0:T(8,128)S(1)}, u32[]{:S(2)}, u32[]{:S(2)}) %collective-permute-start.6) | collective-permute-done | bytes 196640 | tf_op jit(solution)/shard_map/ppermute | solution.py:31
  146.7 86.1 %collective-permute-start.7 = (f32[128,384]{1,0:T(8,128)S(1)}, f32[128,384]{1,0:T(8,128)S(1)}, u32[]{:S(2)}, u32[]{:S(2)}) collective-permute-start(f32[128,384]{1,0:T(8,128)S(1)} %broadcast_select_fusion.11), channel_id=1, source_target_pairs={{0,1},{4,5},{8,9},{12,13},{128,129},{132,133},{136,137},{140,141},... | collective-permute-start | bytes 589832 | tf_op jit(solution)/shard_map/ppermute | solution.py:31
  232.9 1.3 collective-permute-start.12
  234.3 2.1 collective-permute-done.7
  236.5 0.8 pad_maximum_fusion.1
  237.3 6.7 %collective-permute-done.12 = f32[256,512]{1,0:T(8,128)S(1)} collective-permute-done((f32[256,512]{1,0:T(8,128)S(1)}, f32[256,512]{1,0:T(8,128)S(1)}, u32[]{:S(2)}, u32[]{:S(2)}) %collective-permute-start.12) | collective-permute-done | bytes 524320 | tf_op jit(solution)/shard_map/ppermute | solution.py:31
  244.1 2.1 collective-permute-start.13
  246.2 1.2 broadcast_select_fusion.5
  247.5 26.9 %shard_map.68.inverse_ref = f32[512,512]{1,0:T(8,128)S(1)} custom-call(f32[2,256,384]{2,1,0:T(8,128)S(1)} %pad_maximum_fusion.parts_ref), custom_call_target="tpu_custom_call" | custom-call | tf_op jit(solution)/shard_map/pallas_call | solution.py:115
  274.6 2.8 shard_map.69
  277.5 3.4 %copy-done = f32[4096,512]{1,0:T(8,128)S(1)} copy-done((f32[4096,512]{1,0:T(8,128)S(1)}, f32[4096,512]{1,0:T(8,128)}, u32[]{:S(2)}) %copy-start) | copy-done | bytes 8388632
  280.9 2.2 copy-done.2
  283.0 13.7 %shard_map.70 = f32[4096,256]{1,0:T(8,128)} custom-call(s32[6,16]{1,0:T(8,128)S(1)} %stack.21.table, f32[4096,512]{1,0:T(8,128)S(1)} %copy-done, f32[256,512]{1,0:T(8,128)S(1)} %get-tuple-element.9.weight_ref, f32[4096,256]{1,0:T(8,128)S(1)} %copy-done.2, f32[2048,256]{1,0:T(8,128)S(1)} %bitcast.22, f32[2048,256]{1,0:T(8,128)} %collective-permute-done.15.other_ref), custom_call_target="tpu_custom_call" | custom-call | tf_op jit(solution)/shard_map/pallas_call | solution.py:164
  (50 shorter events, 1.8 us)
Async XLA Ops:
  7.2 15.5 %copy-start.4 = (s32[1,8]{1,0:T(1,128)S(1)}, s32[1,8]{1,0:T(1,128)}, u32[]{:S(2)}) copy-start(s32[1,8]{1,0:T(1,128)} %param.8) | copy-start | bytes 100
  7.2 270.3 %all-gather.2.cloned.1.call-start = ((), (), s32[]{:S(2)}) async-start(), calls=%async_computation | async-start | bytes 8912896 | tf_op jit(solution)/shard_map/all_gather | solution.py:267
  7.9 16.2 %collective-permute-start.9 = (f32[256,512]{1,0:T(8,128)}, f32[256,512]{1,0:T(8,128)S(1)}, u32[]{:S(2)}, u32[]{:S(2)}) collective-permute-start(f32[256,512]{1,0:T(8,128)} %panel_ref.1), channel_id=1, source_target_pairs={{2,0},{3,1},{4,2},{5,3},{6,4},{7,5},{8,6},{9,7},{10,8},{11,9},{12,... | collective-permute-start | bytes 1572872 | tf_op jit(solution)/shard_map/ppermute | solution.py:245
  8.6 14.0 %collective-permute-start.14 = (s32[1,8]{1,0:T(1,128)}, s32[1,8]{1,0:T(1,128)S(1)}, u32[]{:S(2)}, u32[]{:S(2)}) collective-permute-start(s32[1,8]{1,0:T(1,128)} %param.8), channel_id=1, source_target_pairs={{0,128},{4,132},{8,136},{12,140},{128,0},{132,4},{136,8},{140,12},... | collective-permute-start | bytes 104 | tf_op jit(solution)/shard_map/ppermute | solution.py:31
  16.1 4.3 %collective-permute-start = (f32[128,384]{1,0:T(8,128)S(1)}, f32[128,384]{1,0:T(8,128)S(1)}, u32[]{:S(2)}, u32[]{:S(2)}) collective-permute-start(f32[128,384]{1,0:T(8,128)S(1)} %slice.25), channel_id=1, source_target_pairs={{0,16},{1,17}} | collective-permute-start | bytes 589832 | tf_op jit(solution)/shard_map/ppermute | solution.py:31
  16.8 260.6 %collective-permute-start.15 = (f32[2048,256]{1,0:T(8,128)}, f32[2048,256]{1,0:T(8,128)}, u32[]{:S(2)}, u32[]{:S(2)}) collective-permute-start(f32[2048,256]{1,0:T(8,128)} %bitcast.21), channel_id=1, source_target_pairs={{0,128},{4,132},{8,136},{12,140},{128,0},{132,4},{136,8},{140,12},... | collective-permute-start | bytes 6291464 | tf_op jit(solution)/shard_map/ppermute | solution.py:31
  20.4 1.3 collective-permute-start.1
  21.8 1.0 collective-permute-start.2
  22.8 2.0 collective-permute-start.3
  24.1 2.3 collective-permute-start.10
  24.8 0.8 collective-permute-start.4
  25.7 1.5 collective-permute-start.5
  26.4 206.4 %collective-permute-start.11 = (f32[256,512]{1,0:T(8,128)S(1)}, f32[256,512]{1,0:T(8,128)S(1)}, u32[]{:S(2)}, u32[]{:S(2)}) collective-permute-start(f32[256,512]{1,0:T(8,128)S(1)} %broadcast_select_fusion), channel_id=1, source_target_pairs={{0,64},{4,68},{8,72},{12,76},{128,192},{132,196},{136,200},{140,20... | collective-permute-start | bytes 1572872 | tf_op jit(solution)/shard_map/ppermute | solution.py:31
  27.2 119.5 %collective-permute-start.6 = (f32[128,384]{1,0:T(8,128)S(1)}, f32[128,384]{1,0:T(8,128)S(1)}, u32[]{:S(2)}, u32[]{:S(2)}) collective-permute-start(f32[128,384]{1,0:T(8,128)S(1)} %broadcast_select_fusion.10), channel_id=1, source_target_pairs={{0,2},{4,6},{8,10},{12,14},{128,130},{132,134},{136,138},{140,142}... | collective-permute-start | bytes 589832 | tf_op jit(solution)/shard_map/ppermute | solution.py:31
  146.7 89.7 %collective-permute-start.7 = (f32[128,384]{1,0:T(8,128)S(1)}, f32[128,384]{1,0:T(8,128)S(1)}, u32[]{:S(2)}, u32[]{:S(2)}) collective-permute-start(f32[128,384]{1,0:T(8,128)S(1)} %broadcast_select_fusion.11), channel_id=1, source_target_pairs={{0,1},{4,5},{8,9},{12,13},{128,129},{132,133},{136,137},{140,141},... | collective-permute-start | bytes 589832 | tf_op jit(solution)/shard_map/ppermute | solution.py:31
  232.9 11.1 %collective-permute-start.12 = (f32[256,512]{1,0:T(8,128)S(1)}, f32[256,512]{1,0:T(8,128)S(1)}, u32[]{:S(2)}, u32[]{:S(2)}) collective-permute-start(f32[256,512]{1,0:T(8,128)S(1)} %broadcast_select_fusion.1), channel_id=1, source_target_pairs={{0,32},{4,36},{8,40},{12,44},{128,160},{132,164},{136,168},{140,17... | collective-permute-start | bytes 1572872 | tf_op jit(solution)/shard_map/ppermute | solution.py:31
  237.3 37.3 %copy-start.1 = (f32[256,512]{1,0:T(8,128)S(1)}, f32[256,512]{1,0:T(8,128)}, u32[]{:S(2)}) copy-start(f32[256,512]{1,0:T(8,128)} %panel_ref.1) | copy-start | bytes 1572868
  237.3 9.0 %collective-permute-start.8 = (f32[2,128,384]{2,1,0:T(8,128)}, f32[2,128,384]{2,1,0:T(8,128)}, u32[]{:S(2)}, u32[]{:S(2)}) collective-permute-start(f32[2,128,384]{2,1,0:T(8,128)} %pad_maximum_fusion.1), channel_id=1, source_target_pairs={{0,16},{4,20},{8,24},{12,28},{128,144},{132,148},{136,152},{140,15... | collective-permute-start | bytes 1179656 | tf_op jit(solution)/shard_map/ppermute | solution.py:31
  244.1 30.4 %collective-permute-start.13 = (f32[256,512]{1,0:T(8,128)S(1)}, f32[256,512]{1,0:T(8,128)}, u32[]{:S(2)}, u32[]{:S(2)}) collective-permute-start(f32[256,512]{1,0:T(8,128)S(1)} %broadcast_select_fusion.2), channel_id=1, source_target_pairs={{0,16},{4,20},{8,24},{12,28},{128,144},{132,148},{136,152},{140,15... | collective-permute-start | bytes 1572872 | tf_op jit(solution)/shard_map/ppermute | solution.py:31
  246.2 31.2 %copy-start.3 = (f32[1,2048,256]{2,1,0:T(8,128)S(1)}, f32[1,2048,256]{2,1,0:T(8,128)}, u32[]{:S(2)}) copy-start(f32[1,2048,256]{2,1,0:T(8,128)} %param.7) | copy-start | bytes 6291460
  277.5 3.4 %copy-start = (f32[4096,512]{1,0:T(8,128)S(1)}, f32[4096,512]{1,0:T(8,128)}, u32[]{:S(2)}) copy-start(f32[4096,512]{1,0:T(8,128)} %all-gather.2.cloned.1.call-done.group_ref) | copy-start | bytes 25165828
  280.8 2.2 copy-start.2
Sparse Core Ops, SparseCore 0:
  9.8 191.7 all-gather.1

commit v2 on v1

--- a/solution.py
+++ b/solution.py
@@ -139,45 +139,81 @@
     )(inverse, panel, window)
 
 
-def final_kernel(table, group_ref, weight_ref, trailing_ref, own_ref, other_ref, out_ref):
+def update_kernel(table, zl, near_ref, far_ref, weight_ref, trailing_ref, own_ref, out_ref):
     i = pl.program_id(0)
+    is_near = i // NY == zl[0]
     out_ref[...] = trailing_ref[...]
 
     @pl.when(table[1, i] == 1)
     def _():
         out_ref[...] += own_ref[...]
 
-    @pl.when(table[3, i] == 1)
+    @pl.when((table[4, i] == 1) & is_near)
     def _():
-        out_ref[...] += other_ref[...]
-
-    @pl.when(table[5, i] == 1)
+        out_ref[...] -= contract(near_ref[...], weight_ref[...], 1, 1)
+
+    @pl.when((table[4, i] == 1) & jnp.logical_not(is_near))
     def _():
-        out_ref[...] -= contract(group_ref[...], weight_ref[...], 1, 1)
-
-
-def final(table, group, weight, trailing, own, other):
+        out_ref[...] -= contract(far_ref[...], weight_ref[...], 1, 1)
+
+
+def near_place(i, table, zl):
+    return (jnp.where(i // NY == zl[0], i % NY, 0), 0)
+
+
+def far_place(i, table, zl):
+    shift = (i // NY) ^ zl[0]
+    return (jnp.where(shift == 0, 0, (i % NY) * 3 + shift - 1), 0)
+
+
+def update(table, zl, near, far, weight, trailing, own):
     size = weight.shape[0]
     width = weight.shape[1]
     blocks = trailing.shape[0] // size
     square = lambda pick: pl.BlockSpec((size, size), pick)
     return pl.pallas_call(
-        final_kernel,
+        update_kernel,
+        grid_spec=pltpu.PrefetchScalarGridSpec(
+            num_scalar_prefetch=2,
+            grid=(blocks,),
+            in_specs=[
+                pl.BlockSpec((size, width), near_place),
+                pl.BlockSpec((size, width), far_place),
+                pl.BlockSpec((size, width), lambda i, t, zl: (0, 0)),
+                square(lambda i, t, zl: (i, 0)),
+                square(lambda i, t, zl: (t[0, i], 0)),
+            ],
+            out_specs=square(lambda i, t, zl: (i, 0)),
+        ),
+        out_shape=jax.ShapeDtypeStruct(trailing.shape, jnp.float32),
+        compiler_params=pltpu.CompilerParams(vmem_limit_bytes=56 << 20),
+    )(table, zl, near, far, weight, trailing, own)
+
+
+def extend_kernel(table, assembled_ref, other_ref, out_ref):
+    i = pl.program_id(0)
+    out_ref[...] = assembled_ref[...]
+
+    @pl.when(table[2, i] == 1)
+    def _():
+        out_ref[...] += other_ref[...]
+
+
+def extend(table, assembled, other):
+    size = assembled.shape[1]
+    square = lambda pick: pl.BlockSpec((size, size), pick)
+    return pl.pallas_call(
+        extend_kernel,
         grid_spec=pltpu.PrefetchScalarGridSpec(
             num_scalar_prefetch=1,
-            grid=(blocks,),
-            in_specs=[
-                pl.BlockSpec((size, width), lambda i, t: (t[4, i], 0)),
-                pl.BlockSpec((size, width), lambda i, t: (0, 0)),
-                square(lambda i, t: (i, 0)),
-                square(lambda i, t: (t[0, i], 0)),
-                square(lambda i, t: (t[2, i], 0)),
-            ],
+            grid=(assembled.shape[0] // size,),
+            in_specs=[square(lambda i, t: (i, 0)), square(lambda i, t: (t[3, i], 0))],
             out_specs=square(lambda i, t: (i, 0)),
         ),
-        out_shape=jax.ShapeDtypeStruct(trailing.shape, jnp.float32),
-        compiler_params=pltpu.CompilerParams(vmem_limit_bytes=32 << 20),
-    )(table, group, weight, trailing, own, other)
+        out_shape=jax.ShapeDtypeStruct(assembled.shape, jnp.float32),
+        input_output_aliases={1: 0},
+        compiler_params=pltpu.CompilerParams(vmem_limit_bytes=56 << 20),
+    )(table, assembled, other)
 
 
 def kept(has, index):
@@ -195,7 +231,10 @@
     return kept(has, index), has.astype(jnp.int32)
 
 
-def pivot_parts(panel, x, core, y, z):
+STEPS = (("z", 4), ("z", 2), ("z", 1), ("y", 2), ("x", 2), ("x", 1))
+
+
+def pivot_split(panel, core, y):
     half = panel.shape[1] // 2
     packed = jnp.concatenate([panel[SB:, 0:SB], panel[SB:, SB:half]], axis=0)
     from_left = panel[:, : half + SB]
@@ -204,53 +243,62 @@
     split = send(
         whole[SB:], lambda x, c, y, z: (x, 1, y, z) if x == 0 and c == 0 and z == 0 and y < 2 else None
     )
-    held = jnp.where(core == 0, whole[:SB], split)
-
-    orders = (
-        (("z", 4), ("z", 2), ("z", 1), ("x", 2), ("x", 1), ("y", 2)),
-        (("x", 2), ("x", 1), ("y", 2), ("z", 4), ("z", 2), ("z", 1)),
-    )
+    return jnp.where(core == 0, whole[:SB], split)
+
+
+def pivot_spread(held, numbers, x, y, z):
     have = {(0, c, y, 0) for c in range(2) for y in range(2)}
-    for number in range(len(orders[0])):
+    for number, (axis, stride) in enumerate(STEPS):
         targets = {}
         for place in sorted(have):
-            axis, stride = orders[place[1]][number]
-            where = "xcyz".index(axis)
             to = list(place)
-            to[where] += stride
+            to["xcyz".index(axis)] += stride
             targets[place] = tuple(to)
+        have = have | set(targets.values())
+        if number not in numbers:
+            continue
         got = send(held, lambda x, c, y, z: targets.get((x, c, y, z)))
-        receives = False
-        for c in range(2):
-            axis, stride = orders[c][number]
-            coordinate = {"x": x, "y": y, "z": z}[axis]
-            receives = receives | ((core == c) & ((coordinate // stride) % 2 == 1))
-        held = jnp.where(receives, got, held)
-        have = have | set(targets.values())
-    other = send(held, lambda x, c, y, z: (x, c, y ^ 1, z))
+        coordinate = {"x": x, "y": y, "z": z}[axis]
+        held = jnp.where((coordinate // stride) % 2 == 1, got, held)
+    return held
+
+
+def join_y(held, y):
+    other = send(held, lambda x, c, y, z: (x, c, y ^ 1, z) if x == 0 else None)
     left = jnp.where(y % 2 == 0, held, other)
     right = jnp.where(y % 2 == 0, other, held)
-    mine = jnp.stack([left, right])
+    return jnp.stack([left, right])
+
+
+def join_core(mine, core):
     theirs = send(mine, lambda x, c, y, z: (x, 1 - c, y, z))
     top = jnp.where(core == 0, mine, theirs)
     bottom = jnp.where(core == 0, theirs, mine)
     return jnp.concatenate([top, bottom], axis=1)
 
 
-def window_rows(panel, x, core, z):
+def window_halves(panel, z):
     place = {}
     for col in range(16):
         block = 2 + col
         place[(block // 16) * 16 + block % 16] = col
     held = lax.ppermute(panel, ALL, sorted(place.items()))
     got = send(held, lambda x, c, y, z: (x, c, y, z + 4) if x == 0 and c == 0 and z < 4 else None)
-    held = jnp.where(z >= 4, got, held)
+    return jnp.where(z >= 4, got, held)
+
+
+def window_rows(held, x, core):
     got = send(held, lambda x, c, y, z: (2, c, y, z) if x == 0 and c == 0 else None)
     held = jnp.where(x == 2, got, held)
     got = send(held, lambda x, c, y, z: (x + 1, c, y, z) if x % 2 == 0 and c == 0 else None)
     held = jnp.where(x % 2 == 1, got, held)
     got = send(held, lambda x, c, y, z: (x, 1, y, z) if c == 0 else None)
     return jnp.where(core == 1, got, held)
+
+
+def gather_y(value):
+    groups = [[zl * NY + y for y in range(NY)] for zl in range(NZ // 2)]
+    return lax.all_gather(value, "col", axis_index_groups=groups, axis=0, tiled=True)
 
 
 def local(panel, trailing, child, child_map, pattern):
@@ -261,22 +309,36 @@
     col = lax.axis_index("col")
     x, core, y, z = row // 2, row % 2, col % NY, sub * 4 + col // NY
     swap = lambda x, c, y, z: (x, c, y, (z + 4) % NZ)
-    parts = pivot_parts(panel, x, core, y, z)
+    near = gather_y(panel)
+    held = pivot_split(panel, core, y)
+    window = window_halves(panel, z)
+    other_map = send(child_map, swap)
+    held = pivot_spread(held, (0, 1, 2), x, y, z)
+    held, window, later = lax.optimization_barrier((held, window, panel))
+    across = [send(later, lambda x, c, y, z, d=d: (x, c, y, z ^ d)) for d in (1, 2, 3)]
+    held = pivot_spread(held, (3,), x, y, z)
+    held, across[0] = lax.optimization_barrier((held, across[0]))
+    held = join_y(held, y)
+    held, across[1] = lax.optimization_barrier((held, across[1]))
+    held = pivot_spread(held, (4,), x, y, z)
+    held, across[2] = lax.optimization_barrier((held, across[2]))
+    far = gather_y(jnp.concatenate(across, axis=0))
     other_child = send(child[0], swap)
-    other_map = send(child_map, swap)
-    group = lax.all_gather(panel, "col", axis=0, tiled=True)
-    window = window_rows(panel, x, core, z)
+    held = pivot_spread(held, (5,), x, y, z)
+    parts = join_core(held, core)
+    window = window_rows(window, x, core)
     base = sub * blocks
     own_index, own_has = lookup(child_map[0], base, blocks)
     other_index, other_has = lookup(other_map[0], base, blocks)
     present = pattern[:, 0] == 1
-    rows_index = kept(present, jnp.arange(blocks, dtype=jnp.int32))
     table = jnp.stack(
-        [own_index, own_has, other_index, other_has, rows_index, present.astype(jnp.int32)]
+        [own_index, own_has, other_has, other_index, present.astype(jnp.int32)]
     )
     inverse = pivot_inverse(parts)
     factor, weight = solve(inverse, panel, window)
-    updated = final(table, group, weight, trailing, child[0], other_child)
+    zl = jnp.broadcast_to(z % 4, (1,)).astype(jnp.int32)
+    assembled = update(table, zl, near, far, weight, trailing, child[0])
+    updated = extend(table, assembled, other_child)
     return (factor, updated)
 
 

time: 306 us -> 225 us (0.74)
  the two profiles are of different devices: /device:TPU:122 before, /device:TPU:33 now
where the time goes in v2:
time: 225 us; the launch traced here: 224 us
  waiting for transfers between devices  93 us (41%)
  Pallas kernels  58.9 us (26%)
  starting transfers between devices  44.4 us (20%)
  between operations  14.7 us (7%)
  other arithmetic  9.29 us (4%)
  local copies, waits for them, and re-layouts  4.04 us (2%)
    ppermute x18, waiting for transfers between devices, send(): return lax.ppermute(value, ALL, pairs_of(move))  93 us
    ppermute x18, starting transfers between devices, send(): return lax.ppermute(value, ALL, pairs_of(move))  43.6 us
    pallas_call x1, Pallas kernels, pivot_inverse(): pl.pallas_call(pivot_kernel, out_shape=jax.ShapeDtypeStruct((width, width...  26.9 us
    pallas_call x1, Pallas kernels, update(): pl.pallas_call(update_kernel, grid_spec=pltpu.PrefetchScalarGridSpec(num_...  17.9 us
    pallas_call x1, Pallas kernels, extend(): pl.pallas_call(extend_kernel, grid_spec=pltpu.PrefetchScalarGridSpec(num_...  11.3 us
  transfers between devices with their start and end apart: 21, of which 8 were waited for; matrix products, arithmetic and copies ran while one was open for 4% of the time, Pallas kernels for 21%

profile of v2, /device:TPU:33, one launch (start us, length us, event | category | flops | bytes accessed | tf_op | source)
XLA Modules:
  0.0 224.3 jit_solution(6013758523266305031)
XLA Ops:
  7.2 0.9 fusion.3
  8.2 1.0 slice.19
  9.1 1.0 maximum_select_fusion
  11.0 0.8 collective-permute-start.1
  13.4 0.7 collective-permute-start.5
  14.1 1.3 collective-permute-start.3
  15.5 25.4 %collective-permute-done.3 = f32[128,384]{1,0:T(8,128)S(1)} collective-permute-done((f32[128,384]{1,0:T(8,128)S(1)}, f32[128,384]{1,0:T(8,128)S(1)}, u32[]{:S(2)}, u32[]{:S(2)}) %collective-permute-start.3) | collective-permute-done | bytes 196640 | tf_op jit(solution)/shard_map/ppermute | solution.py:31
  41.1 1.3 collective-permute-start.6
  42.5 6.4 %collective-permute-done.6 = f32[128,384]{1,0:T(8,128)S(1)} collective-permute-done((f32[128,384]{1,0:T(8,128)S(1)}, f32[128,384]{1,0:T(8,128)S(1)}, u32[]{:S(2)}, u32[]{:S(2)}) %collective-permute-start.6) | collective-permute-done | bytes 196640 | tf_op jit(solution)/shard_map/ppermute | solution.py:31
  48.9 3.1 %collective-permute-done.7 = f32[256,512]{1,0:T(8,128)S(1)} collective-permute-done((f32[256,512]{1,0:T(8,128)S(1)}, f32[256,512]{1,0:T(8,128)S(1)}, u32[]{:S(2)}, u32[]{:S(2)}) %collective-permute-start.7) | collective-permute-done | bytes 524320 | tf_op jit(solution)/shard_map/ppermute | solution.py:31
  52.0 3.2 %collective-permute-start.8 = (f32[128,384]{1,0:T(8,128)S(1)}, f32[128,384]{1,0:T(8,128)S(1)}, u32[]{:S(2)}, u32[]{:S(2)}) collective-permute-start(f32[128,384]{1,0:T(8,128)S(1)} %broadcast_select_fusion.11), channel_id=1, source_target_pairs={{0,1},{4,5},{8,9},{12,13},{128,129},{132,133},{136,137},{140,141},... | collective-permute-start | bytes 589832 | tf_op jit(solution)/shard_map/ppermute | solution.py:31
  55.2 10.2 %collective-permute-start.9 = (f32[256,512]{1,0:T(8,128)S(1)}, f32[256,512]{1,0:T(8,128)S(1)}, u32[]{:S(2)}, u32[]{:S(2)}) collective-permute-start(f32[256,512]{1,0:T(8,128)S(1)} %copy-done.1), channel_id=1, source_target_pairs={{0,8},{4,12},{8,0},{12,4},{128,136},{132,140},{136,128},{140,132},... | collective-permute-start | bytes 1572872 | tf_op jit(solution)/shard_map/ppermute | solution.py:31
  65.5 22.2 %collective-permute-done.9 = f32[256,512]{1,0:T(8,128)S(1)} collective-permute-done((f32[256,512]{1,0:T(8,128)S(1)}, f32[256,512]{1,0:T(8,128)S(1)}, u32[]{:S(2)}, u32[]{:S(2)}) %collective-permute-start.9) | collective-permute-done | bytes 524320 | tf_op jit(solution)/shard_map/ppermute | solution.py:31
  87.7 1.3 collective-permute-start.10
  89.2 8.1 %collective-permute-done.10 = f32[2,128,384]{2,1,0:T(8,128)S(1)} collective-permute-done((f32[2,128,384]{2,1,0:T(8,128)S(1)}, f32[2,128,384]{2,1,0:T(8,128)S(1)}, u32[]{:S(2)}, u32[]{:S(2)}) %collective-permute-start.10) | collective-permute-done | bytes 393248 | tf_op jit(solution)/shard_map/ppermute | solution.py:31
  97.4 16.1 %collective-permute-done.11 = f32[256,512]{1,0:T(8,128)} collective-permute-done((f32[256,512]{1,0:T(8,128)S(1)}, f32[256,512]{1,0:T(8,128)}, u32[]{:S(2)}, u32[]{:S(2)}) %collective-permute-start.11) | collective-permute-done | bytes 524320 | tf_op jit(solution)/shard_map/ppermute | solution.py:31
  113.4 2.6 %pad_maximum_fusion = f32[768,512]{1,0:T(8,128)} fusion(f32[256,512]{1,0:T(8,128)} %collective-permute-done.11, f32[256,512]{1,0:T(8,128)} %copy-done.5, f32[256,512]{1,0:T(8,128)} %copy-done.4), kind=kLoop, calls=%fused_computation | loop fusion | flops 786432 | bytes 3145728 | tf_op jit(solution)/shard_map/concatenate | solution.py:325
  116.2 5.4 %collective-permute-start.18 = (f32[2048,256]{1,0:T(8,128)S(1)}, f32[2048,256]{1,0:T(8,128)}, u32[]{:S(2)}, u32[]{:S(2)}) collective-permute-start(f32[2048,256]{1,0:T(8,128)S(1)} %bitcast.19), channel_id=1, source_target_pairs={{0,128},{4,132},{8,136},{12,140},{128,0},{132,4},{136,8},{140,12},... | collective-permute-start | bytes 6291464 | tf_op jit(solution)/shard_map/ppermute | solution.py:31
  124.5 1.3 collective-permute-start.12
  125.9 1.3 collective-permute-start.16
  127.3 7.4 %collective-permute-done.12 = f32[2,128,384]{2,1,0:T(8,128)S(1)} collective-permute-done((f32[2,128,384]{2,1,0:T(8,128)S(1)}, f32[2,128,384]{2,1,0:T(8,128)S(1)}, u32[]{:S(2)}, u32[]{:S(2)}) %collective-permute-start.12) | collective-permute-done | bytes 393248 | tf_op jit(solution)/shard_map/ppermute | solution.py:31
  134.7 0.8 broadcast_select_fusion.5
  135.5 13.8 %collective-permute-start.13 = (f32[2,128,384]{2,1,0:T(8,128)}, f32[2,128,384]{2,1,0:T(8,128)S(1)}, u32[]{:S(2)}, u32[]{:S(2)}) collective-permute-start(f32[2,128,384]{2,1,0:T(8,128)} %broadcast_select_fusion.5), channel_id=1, source_target_pairs={{0,16},{4,20},{8,24},{12,28},{128,144},{132,148},{136,152},{140,15... | collective-permute-start | bytes 1179656 | tf_op jit(solution)/shard_map/ppermute | solution.py:31
  149.9 1.3 stack.20.table
  151.2 1.1 broadcast_select_fusion.2.window_ref
  152.3 1.1 broadcast_select_fusion.7
  153.4 26.9 %shard_map.68.inverse_ref = f32[512,512]{1,0:T(8,128)S(1)} custom-call(f32[2,256,384]{2,1,0:T(8,128)S(1)} %pad_maximum_fusion.1.parts_ref), custom_call_target="tpu_custom_call" | custom-call | tf_op jit(solution)/shard_map/pallas_call | solution.py:115
  180.4 2.8 %shard_map.69 = (f32[256,512]{1,0:T(8,128)}, f32[256,512]{1,0:T(8,128)S(1)}) custom-call(f32[512,512]{1,0:T(8,128)S(1)} %shard_map.68.inverse_ref, f32[256,512]{1,0:T(8,128)S(1)} %copy-done.1, f32[256,512]{1,0:T(8,128)S(1)} %broadcast_select_fusion.2.window_ref), custom_call_target="tpu_custom_call" | custom-call | tf_op jit(solution)/shard_map/pallas_call | solution.py:135
  183.2 0.8 copy-done.2
  184.1 17.9 %shard_map.70.assembled_ref = f32[4096,256]{1,0:T(8,128)} custom-call(s32[5,16]{1,0:T(8,128)} %stack.20.table, s32[1]{0:T(128)} %bitcast.9.zl, f32[1024,512]{1,0:T(8,128)} %all-gather.3.cloned.1.call-done.near_ref, f32[3072,512]{1,0:T(8,128)} %all-gather.5.cloned.1.call-done.far_ref, f32[256,512]{1,0:T(8,128)} %copy-done.2, f32[4096,256]{1,0:T(8,128)} %trailing_ref.1, ...), custom_call_target="tpu_custom_call" | custom-call | tf_op jit(solution)/shard_map/pallas_call | solution.py:174
  201.9 4.3 %collective-permute-done.18.other_ref = f32[2048,256]{1,0:T(8,128)} collective-permute-done((f32[2048,256]{1,0:T(8,128)S(1)}, f32[2048,256]{1,0:T(8,128)}, u32[]{:S(2)}, u32[]{:S(2)}) %collective-permute-start.18) | collective-permute-done | bytes 2097184 | tf_op jit(solution)/shard_map/ppermute | solution.py:31
  206.2 11.3 %shard_map.71 = f32[4096,256]{1,0:T(8,128)} custom-call(s32[5,16]{1,0:T(8,128)} %stack.20.table, f32[4096,256]{1,0:T(8,128)} %shard_map.70.assembled_ref, f32[2048,256]{1,0:T(8,128)} %collective-permute-done.18.other_ref), custom_call_target="tpu_custom_call", output_to_operand_aliasing={{}: (1, {})} | custom-call | tf_op jit(solution)/shard_map/pallas_call | solution.py:205
  (64 shorter events, 6.5 us)
Async XLA Ops:
  7.2 4.6 %copy-start = (f32[256,512]{1,0:T(8,128)S(1)}, f32[256,512]{1,0:T(8,128)}, u32[]{:S(2)}) copy-start(f32[256,512]{1,0:T(8,128)} %panel_ref.1) | copy-start | bytes 1572868
  7.2 176.9 %all-gather.3.cloned.1.call-start = ((), (), s32[]{:S(2)}) async-start(), calls=%async_computation | async-start | bytes 2621440 | tf_op jit(solution)/shard_map/all_gather | solution.py:301
  10.2 0.7 collective-permute-start
  11.0 30.1 %copy-start.1 = (f32[256,512]{1,0:T(8,128)S(1)}, f32[256,512]{1,0:T(8,128)}, u32[]{:S(2)}) copy-start(f32[256,512]{1,0:T(8,128)} %panel_ref.1) | copy-start | bytes 1572868
  11.0 1.7 collective-permute-start.1
  11.8 1.6 collective-permute-start.4
  12.5 171.5 %all-gather.5.cloned.1.call-start = ((), (), s32[]{:S(2)}) async-start(), calls=%async_computation.1 | async-start | bytes 7864320 | tf_op jit(solution)/shard_map/all_gather | solution.py:301
  12.7 1.4 collective-permute-start.2
  13.4 27.5 %collective-permute-start.5 = (f32[256,512]{1,0:T(8,128)S(1)}, f32[256,512]{1,0:T(8,128)S(1)}, u32[]{:S(2)}, u32[]{:S(2)}) collective-permute-start(f32[256,512]{1,0:T(8,128)S(1)} %collective-permute-done.4), channel_id=1, source_target_pairs={{0,128},{4,132},{8,136},{12,140},{1,129},{5,133},{9,137},{13,141},... | collective-permute-start | bytes 1572872 | tf_op jit(solution)/shard_map/ppermute | solution.py:31
  14.1 26.8 %collective-permute-start.3 = (f32[128,384]{1,0:T(8,128)S(1)}, f32[128,384]{1,0:T(8,128)S(1)}, u32[]{:S(2)}, u32[]{:S(2)}) collective-permute-start(f32[128,384]{1,0:T(8,128)S(1)} %broadcast_select_fusion.9), channel_id=1, source_target_pairs={{0,4},{8,12},{128,132},{136,140},{1,5},{9,13},{129,133},{137,141},... | collective-permute-start | bytes 589832 | tf_op jit(solution)/shard_map/ppermute | solution.py:31
  41.0 11.0 %collective-permute-start.7 = (f32[256,512]{1,0:T(8,128)S(1)}, f32[256,512]{1,0:T(8,128)S(1)}, u32[]{:S(2)}, u32[]{:S(2)}) collective-permute-start(f32[256,512]{1,0:T(8,128)S(1)} %copy-done.1), channel_id=1, source_target_pairs={{0,4},{4,0},{8,12},{12,8},{128,132},{132,128},{136,140},{140,136},... | collective-permute-start | bytes 1572872 | tf_op jit(solution)/shard_map/ppermute | solution.py:31
  41.1 7.7 %collective-permute-start.6 = (f32[128,384]{1,0:T(8,128)S(1)}, f32[128,384]{1,0:T(8,128)S(1)}, u32[]{:S(2)}, u32[]{:S(2)}) collective-permute-start(f32[128,384]{1,0:T(8,128)S(1)} %broadcast_select_fusion.10), channel_id=1, source_target_pairs={{0,2},{4,6},{8,10},{12,14},{128,130},{132,134},{136,138},{140,142}... | collective-permute-start | bytes 589832 | tf_op jit(solution)/shard_map/ppermute | solution.py:31
  52.0 45.3 %copy-start.4 = (f32[256,512]{1,0:T(8,128)}, f32[256,512]{1,0:T(8,128)S(1)}, u32[]{:S(2)}) copy-start(f32[256,512]{1,0:T(8,128)S(1)} %collective-permute-done.7) | copy-start | bytes 1572868
  52.0 13.4 %collective-permute-start.8 = (f32[128,384]{1,0:T(8,128)S(1)}, f32[128,384]{1,0:T(8,128)S(1)}, u32[]{:S(2)}, u32[]{:S(2)}) collective-permute-start(f32[128,384]{1,0:T(8,128)S(1)} %broadcast_select_fusion.11), channel_id=1, source_target_pairs={{0,1},{4,5},{8,9},{12,13},{128,129},{132,133},{136,137},{140,141},... | collective-permute-start | bytes 589832 | tf_op jit(solution)/shard_map/ppermute | solution.py:31
  55.2 32.5 %collective-permute-start.9 = (f32[256,512]{1,0:T(8,128)S(1)}, f32[256,512]{1,0:T(8,128)S(1)}, u32[]{:S(2)}, u32[]{:S(2)}) collective-permute-start(f32[256,512]{1,0:T(8,128)S(1)} %copy-done.1), channel_id=1, source_target_pairs={{0,8},{4,12},{8,0},{12,4},{128,136},{132,140},{136,128},{140,132},... | collective-permute-start | bytes 1572872 | tf_op jit(solution)/shard_map/ppermute | solution.py:31
  87.7 9.6 %copy-start.5 = (f32[256,512]{1,0:T(8,128)}, f32[256,512]{1,0:T(8,128)S(1)}, u32[]{:S(2)}) copy-start(f32[256,512]{1,0:T(8,128)S(1)} %collective-permute-done.9) | copy-start | bytes 1572868
  87.7 9.6 %collective-permute-start.10 = (f32[2,128,384]{2,1,0:T(8,128)S(1)}, f32[2,128,384]{2,1,0:T(8,128)S(1)}, u32[]{:S(2)}, u32[]{:S(2)}) collective-permute-start(f32[2,128,384]{2,1,0:T(8,128)S(1)} %pad_maximum_fusion.2), channel_id=1, source_target_pairs={{0,64},{4,68},{8,72},{12,76},{128,192},{132,196},{136,200},{140,20... | collective-permute-start | bytes 1179656 | tf_op jit(solution)/shard_map/ppermute | solution.py:31
  89.0 24.4 %collective-permute-start.11 = (f32[256,512]{1,0:T(8,128)S(1)}, f32[256,512]{1,0:T(8,128)}, u32[]{:S(2)}, u32[]{:S(2)}) collective-permute-start(f32[256,512]{1,0:T(8,128)S(1)} %copy-done.1), channel_id=1, source_target_pairs={{0,12},{4,8},{8,4},{12,0},{128,140},{132,136},{136,132},{140,128},... | collective-permute-start | bytes 1572872 | tf_op jit(solution)/shard_map/ppermute | solution.py:31
  97.3 18.8 %copy-start.6 = (s32[1,8]{1,0:T(1,128)S(1)}, s32[1,8]{1,0:T(1,128)}, u32[]{:S(2)}) copy-start(s32[1,8]{1,0:T(1,128)} %param.8) | copy-start | bytes 100
  97.3 18.9 %copy-start.3 = (f32[1,2048,256]{2,1,0:T(8,128)S(1)}, f32[1,2048,256]{2,1,0:T(8,128)}, u32[]{:S(2)}) copy-start(f32[1,2048,256]{2,1,0:T(8,128)} %param.7) | copy-start | bytes 6291460
  97.3 24.2 %copy-start.7 = (s32[16,1]{0,1:T(1,128)S(1)}, s32[16,1]{0,1:T(1,128)}, u32[]{:S(2)}) copy-start(s32[16,1]{0,1:T(1,128)} %param.9) | copy-start | bytes 196
  116.1 6.8 %collective-permute-start.17 = (s32[1,8]{1,0:T(1,128)S(1)}, s32[1,8]{1,0:T(1,128)S(1)}, u32[]{:S(2)}, u32[]{:S(2)}) collective-permute-start(s32[1,8]{1,0:T(1,128)S(1)} %copy-done.6), channel_id=1, source_target_pairs={{0,128},{4,132},{8,136},{12,140},{128,0},{132,4},{136,8},{140,12},... | collective-permute-start | bytes 104 | tf_op jit(solution)/shard_map/ppermute | solution.py:31
  116.2 90.0 %collective-permute-start.18 = (f32[2048,256]{1,0:T(8,128)S(1)}, f32[2048,256]{1,0:T(8,128)}, u32[]{:S(2)}, u32[]{:S(2)}) collective-permute-start(f32[2048,256]{1,0:T(8,128)S(1)} %bitcast.19), channel_id=1, source_target_pairs={{0,128},{4,132},{8,136},{12,140},{128,0},{132,4},{136,8},{140,12},... | collective-permute-start | bytes 6291464 | tf_op jit(solution)/shard_map/ppermute | solution.py:31
  122.2 1.4 collective-permute-start.14
  123.7 2.2 collective-permute-start.15
  124.5 10.2 %collective-permute-start.12 = (f32[2,128,384]{2,1,0:T(8,128)S(1)}, f32[2,128,384]{2,1,0:T(8,128)S(1)}, u32[]{:S(2)}, u32[]{:S(2)}) collective-permute-start(f32[2,128,384]{2,1,0:T(8,128)S(1)} %broadcast_select_fusion.4), channel_id=1, source_target_pairs={{0,32},{4,36},{8,40},{12,44},{128,160},{132,164},{136,168},{140,17... | collective-permute-start | bytes 1179656 | tf_op jit(solution)/shard_map/ppermute | solution.py:31
  125.9 25.3 %collective-permute-start.16 = (f32[256,512]{1,0:T(8,128)S(1)}, f32[256,512]{1,0:T(8,128)}, u32[]{:S(2)}, u32[]{:S(2)}) collective-permute-start(f32[256,512]{1,0:T(8,128)S(1)} %broadcast_select_fusion.1), channel_id=1, source_target_pairs={{0,16},{4,20},{8,24},{12,28},{128,144},{132,148},{136,152},{140,15... | collective-permute-start | bytes 1572872 | tf_op jit(solution)/shard_map/ppermute | solution.py:31
  135.5 16.8 %collective-permute-start.13 = (f32[2,128,384]{2,1,0:T(8,128)}, f32[2,128,384]{2,1,0:T(8,128)S(1)}, u32[]{:S(2)}, u32[]{:S(2)}) collective-permute-start(f32[2,128,384]{2,1,0:T(8,128)} %broadcast_select_fusion.5), channel_id=1, source_target_pairs={{0,16},{4,20},{8,24},{12,28},{128,144},{132,148},{136,152},{140,15... | collective-permute-start | bytes 1179656 | tf_op jit(solution)/shard_map/ppermute | solution.py:31
  183.2 0.8 copy-start.2
Sparse Core Ops, SparseCore 0:
  12.6 38.6 all-gather.2
  116.2 61.1 all-gather.4

commit v3 on v2

--- a/solution.py
+++ b/solution.py
@@ -9,6 +9,7 @@
 ALL = ("sub", "row", "col")
 SB = 128
 NX, NY, NZ = 4, 4, 8
+FIRST, MAIN = 1, 6
 
 
 def linear(x, core, y, z):
@@ -139,81 +140,112 @@
     )(inverse, panel, window)
 
 
-def update_kernel(table, zl, near_ref, far_ref, weight_ref, trailing_ref, own_ref, out_ref):
+def take_kernel(order, block_ref, out_ref):
+    out_ref[...] = block_ref[...]
+
+
+def take_blocks(order, blocks, size):
+    count = order.shape[0]
+    return pl.pallas_call(
+        take_kernel,
+        grid_spec=pltpu.PrefetchScalarGridSpec(
+            num_scalar_prefetch=1,
+            grid=(count,),
+            in_specs=[pl.BlockSpec((size, size), lambda i, t: (t[i], 0))],
+            out_specs=pl.BlockSpec((size, size), lambda i, t: (i, 0)),
+        ),
+        out_shape=jax.ShapeDtypeStruct((count * size, size), jnp.float32),
+        compiler_params=pltpu.CompilerParams(vmem_limit_bytes=56 << 20),
+    )(order, blocks)
+
+
+BLOCK, OWN, OWN_HAS, FROM, FROM_HAS, PRESENT, ROWS = 0, 1, 2, (3, 4, 5), 6, 7, 8
+NEAR = 8
+
+
+def near_kernel(table, rows_ref, weight_ref, trailing_ref, own_ref, out_ref):
     i = pl.program_id(0)
-    is_near = i // NY == zl[0]
     out_ref[...] = trailing_ref[...]
 
-    @pl.when(table[1, i] == 1)
+    @pl.when(table[OWN_HAS, i] == 1)
     def _():
         out_ref[...] += own_ref[...]
 
-    @pl.when((table[4, i] == 1) & is_near)
+    @pl.when(table[PRESENT, i] == 1)
     def _():
-        out_ref[...] -= contract(near_ref[...], weight_ref[...], 1, 1)
-
-    @pl.when((table[4, i] == 1) & jnp.logical_not(is_near))
-    def _():
-        out_ref[...] -= contract(far_ref[...], weight_ref[...], 1, 1)
-
-
-def near_place(i, table, zl):
-    return (jnp.where(i // NY == zl[0], i % NY, 0), 0)
-
-
-def far_place(i, table, zl):
-    shift = (i // NY) ^ zl[0]
-    return (jnp.where(shift == 0, 0, (i % NY) * 3 + shift - 1), 0)
-
-
-def update(table, zl, near, far, weight, trailing, own):
-    size = weight.shape[0]
-    width = weight.shape[1]
-    blocks = trailing.shape[0] // size
+        out_ref[...] -= contract(rows_ref[...], weight_ref[...], 1, 1)
+
+
+def update_near(table, near, weight, trailing, own):
+    size, width = weight.shape
     square = lambda pick: pl.BlockSpec((size, size), pick)
     return pl.pallas_call(
-        update_kernel,
+        near_kernel,
         grid_spec=pltpu.PrefetchScalarGridSpec(
-            num_scalar_prefetch=2,
-            grid=(blocks,),
+            num_scalar_prefetch=1,
+            grid=(NEAR,),
             in_specs=[
-                pl.BlockSpec((size, width), near_place),
-                pl.BlockSpec((size, width), far_place),
-                pl.BlockSpec((size, width), lambda i, t, zl: (0, 0)),
-                square(lambda i, t, zl: (i, 0)),
-                square(lambda i, t, zl: (t[0, i], 0)),
+                pl.BlockSpec((size, width), lambda i, t: (t[ROWS, i], 0)),
+                pl.BlockSpec((size, width), lambda i, t: (0, 0)),
+                square(lambda i, t: (t[BLOCK, i], 0)),
+                square(lambda i, t: (t[OWN, i], 0)),
             ],
-            out_specs=square(lambda i, t, zl: (i, 0)),
+            out_specs=square(lambda i, t: (t[BLOCK, i], 0)),
         ),
         out_shape=jax.ShapeDtypeStruct(trailing.shape, jnp.float32),
         compiler_params=pltpu.CompilerParams(vmem_limit_bytes=56 << 20),
-    )(table, zl, near, far, weight, trailing, own)
-
-
-def extend_kernel(table, assembled_ref, other_ref, out_ref):
+    )(table, near, weight, trailing, own)
+
+
+def far_kernel(table, done_ref, rows_ref, weight_ref, trailing_ref, own_ref, first_ref, main_ref, rest_ref, out_ref):
     i = pl.program_id(0)
-    out_ref[...] = assembled_ref[...]
-
-    @pl.when(table[2, i] == 1)
+
+    @pl.when(i < NEAR)
     def _():
-        out_ref[...] += other_ref[...]
-
-
-def extend(table, assembled, other):
-    size = assembled.shape[1]
+        out_ref[...] = done_ref[...]
+
+    @pl.when(i >= NEAR)
+    def _():
+        out_ref[...] = trailing_ref[...]
+
+        @pl.when(table[OWN_HAS, i] == 1)
+        def _():
+            out_ref[...] += own_ref[...]
+
+        @pl.when(table[PRESENT, i] == 1)
+        def _():
+            out_ref[...] -= contract(rows_ref[...], weight_ref[...], 1, 1)
+
+    for number, other_ref in enumerate((first_ref, main_ref, rest_ref)):
+
+        @pl.when(table[FROM_HAS, i] == number + 1)
+        def _():
+            out_ref[...] += other_ref[...]
+
+
+def update_far(table, done, far, weight, trailing, own, others):
+    size, width = weight.shape
+    last = NEAR - 1
     square = lambda pick: pl.BlockSpec((size, size), pick)
     return pl.pallas_call(
-        extend_kernel,
+        far_kernel,
         grid_spec=pltpu.PrefetchScalarGridSpec(
             num_scalar_prefetch=1,
-            grid=(assembled.shape[0] // size,),
-            in_specs=[square(lambda i, t: (i, 0)), square(lambda i, t: (t[3, i], 0))],
-            out_specs=square(lambda i, t: (i, 0)),
+            grid=(trailing.shape[0] // size,),
+            in_specs=[
+                square(lambda i, t: (t[BLOCK, jnp.minimum(i, last)], 0)),
+                pl.BlockSpec((size, width), lambda i, t: (t[ROWS, jnp.maximum(i, NEAR)], 0)),
+                pl.BlockSpec((size, width), lambda i, t: (0, 0)),
+                square(lambda i, t: (t[BLOCK, jnp.maximum(i, NEAR)], 0)),
+                square(lambda i, t: (t[OWN, jnp.maximum(i, NEAR)], 0)),
+                *[square(lambda i, t, at=at: (t[at, i], 0)) for at in FROM],
+            ],
+            out_specs=square(lambda i, t: (t[BLOCK, i], 0)),
         ),
-        out_shape=jax.ShapeDtypeStruct(assembled.shape, jnp.float32),
+        out_shape=jax.ShapeDtypeStruct(trailing.shape, jnp.float32),
         input_output_aliases={1: 0},
         compiler_params=pltpu.CompilerParams(vmem_limit_bytes=56 << 20),
-    )(table, assembled, other)
+    )(table, done, far, weight, trailing, own, *others)
 
 
 def kept(has, index):
@@ -224,11 +256,20 @@
     return jnp.where(latest >= 0, latest % blocks, 0)
 
 
-def lookup(slots, base, blocks):
-    match = slots[None, :] == base + jnp.arange(blocks, dtype=jnp.int32)[:, None]
-    has = jnp.any(match, axis=1)
-    index = jnp.argmax(match, axis=1).astype(jnp.int32)
-    return kept(has, index), has.astype(jnp.int32)
+def lookup(slots, target):
+    match = slots[None, :] == target[:, None]
+    return jnp.any(match, axis=1), jnp.argmax(match, axis=1).astype(jnp.int32)
+
+
+def crossing(slots, home, blocks):
+    cross = slots // blocks != home
+    k = jnp.arange(slots.shape[0])
+    earlier = k[None, :] < k[:, None]
+    ahead = jnp.sum(earlier & cross[None, :], axis=1)
+    count = jnp.sum(cross)
+    place = jnp.where(cross, ahead, count + k - ahead)
+    order = jnp.sum(jnp.where(place[None, :] == k[:, None], k[None, :], 0), axis=1)
+    return count, place.astype(jnp.int32), order.astype(jnp.int32)
 
 
 STEPS = (("z", 4), ("z", 2), ("z", 1), ("y", 2), ("x", 2), ("x", 1))
@@ -277,12 +318,15 @@
     return jnp.concatenate([top, bottom], axis=1)
 
 
-def window_halves(panel, z):
+def window_owned(panel):
     place = {}
     for col in range(16):
         block = 2 + col
         place[(block // 16) * 16 + block % 16] = col
-    held = lax.ppermute(panel, ALL, sorted(place.items()))
+    return lax.ppermute(panel, ALL, sorted(place.items()))
+
+
+def window_halves(held, z):
     got = send(held, lambda x, c, y, z: (x, c, y, z + 4) if x == 0 and c == 0 and z < 4 else None)
     return jnp.where(z >= 4, got, held)
 
@@ -301,6 +345,18 @@
     return lax.all_gather(value, "col", axis_index_groups=groups, axis=0, tiled=True)
 
 
+def swap(value):
+    return send(value, lambda x, c, y, z: (x, c, y, (z + 4) % NZ))
+
+
+def send_rest(order, child, size, both):
+    first = swap(take_blocks(order[:1], child, size))
+    second = lax.cond(
+        both, lambda: swap(take_blocks(order[1:], child, size)), lambda: jnp.zeros_like(first)
+    )
+    return jnp.concatenate([first, second], axis=0)
+
+
 def local(panel, trailing, child, child_map, pattern):
     size = trailing.shape[1]
     blocks = trailing.shape[0] // size
@@ -308,37 +364,79 @@
     row = lax.axis_index("row")
     col = lax.axis_index("col")
     x, core, y, z = row // 2, row % 2, col % NY, sub * 4 + col // NY
-    swap = lambda x, c, y, z: (x, c, y, (z + 4) % NZ)
-    near = gather_y(panel)
+    own_slots = child_map[0]
+    own_count, own_place, order = crossing(own_slots, sub, blocks)
+    outgoing = take_blocks(order[:MAIN], child[0], size)
+    other_slots = swap(child_map)[0]
+
+    tie = lax.optimization_barrier
+    exchange = lambda value, d: send(value, lambda x, c, y, z: (x, c, y, z ^ d))
     held = pivot_split(panel, core, y)
-    window = window_halves(panel, z)
-    other_map = send(child_map, swap)
-    held = pivot_spread(held, (0, 1, 2), x, y, z)
-    held, window, later = lax.optimization_barrier((held, window, panel))
-    across = [send(later, lambda x, c, y, z, d=d: (x, c, y, z ^ d)) for d in (1, 2, 3)]
+    window = window_owned(panel)
+    across1 = exchange(panel, 1)
+    held = pivot_spread(held, (0,), x, y, z)
+    held, window = tie((held, window))
+    window = window_halves(window, z)
+    held = pivot_spread(held, (1,), x, y, z)
+    held, across1, panel2 = tie((held, across1, panel))
+    across2 = exchange(panel2, 2)
+    near = gather_y(jnp.concatenate([panel, across1], axis=0))
+    held = pivot_spread(held, (2,), x, y, z)
+    held, across2, window, panel3 = tie((held, across2, window, panel))
+    across3 = exchange(panel3, 3)
     held = pivot_spread(held, (3,), x, y, z)
-    held, across[0] = lax.optimization_barrier((held, across[0]))
+    held, outgoing = tie((held, outgoing))
+    first = swap(outgoing[: FIRST * size])
     held = join_y(held, y)
-    held, across[1] = lax.optimization_barrier((held, across[1]))
+    held, across3 = tie((held, across3))
+    far = gather_y(jnp.concatenate([across2, across3], axis=0))
     held = pivot_spread(held, (4,), x, y, z)
-    held, across[2] = lax.optimization_barrier((held, across[2]))
-    far = gather_y(jnp.concatenate(across, axis=0))
-    other_child = send(child[0], swap)
+    held, first = tie((held, first))
+    main = swap(outgoing[FIRST * size :])
     held = pivot_spread(held, (5,), x, y, z)
     parts = join_core(held, core)
     window = window_rows(window, x, core)
-    base = sub * blocks
-    own_index, own_has = lookup(child_map[0], base, blocks)
-    other_index, other_has = lookup(other_map[0], base, blocks)
-    present = pattern[:, 0] == 1
+
+    other_count, other_place, _ = crossing(other_slots, 1 - sub, blocks)
+    need = jnp.maximum(own_count, other_count)
+    step = jnp.arange(blocks, dtype=jnp.int32)
+    shift = (step // NEAR) * 2 + step % 2
+    block = ((col // NY) ^ shift) * NY + (step % NEAR) // 2
+    target = sub * blocks + block
+    own_has, own_index = lookup(own_slots, target)
+    other_has, other_index = lookup(other_slots, target)
+    place = jnp.sum(
+        jnp.where(other_index[:, None] == jnp.arange(other_place.shape[0])[None, :], other_place[None, :], 0),
+        axis=1,
+    )
+    starts = (0, FIRST, MAIN)
+    ends = (FIRST, MAIN, other_place.shape[0])
+    inside = [other_has & (place >= low) & (place < high) for low, high in zip(starts, ends)]
+    present = jnp.sum(jnp.where(block[:, None] == step[None, :], pattern[:, 0][None, :], 0), axis=1) == 1
+    rows = step % NEAR
+    rows = jnp.concatenate([kept(present[:NEAR], rows[:NEAR]), kept(present[NEAR:], rows[NEAR:])])
     table = jnp.stack(
-        [own_index, own_has, other_has, other_index, present.astype(jnp.int32)]
-    )
+        [
+            block,
+            kept(own_has, own_index),
+            own_has.astype(jnp.int32),
+            *[kept(has, place - low) for has, low in zip(inside, starts)],
+            sum((number + 1) * has.astype(jnp.int32) for number, has in enumerate(inside)),
+            present.astype(jnp.int32),
+            rows,
+        ]
+    ).astype(jnp.int32)
+
     inverse = pivot_inverse(parts)
     factor, weight = solve(inverse, panel, window)
-    zl = jnp.broadcast_to(z % 4, (1,)).astype(jnp.int32)
-    assembled = update(table, zl, near, far, weight, trailing, child[0])
-    updated = extend(table, assembled, other_child)
+    done = update_near(table, near, weight, trailing, child[0])
+    done, main, need = tie((done, main, need))
+    rest = lax.cond(
+        need > MAIN,
+        lambda: send_rest(order[MAIN:], child[0], size, need > MAIN + 1),
+        lambda: jnp.zeros((2 * size, size), jnp.float32),
+    )
+    updated = update_far(table, done, far, weight, trailing, child[0], (first, main, rest))
     return (factor, updated)
 
 

time: 225 us -> 219 us (0.973)
  the two profiles are of different devices: /device:TPU:33 before, /device:TPU:41 now
where the time goes in v3:
time: 219 us; the launch traced here: 218 us
  waiting for transfers between devices  70.2 us (32%)
  Pallas kernels  58.2 us (27%)
  starting transfers between devices  44.4 us (20%)
  other arithmetic  22.4 us (10%)
  between operations  15.8 us (7%)
  local copies, waits for them, and re-layouts  6.87 us (3%)
    ppermute x19, waiting for transfers between devices, send(): return lax.ppermute(value, ALL, pairs_of(move))  70.1 us
    ppermute x19, starting transfers between devices, send(): return lax.ppermute(value, ALL, pairs_of(move))  42.8 us
    pallas_call x1, Pallas kernels, pivot_inverse(): pl.pallas_call(pivot_kernel, out_shape=jax.ShapeDtypeStruct((width, width...  27.1 us
    pallas_call x1, Pallas kernels, update_far(): pl.pallas_call(far_kernel, grid_spec=pltpu.PrefetchScalarGridSpec(num_sca...  15.2 us
    pallas_call x1, Pallas kernels, update_near(): pl.pallas_call(near_kernel, grid_spec=pltpu.PrefetchScalarGridSpec(num_sc...  10.3 us
  transfers between devices with their start and end apart: 22, of which 7 were waited for; matrix products, arithmetic and copies ran while one was open for 11% of the time, Pallas kernels for 20%

profile of v3, /device:TPU:41, one launch (start us, length us, event | category | flops | bytes accessed | tf_op | source)
XLA Modules:
  0.0 217.9 jit_solution(3138156215693968297)
XLA Ops:
  9.2 1.2 maximum_select_fusion
  11.1 1.5 collective-permute-start.4
  13.3 8.4 %collective-permute-start.6 = (f32[256,512]{1,0:T(8,128)}, f32[256,512]{1,0:T(8,128)}, u32[]{:S(2)}, u32[]{:S(2)}) collective-permute-start(f32[256,512]{1,0:T(8,128)} %panel_ref.1), channel_id=1, source_target_pairs={{0,4},{4,0},{8,12},{12,8},{128,132},{132,128},{136,140},{140,136},... | collective-permute-start | bytes 1572872 | tf_op jit(solution)/shard_map/ppermute | solution.py:32
  22.5 21.3 %collective-permute-done.6 = f32[256,512]{1,0:T(8,128)} collective-permute-done((f32[256,512]{1,0:T(8,128)}, f32[256,512]{1,0:T(8,128)}, u32[]{:S(2)}, u32[]{:S(2)}) %collective-permute-start.6) | collective-permute-done | bytes 524320 | tf_op jit(solution)/shard_map/ppermute | solution.py:32
  43.9 2.2 %pad_maximum_fusion.1 = f32[512,512]{1,0:T(8,128)} fusion(f32[256,512]{1,0:T(8,128)} %collective-permute-done.6, f32[256,512]{1,0:T(8,128)S(1)} %copy-done), kind=kLoop, calls=%fused_computation.1 | loop fusion | flops 262144 | bytes 2097152 | tf_op jit(solution)/shard_map/concatenate | solution.py:383
  46.3 1.5 collective-permute-start.9
  47.8 1.3 collective-permute-start.7
  49.9 4.3 %collective-permute-done.7 = f32[128,384]{1,0:T(8,128)S(1)} collective-permute-done((f32[128,384]{1,0:T(8,128)S(1)}, f32[128,384]{1,0:T(8,128)S(1)}, u32[]{:S(2)}, u32[]{:S(2)}) %collective-permute-start.7) | collective-permute-done | bytes 196640 | tf_op jit(solution)/shard_map/ppermute | solution.py:32
  54.2 1.2 broadcast_select_fusion.3
  55.4 19.3 %collective-permute-done.8 = f32[256,512]{1,0:T(8,128)} collective-permute-done((f32[256,512]{1,0:T(8,128)S(1)}, f32[256,512]{1,0:T(8,128)}, u32[]{:S(2)}, u32[]{:S(2)}) %collective-permute-start.8) | collective-permute-done | bytes 524320 | tf_op jit(solution)/shard_map/ppermute | solution.py:32
  74.7 2.0 collective-permute-start.10
  77.5 2.8 %shard_map.68 = f32[1536,256]{1,0:T(8,128)} custom-call(s32[6]{0:T(128)S(1)} %bitcast.53, f32[2048,256]{1,0:T(8,128)S(1)} %bitcast.44), custom_call_target="tpu_custom_call" | custom-call | tf_op jit(solution)/shard_map/pallas_call | solution.py:149
  80.3 5.3 %collective-permute-start.12 = (f32[256,512]{1,0:T(8,128)S(1)}, f32[256,512]{1,0:T(8,128)}, u32[]{:S(2)}, u32[]{:S(2)}) collective-permute-start(f32[256,512]{1,0:T(8,128)S(1)} %copy-done), channel_id=1, source_target_pairs={{0,12},{4,8},{8,4},{12,0},{128,140},{132,136},{136,132},{140,128},... | collective-permute-start | bytes 1572872 | tf_op jit(solution)/shard_map/ppermute | solution.py:32
  85.6 2.1 collective-permute-start.11
  88.3 9.4 %collective-permute-done.11 = f32[128,384]{1,0:T(8,128)S(1)} collective-permute-done((f32[128,384]{1,0:T(8,128)S(1)}, f32[128,384]{1,0:T(8,128)S(1)}, u32[]{:S(2)}, u32[]{:S(2)}) %collective-permute-start.11) | collective-permute-done | bytes 196640 | tf_op jit(solution)/shard_map/ppermute | solution.py:32
  97.8 10.9 %collective-permute-done.12 = f32[256,512]{1,0:T(8,128)} collective-permute-done((f32[256,512]{1,0:T(8,128)S(1)}, f32[256,512]{1,0:T(8,128)}, u32[]{:S(2)}, u32[]{:S(2)}) %collective-permute-start.12) | collective-permute-done | bytes 524320 | tf_op jit(solution)/shard_map/ppermute | solution.py:32
  108.7 2.2 %pad_maximum_fusion.2 = f32[512,512]{1,0:T(8,128)} fusion(f32[256,512]{1,0:T(8,128)} %collective-permute-done.12, f32[256,512]{1,0:T(8,128)} %collective-permute-done.8), kind=kLoop, calls=%fused_computation.2 | loop fusion | flops 262144 | bytes 2097152 | tf_op jit(solution)/shard_map/concatenate | solution.py:392
  117.7 1.3 collective-permute-start.13
  120.5 3.6 %collective-permute-start.14 = (f32[256,256]{1,0:T(8,128)S(1)}, f32[256,256]{1,0:T(8,128)}, u32[]{:S(2)}, u32[]{:S(2)}) collective-permute-start(f32[256,256]{1,0:T(8,128)S(1)} %slice.56), channel_id=1, source_target_pairs={{0,128},{4,132},{8,136},{12,140},{128,0},{132,4},{136,8},{140,12},... | collective-permute-start | bytes 786440 | tf_op jit(solution)/shard_map/ppermute | solution.py:32
  125.0 2.9 %collective-permute-done.13 = f32[2,128,384]{2,1,0:T(8,128)S(1)} collective-permute-done((f32[2,128,384]{2,1,0:T(8,128)S(1)}, f32[2,128,384]{2,1,0:T(8,128)S(1)}, u32[]{:S(2)}, u32[]{:S(2)}) %collective-permute-start.13) | collective-permute-done | bytes 393248 | tf_op jit(solution)/shard_map/ppermute | solution.py:32
  128.7 2.0 collective-permute-done.14.first_ref
  130.7 2.0 collective-permute-start.15
  133.2 1.2 slice.61
  134.4 4.1 %collective-permute-start.21 = (f32[1280,256]{1,0:T(8,128)}, f32[1280,256]{1,0:T(8,128)}, u32[]{:S(2)}, u32[]{:S(2)}) collective-permute-start(f32[1280,256]{1,0:T(8,128)} %slice.61), channel_id=1, source_target_pairs={{0,128},{4,132},{8,136},{12,140},{128,0},{132,4},{136,8},{140,12},... | collective-permute-start | bytes 3932168 | tf_op jit(solution)/shard_map/ppermute | solution.py:32
  138.6 1.3 collective-permute-start.19
  142.8 6.5 %collective-permute-start.16 = (f32[2,128,384]{2,1,0:T(8,128)S(1)}, f32[2,128,384]{2,1,0:T(8,128)}, u32[]{:S(2)}, u32[]{:S(2)}) collective-permute-start(f32[2,128,384]{2,1,0:T(8,128)S(1)} %broadcast_select_fusion.5), channel_id=1, source_target_pairs={{0,16},{4,20},{8,24},{12,28},{128,144},{132,148},{136,152},{140,15... | collective-permute-start | bytes 1179656 | tf_op jit(solution)/shard_map/ppermute | solution.py:32
  149.3 1.2 compare_select_fusion.17
  150.5 1.9 stack.27.table
  154.7 27.1 %shard_map.69.inverse_ref = f32[512,512]{1,0:T(8,128)S(1)} custom-call(f32[2,256,384]{2,1,0:T(8,128)S(1)} %pad_maximum_fusion.3.parts_ref), custom_call_target="tpu_custom_call" | custom-call | tf_op jit(solution)/shard_map/pallas_call | solution.py:116
  181.7 2.9 %shard_map.70 = (f32[256,512]{1,0:T(8,128)}, f32[256,512]{1,0:T(8,128)S(1)}) custom-call(f32[512,512]{1,0:T(8,128)S(1)} %shard_map.69.inverse_ref, f32[256,512]{1,0:T(8,128)S(1)} %copy-done, f32[256,512]{1,0:T(8,128)S(1)} %broadcast_select_fusion.2.window_ref), custom_call_target="tpu_custom_call" | custom-call | tf_op jit(solution)/shard_map/pallas_call | solution.py:136
  185.5 10.3 %shard_map.71.done_ref = f32[4096,256]{1,0:T(8,128)} custom-call(s32[9,16]{1,0:T(8,128)} %stack.27.table, f32[2048,512]{1,0:T(8,128)} %all-gather.3.cloned.1.call-done.rows_ref, f32[256,512]{1,0:T(8,128)} %copy-done.1, f32[4096,256]{1,0:T(8,128)} %trailing_ref.3, f32[2048,256]{1,0:T(8,128)S(1)} %bitcast.45), custom_call_target="tpu_custom_call" | custom-call | tf_op jit(solution)/shard_map/pallas_call | solution.py:182
  195.8 15.2 %shard_map.72 = f32[4096,256]{1,0:T(8,128)} custom-call(s32[9,16]{1,0:T(8,128)} %stack.27.table, f32[4096,256]{1,0:T(8,128)} %shard_map.71.done_ref, f32[2048,512]{1,0:T(8,128)} %all-gather.5.cloned.1.call-done.rows_ref, f32[256,512]{1,0:T(8,128)} %copy-done.1, f32[4096,256]{1,0:T(8,128)} %trailing_ref.3, ...), custom_call_target="tpu_custom_call", output_to_operand_aliasing={{}: (1, {})} | custom-call | tf_op jit(solution)/shard_map/pallas_call | solution.py:230
  (95 shorter events, 21.9 us)
Async XLA Ops:
  7.2 36.7 %copy-start = (f32[256,512]{1,0:T(8,128)S(1)}, f32[256,512]{1,0:T(8,128)}, u32[]{:S(2)}) copy-start(f32[256,512]{1,0:T(8,128)} %panel_ref.1) | copy-start | bytes 1572868
  7.2 39.0 %copy-start.4 = (s32[1,8]{1,0:T(1,128)S(1)}, s32[1,8]{1,0:T(1,128)}, u32[]{:S(2)}) copy-start(s32[1,8]{1,0:T(1,128)} %param.12) | copy-start | bytes 100
  7.2 178.3 %all-gather.3.cloned.1.call-start = ((), (), s32[]{:S(2)}) async-start(), calls=%async_computation | async-start | bytes 5242880 | tf_op jit(solution)/shard_map/all_gather | solution.py:345
  9.2 68.3 %copy-start.2 = (f32[1,2048,256]{2,1,0:T(8,128)S(1)}, f32[1,2048,256]{2,1,0:T(8,128)}, u32[]{:S(2)}) copy-start(f32[1,2048,256]{2,1,0:T(8,128)} %param.11) | copy-start | bytes 6291460
  10.4 2.2 %collective-permute-start.2 = (f32[128,384]{1,0:T(8,128)S(1)}, f32[128,384]{1,0:T(8,128)S(1)}, u32[]{:S(2)}, u32[]{:S(2)}) collective-permute-start(f32[128,384]{1,0:T(8,128)S(1)} %slice.63), channel_id=1, source_target_pairs={{0,16},{1,17}} | collective-permute-start | bytes 589832 | tf_op jit(solution)/shard_map/ppermute | solution.py:32
  11.1 10.7 %collective-permute-start.4 = (f32[256,512]{1,0:T(8,128)}, f32[256,512]{1,0:T(8,128)}, u32[]{:S(2)}, u32[]{:S(2)}) collective-permute-start(f32[256,512]{1,0:T(8,128)} %panel_ref.1), channel_id=1, source_target_pairs={{2,0},{3,1},{4,2},{5,3},{6,4},{7,5},{8,6},{9,7},{10,8},{11,9},{12,... | collective-permute-start | bytes 1572872 | tf_op jit(solution)/shard_map/ppermute | solution.py:326
  12.6 9.1 %collective-permute-start.3 = (f32[128,384]{1,0:T(8,128)S(1)}, f32[128,384]{1,0:T(8,128)S(1)}, u32[]{:S(2)}, u32[]{:S(2)}) collective-permute-start(f32[128,384]{1,0:T(8,128)S(1)} %slice_select_fusion), channel_id=1, source_target_pairs={{0,128},{1,129},{16,144},{17,145}} | collective-permute-start | bytes 589832 | tf_op jit(solution)/shard_map/ppermute | solution.py:32
  13.3 30.6 %collective-permute-start.6 = (f32[256,512]{1,0:T(8,128)}, f32[256,512]{1,0:T(8,128)}, u32[]{:S(2)}, u32[]{:S(2)}) collective-permute-start(f32[256,512]{1,0:T(8,128)} %panel_ref.1), channel_id=1, source_target_pairs={{0,4},{4,0},{8,12},{12,8},{128,132},{132,128},{136,140},{140,136},... | collective-permute-start | bytes 1572872 | tf_op jit(solution)/shard_map/ppermute | solution.py:32
  21.8 0.7 collective-permute-start.5
  46.1 149.7 %all-gather.5.cloned.1.call-start = ((), (), s32[]{:S(2)}) async-start(), calls=%async_computation.1 | async-start | bytes 5242880 | tf_op jit(solution)/shard_map/all_gather | solution.py:345
  46.2 67.2 %collective-permute-start.20 = (s32[1,8]{1,0:T(1,128)S(1)}, s32[1,8]{1,0:T(1,128)S(1)}, u32[]{:S(2)}, u32[]{:S(2)}) collective-permute-start(s32[1,8]{1,0:T(1,128)S(1)} %copy-done.4), channel_id=1, source_target_pairs={{0,128},{4,132},{8,136},{12,140},{128,0},{132,4},{136,8},{140,12},... | collective-permute-start | bytes 104 | tf_op jit(solution)/shard_map/ppermute | solution.py:32
  46.3 7.9 %collective-permute-start.9 = (f32[256,512]{1,0:T(8,128)}, f32[256,512]{1,0:T(8,128)}, u32[]{:S(2)}, u32[]{:S(2)}) collective-permute-start(f32[256,512]{1,0:T(8,128)} %collective-permute-done.4), channel_id=1, source_target_pairs={{0,128},{4,132},{8,136},{12,140},{1,129},{5,133},{9,137},{13,141},... | collective-permute-start | bytes 1572872 | tf_op jit(solution)/shard_map/ppermute | solution.py:32
  47.8 6.4 %collective-permute-start.7 = (f32[128,384]{1,0:T(8,128)S(1)}, f32[128,384]{1,0:T(8,128)S(1)}, u32[]{:S(2)}, u32[]{:S(2)}) collective-permute-start(f32[128,384]{1,0:T(8,128)S(1)} %broadcast_select_fusion.9), channel_id=1, source_target_pairs={{0,4},{8,12},{128,132},{136,140},{1,5},{9,13},{129,133},{137,141},... | collective-permute-start | bytes 589832 | tf_op jit(solution)/shard_map/ppermute | solution.py:32
  49.8 24.9 %collective-permute-start.8 = (f32[256,512]{1,0:T(8,128)S(1)}, f32[256,512]{1,0:T(8,128)}, u32[]{:S(2)}, u32[]{:S(2)}) collective-permute-start(f32[256,512]{1,0:T(8,128)S(1)} %copy-done), channel_id=1, source_target_pairs={{0,8},{4,12},{8,0},{12,4},{128,136},{132,140},{136,128},{140,132},... | collective-permute-start | bytes 1572872 | tf_op jit(solution)/shard_map/ppermute | solution.py:32
  74.7 10.9 %collective-permute-start.10 = (f32[128,384]{1,0:T(8,128)S(1)}, f32[128,384]{1,0:T(8,128)}, u32[]{:S(2)}, u32[]{:S(2)}) collective-permute-start(f32[128,384]{1,0:T(8,128)S(1)} %broadcast_select_fusion.10), channel_id=1, source_target_pairs={{0,2},{4,6},{8,10},{12,14},{128,130},{132,134},{136,138},{140,142}... | collective-permute-start | bytes 589832 | tf_op jit(solution)/shard_map/ppermute | solution.py:32
  77.5 8.1 %copy-start.6 = (s32[8]{0:T(128)}, s32[8]{0:T(128)S(1)}, u32[]{:S(2)}) copy-start(s32[8]{0:T(128)S(1)} %select_reduce_fusion.8) | copy-start | bytes 100
  80.3 28.4 %collective-permute-start.12 = (f32[256,512]{1,0:T(8,128)S(1)}, f32[256,512]{1,0:T(8,128)}, u32[]{:S(2)}, u32[]{:S(2)}) collective-permute-start(f32[256,512]{1,0:T(8,128)S(1)} %copy-done), channel_id=1, source_target_pairs={{0,12},{4,8},{8,4},{12,0},{128,140},{132,136},{136,132},{140,128},... | collective-permute-start | bytes 1572872 | tf_op jit(solution)/shard_map/ppermute | solution.py:32
  85.6 12.1 %collective-permute-start.11 = (f32[128,384]{1,0:T(8,128)S(1)}, f32[128,384]{1,0:T(8,128)S(1)}, u32[]{:S(2)}, u32[]{:S(2)}) collective-permute-start(f32[128,384]{1,0:T(8,128)S(1)} %broadcast_select_fusion.11), channel_id=1, source_target_pairs={{0,1},{4,5},{8,9},{12,13},{128,129},{132,133},{136,137},{140,141},... | collective-permute-start | bytes 589832 | tf_op jit(solution)/shard_map/ppermute | solution.py:32
  110.9 22.3 %copy-start.3 = (f32[1536,256]{1,0:T(8,128)S(1)}, f32[1536,256]{1,0:T(8,128)}, u32[]{:S(2)}) copy-start(f32[1536,256]{1,0:T(8,128)} %shard_map.68) | copy-start | bytes 4718596
  116.3 7.7 %collective-permute-start.17 = (f32[256,512]{1,0:T(8,128)S(1)}, f32[256,512]{1,0:T(8,128)S(1)}, u32[]{:S(2)}, u32[]{:S(2)}) collective-permute-start(f32[256,512]{1,0:T(8,128)S(1)} %broadcast_select_fusion.3), channel_id=1, source_target_pairs={{0,64},{4,68},{8,72},{12,76},{128,192},{132,196},{136,200},{140,20... | collective-permute-start | bytes 1572872 | tf_op jit(solution)/shard_map/ppermute | solution.py:32
  117.7 10.2 %collective-permute-start.13 = (f32[2,128,384]{2,1,0:T(8,128)S(1)}, f32[2,128,384]{2,1,0:T(8,128)S(1)}, u32[]{:S(2)}, u32[]{:S(2)}) collective-permute-start(f32[2,128,384]{2,1,0:T(8,128)S(1)} %pad_maximum_fusion.4), channel_id=1, source_target_pairs={{0,64},{4,68},{8,72},{12,76},{128,192},{132,196},{136,200},{140,20... | collective-permute-start | bytes 1179656 | tf_op jit(solution)/shard_map/ppermute | solution.py:32
  120.5 30.0 %copy-start.5 = (s32[1,16]{1,0:T(1,128)S(1)}, s32[1,16]{1,0:T(1,128)}, u32[]{:S(2)}) copy-start(s32[1,16]{1,0:T(1,128)} %add_bitcast_fusion) | copy-start | bytes 196
  120.5 10.1 %collective-permute-start.14 = (f32[256,256]{1,0:T(8,128)S(1)}, f32[256,256]{1,0:T(8,128)}, u32[]{:S(2)}, u32[]{:S(2)}) collective-permute-start(f32[256,256]{1,0:T(8,128)S(1)} %slice.56), channel_id=1, source_target_pairs={{0,128},{4,132},{8,136},{12,140},{128,0},{132,4},{136,8},{140,12},... | collective-permute-start | bytes 786440 | tf_op jit(solution)/shard_map/ppermute | solution.py:32
  124.2 14.3 %collective-permute-start.18 = (f32[256,512]{1,0:T(8,128)S(1)}, f32[256,512]{1,0:T(8,128)S(1)}, u32[]{:S(2)}, u32[]{:S(2)}) collective-permute-start(f32[256,512]{1,0:T(8,128)S(1)} %broadcast_select_fusion), channel_id=1, source_target_pairs={{0,32},{4,36},{8,40},{12,44},{128,160},{132,164},{136,168},{140,17... | collective-permute-start | bytes 1572872 | tf_op jit(solution)/shard_map/ppermute | solution.py:32
  130.7 11.1 %collective-permute-start.15 = (f32[2,128,384]{2,1,0:T(8,128)}, f32[2,128,384]{2,1,0:T(8,128)}, u32[]{:S(2)}, u32[]{:S(2)}) collective-permute-start(f32[2,128,384]{2,1,0:T(8,128)} %broadcast_select_fusion.4), channel_id=1, source_target_pairs={{0,32},{4,36},{8,40},{12,44},{128,160},{132,164},{136,168},{140,17... | collective-permute-start | bytes 1179656 | tf_op jit(solution)/shard_map/ppermute | solution.py:32
  134.4 61.3 %collective-permute-start.21 = (f32[1280,256]{1,0:T(8,128)}, f32[1280,256]{1,0:T(8,128)}, u32[]{:S(2)}, u32[]{:S(2)}) collective-permute-start(f32[1280,256]{1,0:T(8,128)} %slice.61), channel_id=1, source_target_pairs={{0,128},{4,132},{8,136},{12,140},{128,0},{132,4},{136,8},{140,12},... | collective-permute-start | bytes 3932168 | tf_op jit(solution)/shard_map/ppermute | solution.py:32
  138.6 13.8 %collective-permute-start.19 = (f32[256,512]{1,0:T(8,128)S(1)}, f32[256,512]{1,0:T(8,128)}, u32[]{:S(2)}, u32[]{:S(2)}) collective-permute-start(f32[256,512]{1,0:T(8,128)S(1)} %broadcast_select_fusion.1), channel_id=1, source_target_pairs={{0,16},{4,20},{8,24},{12,28},{128,144},{132,148},{136,152},{140,15... | collective-permute-start | bytes 1572872 | tf_op jit(solution)/shard_map/ppermute | solution.py:32
  142.8 10.7 %collective-permute-start.16 = (f32[2,128,384]{2,1,0:T(8,128)S(1)}, f32[2,128,384]{2,1,0:T(8,128)}, u32[]{:S(2)}, u32[]{:S(2)}) collective-permute-start(f32[2,128,384]{2,1,0:T(8,128)S(1)} %broadcast_select_fusion.5), channel_id=1, source_target_pairs={{0,16},{4,20},{8,24},{12,28},{128,144},{132,148},{136,152},{140,15... | collective-permute-start | bytes 1179656 | tf_op jit(solution)/shard_map/ppermute | solution.py:32
  184.6 0.8 copy-start.1
  185.5 10.3 %copy-start.7 = (s32[8]{0:T(128)S(1)}, s32[8]{0:T(128)}, u32[]{:S(2)}) copy-start(s32[8]{0:T(128)} %copy-done.6) | copy-start | bytes 100
Sparse Core Ops, SparseCore 0:
  46.3 51.6 all-gather.2
  111.1 45.5 all-gather.4

commit v4 on v3

--- a/solution.py
+++ b/solution.py
@@ -9,7 +9,7 @@
 ALL = ("sub", "row", "col")
 SB = 128
 NX, NY, NZ = 4, 4, 8
-FIRST, MAIN = 1, 6
+FIRST, MAIN = 2, 6
 
 
 def linear(x, core, y, z):
@@ -160,7 +160,7 @@
 
 
 BLOCK, OWN, OWN_HAS, FROM, FROM_HAS, PRESENT, ROWS = 0, 1, 2, (3, 4, 5), 6, 7, 8
-NEAR = 8
+NEAR = 4
 
 
 def near_kernel(table, rows_ref, weight_ref, trailing_ref, own_ref, out_ref):
@@ -331,11 +331,14 @@
     return jnp.where(z >= 4, got, held)
 
 
-def window_rows(held, x, core):
-    got = send(held, lambda x, c, y, z: (2, c, y, z) if x == 0 and c == 0 else None)
-    held = jnp.where(x == 2, got, held)
-    got = send(held, lambda x, c, y, z: (x + 1, c, y, z) if x % 2 == 0 and c == 0 else None)
-    held = jnp.where(x % 2 == 1, got, held)
+def window_x(held, x, stride):
+    got = send(
+        held, lambda x, c, y, z: (x + stride, c, y, z) if x % (2 * stride) == 0 and c == 0 else None
+    )
+    return jnp.where((x // stride) % 2 == 1, got, held)
+
+
+def window_core(held, core):
     got = send(held, lambda x, c, y, z: (x, 1, y, z) if c == 0 else None)
     return jnp.where(core == 1, got, held)
 
@@ -370,38 +373,49 @@
     other_slots = swap(child_map)[0]
 
     tie = lax.optimization_barrier
-    exchange = lambda value, d: send(value, lambda x, c, y, z: (x, c, y, z ^ d))
+    zl = z % 4
+    right = lambda value, at: send(value, lambda x, c, y, z: (x, c, y, z + 1) if z % 4 in at else None)
+    left = lambda value, at: send(value, lambda x, c, y, z: (x, c, y, z - 1) if z % 4 in at else None)
+    near = gather_y(panel)
     held = pivot_split(panel, core, y)
     window = window_owned(panel)
-    across1 = exchange(panel, 1)
     held = pivot_spread(held, (0,), x, y, z)
     held, window = tie((held, window))
     window = window_halves(window, z)
-    held = pivot_spread(held, (1,), x, y, z)
-    held, across1, panel2 = tie((held, across1, panel))
-    across2 = exchange(panel2, 2)
-    near = gather_y(jnp.concatenate([panel, across1], axis=0))
-    held = pivot_spread(held, (2,), x, y, z)
-    held, across2, window, panel3 = tie((held, across2, window, panel))
-    across3 = exchange(panel3, 3)
+    held = pivot_spread(held, (1, 2), x, y, z)
+    held, window, bulk = tie((held, window, panel))
+    window = window_x(window, x, 2)
+    from_left1, from_right1 = right(bulk, (0, 1, 2)), left(bulk, (1, 2, 3))
     held = pivot_spread(held, (3,), x, y, z)
-    held, outgoing = tie((held, outgoing))
+    held = join_y(held, y)
+    held, from_left1, from_right1, near, window = tie((held, from_left1, from_right1, near, window))
+    slot1 = jnp.where(zl == 3, from_left1, from_right1)
+    window = window_x(window, x, 1)
+    from_left2, from_right2 = right(from_left1, (1, 2)), left(from_right1, (1, 2))
+    held = pivot_spread(held, (4,), x, y, z)
+    held, from_left2, from_right2, window = tie((held, from_left2, from_right2, window))
+    window = window_core(window, core)
+    ends = send(
+        jnp.where(zl == 2, from_left2, from_right2),
+        lambda x, c, y, z: {1: (x, c, y, z - 1), 2: (x, c, y, z + 1)}.get(z % 4),
+    )
+    held = pivot_spread(held, (5,), x, y, z)
+    held, ends, outgoing = tie((held, ends, outgoing))
+    slot2 = jnp.where(zl == 0, from_right2, jnp.where(zl == 3, from_left2, from_left1))
+    slot3 = jnp.where(zl == 1, from_right2, jnp.where(zl == 2, from_left2, ends))
+    far = gather_y(jnp.concatenate([slot1, slot2, slot3], axis=0))
     first = swap(outgoing[: FIRST * size])
-    held = join_y(held, y)
-    held, across3 = tie((held, across3))
-    far = gather_y(jnp.concatenate([across2, across3], axis=0))
-    held = pivot_spread(held, (4,), x, y, z)
-    held, first = tie((held, first))
+    parts = join_core(held, core)
     main = swap(outgoing[FIRST * size :])
-    held = pivot_spread(held, (5,), x, y, z)
-    parts = join_core(held, core)
-    window = window_rows(window, x, core)
 
     other_count, other_place, _ = crossing(other_slots, 1 - sub, blocks)
     need = jnp.maximum(own_count, other_count)
     step = jnp.arange(blocks, dtype=jnp.int32)
-    shift = (step // NEAR) * 2 + step % 2
-    block = ((col // NY) ^ shift) * NY + (step % NEAR) // 2
+    later = jnp.maximum(step - NEAR, 0)
+    shift = jnp.where(step < NEAR, 0, 1 + later % 3)
+    slots_z = jnp.array([[0, 1, 2, 3], [1, 2, 0, 3], [2, 3, 1, 0], [3, 2, 1, 0]], jnp.int32)[zl]
+    step_z = jnp.sum(jnp.where(shift[:, None] == jnp.arange(4)[None, :], slots_z[None, :], 0), axis=1)
+    block = step_z * NY + jnp.where(step < NEAR, step, later // 3)
     target = sub * blocks + block
     own_has, own_index = lookup(own_slots, target)
     other_has, other_index = lookup(other_slots, target)
@@ -413,8 +427,7 @@
     ends = (FIRST, MAIN, other_place.shape[0])
     inside = [other_has & (place >= low) & (place < high) for low, high in zip(starts, ends)]
     present = jnp.sum(jnp.where(block[:, None] == step[None, :], pattern[:, 0][None, :], 0), axis=1) == 1
-    rows = step % NEAR
-    rows = jnp.concatenate([kept(present[:NEAR], rows[:NEAR]), kept(present[NEAR:], rows[NEAR:])])
+    rows = jnp.concatenate([kept(present[:NEAR], step[:NEAR]), kept(present[NEAR:], later[NEAR:])])
     table = jnp.stack(
         [
             block,

time: 219 us -> 222 us (1.014)
  the two profiles are of different devices: /device:TPU:41 before, /device:TPU:1 now
where the time goes in v4:
time: 222 us; the launch traced here: 219 us
  waiting for transfers between devices  69.3 us (31%)
  Pallas kernels  54.7 us (25%)
  starting transfers between devices  50.4 us (23%)
  other arithmetic  19.2 us (9%)
  between operations  16 us (7%)
  local copies, waits for them, and re-layouts  9.71 us (4%)
    ppermute x21, waiting for transfers between devices, send(): return lax.ppermute(value, ALL, pairs_of(move))  69.3 us
    ppermute x21, starting transfers between devices, send(): return lax.ppermute(value, ALL, pairs_of(move))  40.7 us
    pallas_call x1, Pallas kernels, pivot_inverse(): pl.pallas_call(pivot_kernel, out_shape=jax.ShapeDtypeStruct((width, width...  26.9 us
    pallas_call x1, Pallas kernels, update_far(): pl.pallas_call(far_kernel, grid_spec=pltpu.PrefetchScalarGridSpec(num_sca...  16.4 us
    ppermute x1, starting transfers between devices, window_owned(): return lax.ppermute(panel, ALL, sorted(place.items()))  9.68 us
    pallas_call x1, Pallas kernels, update_near(): pl.pallas_call(near_kernel, grid_spec=pltpu.PrefetchScalarGridSpec(num_sc...  5.73 us
  transfers between devices with their start and end apart: 24, of which 11 were waited for; matrix products, arithmetic and copies ran while one was open for 10% of the time, Pallas kernels for 17%

profile of v4, /device:TPU:1, one launch (start us, length us, event | category | flops | bytes accessed | tf_op | source)
XLA Modules:
  0.0 219.3 jit_solution(9351418036965670084)
XLA Ops:
  11.6 9.7 %collective-permute-start.4 = (f32[256,512]{1,0:T(8,128)S(1)}, f32[256,512]{1,0:T(8,128)S(1)}, u32[]{:S(2)}, u32[]{:S(2)}) collective-permute-start(f32[256,512]{1,0:T(8,128)S(1)} %copy-done), channel_id=1, source_target_pairs={{2,0},{3,1},{4,2},{5,3},{6,4},{7,5},{8,6},{9,7},{10,8},{11,9},{12,... | collective-permute-start | bytes 1572872 | tf_op jit(solution)/shard_map/ppermute | solution.py:326
  22.7 9.5 %collective-permute-done.3 = f32[128,384]{1,0:T(8,128)S(1)} collective-permute-done((f32[128,384]{1,0:T(8,128)S(1)}, f32[128,384]{1,0:T(8,128)S(1)}, u32[]{:S(2)}, u32[]{:S(2)}) %collective-permute-start.3) | collective-permute-done | bytes 196640 | tf_op jit(solution)/shard_map/ppermute | solution.py:32
  34.3 1.8 collective-permute-done.5
  37.5 4.6 %collective-permute-done.6 = f32[128,384]{1,0:T(8,128)S(1)} collective-permute-done((f32[128,384]{1,0:T(8,128)S(1)}, f32[128,384]{1,0:T(8,128)S(1)}, u32[]{:S(2)}, u32[]{:S(2)}) %collective-permute-start.6) | collective-permute-done | bytes 196640 | tf_op jit(solution)/shard_map/ppermute | solution.py:32
  43.5 3.5 %collective-permute-done.8 = f32[128,384]{1,0:T(8,128)S(1)} collective-permute-done((f32[128,384]{1,0:T(8,128)S(1)}, f32[128,384]{1,0:T(8,128)S(1)}, u32[]{:S(2)}, u32[]{:S(2)}) %collective-permute-start.8) | collective-permute-done | bytes 196640 | tf_op jit(solution)/shard_map/ppermute | solution.py:32
  47.0 3.5 %collective-permute-start.9 = (f32[128,384]{1,0:T(8,128)S(1)}, f32[128,384]{1,0:T(8,128)S(1)}, u32[]{:S(2)}, u32[]{:S(2)}) collective-permute-start(f32[128,384]{1,0:T(8,128)S(1)} %broadcast_select_fusion.13), channel_id=1, source_target_pairs={{0,1},{4,5},{8,9},{12,13},{128,129},{132,133},{136,137},{140,141},... | collective-permute-start | bytes 589832 | tf_op jit(solution)/shard_map/ppermute | solution.py:32
  52.6 4.8 %collective-permute-start.10 = (f32[256,512]{1,0:T(8,128)S(1)}, f32[256,512]{1,0:T(8,128)}, u32[]{:S(2)}, u32[]{:S(2)}) collective-permute-start(f32[256,512]{1,0:T(8,128)S(1)} %copy-done), channel_id=1, source_target_pairs={{0,4},{4,8},{8,12},{128,132},{132,136},{136,140},{1,5},{5,9},{9,13... | collective-permute-start | bytes 1572872 | tf_op jit(solution)/shard_map/ppermute | solution.py:32
  57.6 3.7 %collective-permute-done.11 = f32[256,512]{1,0:T(8,128)} collective-permute-done((f32[256,512]{1,0:T(8,128)S(1)}, f32[256,512]{1,0:T(8,128)}, u32[]{:S(2)}, u32[]{:S(2)}) %collective-permute-start.11) | collective-permute-done | bytes 524320 | tf_op jit(solution)/shard_map/ppermute | solution.py:32
  61.4 1.4 collective-permute-done.10
  62.7 1.3 collective-permute-start.13
  64.0 1.5 collective-permute-start.16
  66.2 1.5 collective-permute-start.14
  70.4 22.2 %collective-permute-done.15 = f32[256,512]{1,0:T(8,128)} collective-permute-done((f32[256,512]{1,0:T(8,128)}, f32[256,512]{1,0:T(8,128)}, u32[]{:S(2)}, u32[]{:S(2)}) %collective-permute-start.15) | collective-permute-done | bytes 524320 | tf_op jit(solution)/shard_map/ppermute | solution.py:32
  92.7 1.3 collective-permute-start.17
  97.1 2.8 %shard_map.77 = f32[1536,256]{1,0:T(8,128)} custom-call(s32[6]{0:T(128)S(1)} %bitcast.57, f32[2048,256]{1,0:T(8,128)S(1)} %bitcast.48), custom_call_target="tpu_custom_call" | custom-call | tf_op jit(solution)/shard_map/pallas_call | solution.py:149
  100.0 6.7 %collective-permute-done.18 = f32[256,512]{1,0:T(8,128)S(1)} collective-permute-done((f32[256,512]{1,0:T(8,128)S(1)}, f32[256,512]{1,0:T(8,128)S(1)}, u32[]{:S(2)}, u32[]{:S(2)}) %collective-permute-start.18) | collective-permute-done | bytes 524320 | tf_op jit(solution)/shard_map/ppermute | solution.py:32
  106.7 1.8 select_select_fusion.1
  108.5 1.4 pad_maximum_fusion.1
  109.9 1.5 collective-permute-start.21
  114.0 2.3 %collective-permute-done.21 = s32[1,8]{1,0:T(1,128)S(1)} collective-permute-done((s32[1,8]{1,0:T(1,128)S(1)}, s32[1,8]{1,0:T(1,128)S(1)}, u32[]{:S(2)}, u32[]{:S(2)}) %collective-permute-start.21) | collective-permute-done | bytes 64 | tf_op jit(solution)/shard_map/ppermute | solution.py:32
  122.4 2.4 %slice.60 = f32[1024,256]{1,0:T(8,128)} slice(f32[1536,256]{1,0:T(8,128)} %shard_map.77), slice={[512:1536], [0:256]} | slice | bytes 2097152 | tf_op jit(solution)/shard_map/slice | solution.py:409
  124.8 1.5 collective-permute-start.22
  128.8 8.1 %collective-permute-start.19 = (f32[2,128,384]{2,1,0:T(8,128)S(1)}, f32[2,128,384]{2,1,0:T(8,128)}, u32[]{:S(2)}, u32[]{:S(2)}) collective-permute-start(f32[2,128,384]{2,1,0:T(8,128)S(1)} %broadcast_select_fusion.7), channel_id=1, source_target_pairs={{0,16},{4,20},{8,24},{12,28},{128,144},{132,148},{136,152},{140,15... | collective-permute-start | bytes 1179656 | tf_op jit(solution)/shard_map/ppermute | solution.py:32
  137.4 1.9 stack.27.table
  139.3 1.9 slice.61
  141.3 2.7 %collective-permute-start.23 = (f32[512,256]{1,0:T(8,128)}, f32[512,256]{1,0:T(8,128)}, u32[]{:S(2)}, u32[]{:S(2)}) collective-permute-start(f32[512,256]{1,0:T(8,128)} %slice.61), channel_id=1, source_target_pairs={{0,128},{4,132},{8,136},{12,140},{128,0},{132,4},{136,8},{140,12},... | collective-permute-start | bytes 1572872 | tf_op jit(solution)/shard_map/ppermute | solution.py:32
  146.2 26.9 %shard_map.78.inverse_ref = f32[512,512]{1,0:T(8,128)S(1)} custom-call(f32[2,256,384]{2,1,0:T(8,128)S(1)} %pad_maximum_fusion.2.parts_ref), custom_call_target="tpu_custom_call" | custom-call | tf_op jit(solution)/shard_map/pallas_call | solution.py:116
  173.1 2.8 %shard_map.79 = (f32[256,512]{1,0:T(8,128)}, f32[256,512]{1,0:T(8,128)S(1)}) custom-call(f32[512,512]{1,0:T(8,128)S(1)} %shard_map.78.inverse_ref, f32[256,512]{1,0:T(8,128)S(1)} %copy-done, f32[256,512]{1,0:T(8,128)S(1)} %broadcast_select_fusion.1.window_ref), custom_call_target="tpu_custom_call" | custom-call | tf_op jit(solution)/shard_map/pallas_call | solution.py:136
  176.8 5.7 %shard_map.80.done_ref = f32[4096,256]{1,0:T(8,128)} custom-call(s32[9,16]{1,0:T(8,128)} %stack.27.table, f32[1024,512]{1,0:T(8,128)} %all-gather.3.cloned.1.call-done.rows_ref, f32[256,512]{1,0:T(8,128)} %copy-done.1, f32[4096,256]{1,0:T(8,128)} %trailing_ref.3, f32[2048,256]{1,0:T(8,128)S(1)} %bitcast.49), custom_call_target="tpu_custom_call" | custom-call | tf_op jit(solution)/shard_map/pallas_call | solution.py:182
  182.5 2.4 %collective-permute-done.22.main_ref = f32[1024,256]{1,0:T(8,128)} collective-permute-done((f32[1024,256]{1,0:T(8,128)}, f32[1024,256]{1,0:T(8,128)}, u32[]{:S(2)}, u32[]{:S(2)}) %collective-permute-start.22) | collective-permute-done | bytes 1048608 | tf_op jit(solution)/shard_map/ppermute | solution.py:32
  184.9 11.2 %collective-permute-done.23.first_ref = f32[512,256]{1,0:T(8,128)} collective-permute-done((f32[512,256]{1,0:T(8,128)}, f32[512,256]{1,0:T(8,128)}, u32[]{:S(2)}, u32[]{:S(2)}) %collective-permute-start.23) | collective-permute-done | bytes 524320 | tf_op jit(solution)/shard_map/ppermute | solution.py:32
  196.1 16.4 %shard_map.81 = f32[4096,256]{1,0:T(8,128)} custom-call(s32[9,16]{1,0:T(8,128)} %stack.27.table, f32[4096,256]{1,0:T(8,128)} %shard_map.80.done_ref, f32[3072,512]{1,0:T(8,128)} %all-gather.5.cloned.1.call-done.rows_ref, f32[256,512]{1,0:T(8,128)} %copy-done.1, f32[4096,256]{1,0:T(8,128)} %trailing_ref.3, ...), custom_call_target="tpu_custom_call", output_to_operand_aliasing={{}: (1, {})} | custom-call | tf_op jit(solution)/shard_map/pallas_call | solution.py:230
  (107 shorter events, 32.7 us)
Async XLA Ops:
  7.2 4.4 %copy-start = (f32[256,512]{1,0:T(8,128)S(1)}, f32[256,512]{1,0:T(8,128)}, u32[]{:S(2)}) copy-start(f32[256,512]{1,0:T(8,128)} %panel_ref.1) | copy-start | bytes 1572868
  7.2 55.6 %all-gather.3.cloned.1.call-start = ((), (), s32[]{:S(2)}) async-start(), calls=%async_computation | async-start | bytes 2621440 | tf_op jit(solution)/shard_map/all_gather | solution.py:348
  10.2 11.1 %collective-permute-start.2 = (f32[128,384]{1,0:T(8,128)S(1)}, f32[128,384]{1,0:T(8,128)S(1)}, u32[]{:S(2)}, u32[]{:S(2)}) collective-permute-start(f32[128,384]{1,0:T(8,128)S(1)} %slice.63), channel_id=1, source_target_pairs={{0,16},{1,17}} | collective-permute-start | bytes 589832 | tf_op jit(solution)/shard_map/ppermute | solution.py:32
  11.5 184.6 %all-gather.5.cloned.1.call-start = ((), (), s32[]{:S(2)}) async-start(), calls=%async_computation.1 | async-start | bytes 7864320 | tf_op jit(solution)/shard_map/all_gather | solution.py:348
  11.6 20.6 %collective-permute-start.4 = (f32[256,512]{1,0:T(8,128)S(1)}, f32[256,512]{1,0:T(8,128)S(1)}, u32[]{:S(2)}, u32[]{:S(2)}) collective-permute-start(f32[256,512]{1,0:T(8,128)S(1)} %copy-done), channel_id=1, source_target_pairs={{2,0},{3,1},{4,2},{5,3},{6,4},{7,5},{8,6},{9,7},{10,8},{11,9},{12,... | collective-permute-start | bytes 1572872 | tf_op jit(solution)/shard_map/ppermute | solution.py:326
  21.4 10.8 %collective-permute-start.3 = (f32[128,384]{1,0:T(8,128)S(1)}, f32[128,384]{1,0:T(8,128)S(1)}, u32[]{:S(2)}, u32[]{:S(2)}) collective-permute-start(f32[128,384]{1,0:T(8,128)S(1)} %slice_select_fusion), channel_id=1, source_target_pairs={{0,128},{1,129},{16,144},{17,145}} | collective-permute-start | bytes 589832 | tf_op jit(solution)/shard_map/ppermute | solution.py:32
  32.2 3.9 %collective-permute-start.5 = (f32[128,384]{1,0:T(8,128)S(1)}, f32[128,384]{1,0:T(8,128)S(1)}, u32[]{:S(2)}, u32[]{:S(2)}) collective-permute-start(f32[128,384]{1,0:T(8,128)S(1)} %broadcast_select_fusion.10), channel_id=1, source_target_pairs={{0,8},{128,136},{1,9},{129,137},{16,24},{144,152},{17,25},{145,153}} | collective-permute-start | bytes 589832 | tf_op jit(solution)/shard_map/ppermute | solution.py:32
  33.6 8.5 %collective-permute-start.7 = (f32[256,512]{1,0:T(8,128)S(1)}, f32[256,512]{1,0:T(8,128)S(1)}, u32[]{:S(2)}, u32[]{:S(2)}) collective-permute-start(f32[256,512]{1,0:T(8,128)S(1)} %collective-permute-done.4), channel_id=1, source_target_pairs={{0,128},{4,132},{8,136},{12,140},{1,129},{5,133},{9,137},{13,141},... | collective-permute-start | bytes 1572872 | tf_op jit(solution)/shard_map/ppermute | solution.py:32
  36.1 5.9 %collective-permute-start.6 = (f32[128,384]{1,0:T(8,128)S(1)}, f32[128,384]{1,0:T(8,128)S(1)}, u32[]{:S(2)}, u32[]{:S(2)}) collective-permute-start(f32[128,384]{1,0:T(8,128)S(1)} %broadcast_select_fusion.11), channel_id=1, source_target_pairs={{0,4},{8,12},{128,132},{136,140},{1,5},{9,13},{129,133},{137,141},... | collective-permute-start | bytes 589832 | tf_op jit(solution)/shard_map/ppermute | solution.py:32
  42.2 4.8 %collective-permute-start.8 = (f32[128,384]{1,0:T(8,128)S(1)}, f32[128,384]{1,0:T(8,128)S(1)}, u32[]{:S(2)}, u32[]{:S(2)}) collective-permute-start(f32[128,384]{1,0:T(8,128)S(1)} %broadcast_select_fusion.12), channel_id=1, source_target_pairs={{0,2},{4,6},{8,10},{12,14},{128,130},{132,134},{136,138},{140,142}... | collective-permute-start | bytes 589832 | tf_op jit(solution)/shard_map/ppermute | solution.py:32
  47.0 10.4 %collective-permute-start.9 = (f32[128,384]{1,0:T(8,128)S(1)}, f32[128,384]{1,0:T(8,128)S(1)}, u32[]{:S(2)}, u32[]{:S(2)}) collective-permute-start(f32[128,384]{1,0:T(8,128)S(1)} %broadcast_select_fusion.13), channel_id=1, source_target_pairs={{0,1},{4,5},{8,9},{12,13},{128,129},{132,133},{136,137},{140,141},... | collective-permute-start | bytes 589832 | tf_op jit(solution)/shard_map/ppermute | solution.py:32
  50.5 7.0 %collective-permute-start.12 = (f32[256,512]{1,0:T(8,128)S(1)}, f32[256,512]{1,0:T(8,128)S(1)}, u32[]{:S(2)}, u32[]{:S(2)}) collective-permute-start(f32[256,512]{1,0:T(8,128)S(1)} %broadcast_select_fusion.5), channel_id=1, source_target_pairs={{0,64},{4,68},{8,72},{12,76},{128,192},{132,196},{136,200},{140,20... | collective-permute-start | bytes 1572872 | tf_op jit(solution)/shard_map/ppermute | solution.py:32
  51.3 14.2 %copy-start.4 = (s32[1,8]{1,0:T(1,128)S(1)}, s32[1,8]{1,0:T(1,128)}, u32[]{:S(2)}) copy-start(s32[1,8]{1,0:T(1,128)} %param.13) | copy-start | bytes 100
  51.3 10.0 %collective-permute-start.11 = (f32[256,512]{1,0:T(8,128)S(1)}, f32[256,512]{1,0:T(8,128)}, u32[]{:S(2)}, u32[]{:S(2)}) collective-permute-start(f32[256,512]{1,0:T(8,128)S(1)} %copy-done), channel_id=1, source_target_pairs={{4,0},{8,4},{12,8},{132,128},{136,132},{140,136},{5,1},{9,5},{13,9... | collective-permute-start | bytes 1572872 | tf_op jit(solution)/shard_map/ppermute | solution.py:32
  52.6 10.1 %collective-permute-start.10 = (f32[256,512]{1,0:T(8,128)S(1)}, f32[256,512]{1,0:T(8,128)}, u32[]{:S(2)}, u32[]{:S(2)}) collective-permute-start(f32[256,512]{1,0:T(8,128)S(1)} %copy-done), channel_id=1, source_target_pairs={{0,4},{4,8},{8,12},{128,132},{132,136},{136,140},{1,5},{5,9},{9,13... | collective-permute-start | bytes 1572872 | tf_op jit(solution)/shard_map/ppermute | solution.py:32
  57.6 11.5 %copy-start.3 = (f32[256,512]{1,0:T(8,128)}, f32[256,512]{1,0:T(8,128)S(1)}, u32[]{:S(2)}) copy-start(f32[256,512]{1,0:T(8,128)S(1)} %broadcast_select_fusion.4) | copy-start | bytes 1572868
  62.7 6.3 %collective-permute-start.13 = (f32[2,128,384]{2,1,0:T(8,128)S(1)}, f32[2,128,384]{2,1,0:T(8,128)S(1)}, u32[]{:S(2)}, u32[]{:S(2)}) collective-permute-start(f32[2,128,384]{2,1,0:T(8,128)S(1)} %pad_maximum_fusion.3), channel_id=1, source_target_pairs={{0,64},{4,68},{8,72},{12,76},{128,192},{132,196},{136,200},{140,20... | collective-permute-start | bytes 1179656 | tf_op jit(solution)/shard_map/ppermute | solution.py:32
  64.0 5.1 %collective-permute-start.16 = (f32[256,512]{1,0:T(8,128)S(1)}, f32[256,512]{1,0:T(8,128)}, u32[]{:S(2)}, u32[]{:S(2)}) collective-permute-start(f32[256,512]{1,0:T(8,128)S(1)} %broadcast_select_fusion.4), channel_id=1, source_target_pairs={{0,32},{4,36},{8,40},{12,44},{128,160},{132,164},{136,168},{140,17... | collective-permute-start | bytes 1572872 | tf_op jit(solution)/shard_map/ppermute | solution.py:32
  66.2 4.3 %collective-permute-start.14 = (f32[256,512]{1,0:T(8,128)}, f32[256,512]{1,0:T(8,128)}, u32[]{:S(2)}, u32[]{:S(2)}) collective-permute-start(f32[256,512]{1,0:T(8,128)} %collective-permute-done.10), channel_id=1, source_target_pairs={{4,8},{8,12},{132,136},{136,140},{5,9},{9,13},{133,137},{137,141},... | collective-permute-start | bytes 1572872 | tf_op jit(solution)/shard_map/ppermute | solution.py:32
  67.6 25.0 %collective-permute-start.15 = (f32[256,512]{1,0:T(8,128)}, f32[256,512]{1,0:T(8,128)}, u32[]{:S(2)}, u32[]{:S(2)}) collective-permute-start(f32[256,512]{1,0:T(8,128)} %collective-permute-done.11), channel_id=1, source_target_pairs={{4,0},{8,4},{132,128},{136,132},{5,1},{9,5},{133,129},{137,133},{6... | collective-permute-start | bytes 1572872 | tf_op jit(solution)/shard_map/ppermute | solution.py:32
  69.1 28.0 %copy-start.2 = (f32[1,2048,256]{2,1,0:T(8,128)S(1)}, f32[1,2048,256]{2,1,0:T(8,128)}, u32[]{:S(2)}) copy-start(f32[1,2048,256]{2,1,0:T(8,128)} %param.12) | copy-start | bytes 6291460
  92.7 7.3 %collective-permute-start.17 = (f32[2,128,384]{2,1,0:T(8,128)S(1)}, f32[2,128,384]{2,1,0:T(8,128)S(1)}, u32[]{:S(2)}, u32[]{:S(2)}) collective-permute-start(f32[2,128,384]{2,1,0:T(8,128)S(1)} %broadcast_select_fusion.6), channel_id=1, source_target_pairs={{0,32},{4,36},{8,40},{12,44},{128,160},{132,164},{136,168},{140,17... | collective-permute-start | bytes 1179656 | tf_op jit(solution)/shard_map/ppermute | solution.py:32
  95.1 11.6 %collective-permute-start.18 = (f32[256,512]{1,0:T(8,128)S(1)}, f32[256,512]{1,0:T(8,128)S(1)}, u32[]{:S(2)}, u32[]{:S(2)}) collective-permute-start(f32[256,512]{1,0:T(8,128)S(1)} %broadcast_select_fusion.2), channel_id=1, source_target_pairs={{4,0},{8,12},{132,128},{136,140},{5,1},{9,13},{133,129},{137,141},... | collective-permute-start | bytes 1572872 | tf_op jit(solution)/shard_map/ppermute | solution.py:32
  97.1 2.8 %copy-start.6 = (s32[8]{0:T(128)}, s32[8]{0:T(128)S(1)}, u32[]{:S(2)}) copy-start(s32[8]{0:T(128)S(1)} %select_reduce_fusion.7) | copy-start | bytes 100
  109.9 2.4 %copy-start.8 = (s32[16,1]{0,1:T(1,128)S(1)}, s32[16,1]{0,1:T(1,128)}, u32[]{:S(2)}) copy-start(s32[16,1]{0,1:T(1,128)} %param.14) | copy-start | bytes 196
  109.9 6.4 %collective-permute-start.21 = (s32[1,8]{1,0:T(1,128)S(1)}, s32[1,8]{1,0:T(1,128)S(1)}, u32[]{:S(2)}, u32[]{:S(2)}) collective-permute-start(s32[1,8]{1,0:T(1,128)S(1)} %copy-done.4), channel_id=1, source_target_pairs={{0,128},{4,132},{8,136},{12,140},{128,0},{132,4},{136,8},{140,12},... | collective-permute-start | bytes 104 | tf_op jit(solution)/shard_map/ppermute | solution.py:32
  118.5 18.9 %copy-start.5 = (s32[1,16]{1,0:T(1,128)S(1)}, s32[1,16]{1,0:T(1,128)}, u32[]{:S(2)}) copy-start(s32[1,16]{1,0:T(1,128)} %fusion.13) | copy-start | bytes 196
  121.1 22.8 %collective-permute-start.20 = (f32[256,512]{1,0:T(8,128)S(1)}, f32[256,512]{1,0:T(8,128)}, u32[]{:S(2)}, u32[]{:S(2)}) collective-permute-start(f32[256,512]{1,0:T(8,128)S(1)} %broadcast_select_fusion.3), channel_id=1, source_target_pairs={{0,16},{4,20},{8,24},{12,28},{128,144},{132,148},{136,152},{140,15... | collective-permute-start | bytes 1572872 | tf_op jit(solution)/shard_map/ppermute | solution.py:32
  124.8 60.1 %collective-permute-start.22 = (f32[1024,256]{1,0:T(8,128)}, f32[1024,256]{1,0:T(8,128)}, u32[]{:S(2)}, u32[]{:S(2)}) collective-permute-start(f32[1024,256]{1,0:T(8,128)} %slice.60), channel_id=1, source_target_pairs={{0,128},{4,132},{8,136},{12,140},{128,0},{132,4},{136,8},{140,12},... | collective-permute-start | bytes 3145736 | tf_op jit(solution)/shard_map/ppermute | solution.py:32
  128.8 16.3 %collective-permute-start.19 = (f32[2,128,384]{2,1,0:T(8,128)S(1)}, f32[2,128,384]{2,1,0:T(8,128)}, u32[]{:S(2)}, u32[]{:S(2)}) collective-permute-start(f32[2,128,384]{2,1,0:T(8,128)S(1)} %broadcast_select_fusion.7), channel_id=1, source_target_pairs={{0,16},{4,20},{8,24},{12,28},{128,144},{132,148},{136,152},{140,15... | collective-permute-start | bytes 1179656 | tf_op jit(solution)/shard_map/ppermute | solution.py:32
  141.3 54.9 %collective-permute-start.23 = (f32[512,256]{1,0:T(8,128)}, f32[512,256]{1,0:T(8,128)}, u32[]{:S(2)}, u32[]{:S(2)}) collective-permute-start(f32[512,256]{1,0:T(8,128)} %slice.61), channel_id=1, source_target_pairs={{0,128},{4,132},{8,136},{12,140},{128,0},{132,4},{136,8},{140,12},... | collective-permute-start | bytes 1572872 | tf_op jit(solution)/shard_map/ppermute | solution.py:32
  176.8 8.1 %copy-start.7 = (s32[8]{0:T(128)S(1)}, s32[8]{0:T(128)}, u32[]{:S(2)}) copy-start(s32[8]{0:T(128)} %copy-done.6) | copy-start | bytes 100
  (1 other events, 0.8 us)
Sparse Core Ops, SparseCore 0:
  11.7 37.1 all-gather.2
  110.0 69.9 all-gather.4

commit v5 on v4

--- a/solution.py
+++ b/solution.py
@@ -9,7 +9,7 @@
 ALL = ("sub", "row", "col")
 SB = 128
 NX, NY, NZ = 4, 4, 8
-FIRST, MAIN = 2, 6
+FIRST, MAIN = 1, 6
 
 
 def linear(x, core, y, z):
@@ -369,8 +369,8 @@
     x, core, y, z = row // 2, row % 2, col % NY, sub * 4 + col // NY
     own_slots = child_map[0]
     own_count, own_place, order = crossing(own_slots, sub, blocks)
-    outgoing = take_blocks(order[:MAIN], child[0], size)
-    other_slots = swap(child_map)[0]
+    outgoing = [take_blocks(order[low:high], child[0], size) for low, high in ((0, FIRST), (FIRST, MAIN))]
+    other_slots = swap(child_map)
 
     tie = lax.optimization_barrier
     zl = z % 4
@@ -380,33 +380,10 @@
     held = pivot_split(panel, core, y)
     window = window_owned(panel)
     held = pivot_spread(held, (0,), x, y, z)
-    held, window = tie((held, window))
+    held, window, other_slots = tie((held, window, other_slots))
+    other_slots = other_slots[0]
     window = window_halves(window, z)
-    held = pivot_spread(held, (1, 2), x, y, z)
-    held, window, bulk = tie((held, window, panel))
-    window = window_x(window, x, 2)
-    from_left1, from_right1 = right(bulk, (0, 1, 2)), left(bulk, (1, 2, 3))
-    held = pivot_spread(held, (3,), x, y, z)
-    held = join_y(held, y)
-    held, from_left1, from_right1, near, window = tie((held, from_left1, from_right1, near, window))
-    slot1 = jnp.where(zl == 3, from_left1, from_right1)
-    window = window_x(window, x, 1)
-    from_left2, from_right2 = right(from_left1, (1, 2)), left(from_right1, (1, 2))
-    held = pivot_spread(held, (4,), x, y, z)
-    held, from_left2, from_right2, window = tie((held, from_left2, from_right2, window))
-    window = window_core(window, core)
-    ends = send(
-        jnp.where(zl == 2, from_left2, from_right2),
-        lambda x, c, y, z: {1: (x, c, y, z - 1), 2: (x, c, y, z + 1)}.get(z % 4),
-    )
-    held = pivot_spread(held, (5,), x, y, z)
-    held, ends, outgoing = tie((held, ends, outgoing))
-    slot2 = jnp.where(zl == 0, from_right2, jnp.where(zl == 3, from_left2, from_left1))
-    slot3 = jnp.where(zl == 1, from_right2, jnp.where(zl == 2, from_left2, ends))
-    far = gather_y(jnp.concatenate([slot1, slot2, slot3], axis=0))
-    first = swap(outgoing[: FIRST * size])
-    parts = join_core(held, core)
-    main = swap(outgoing[FIRST * size :])
+    held = pivot_spread(held, (1,), x, y, z)
 
     other_count, other_place, _ = crossing(other_slots, 1 - sub, blocks)
     need = jnp.maximum(own_count, other_count)
@@ -440,6 +417,32 @@
         ]
     ).astype(jnp.int32)
 
+    held, table, need, outgoing = tie((held, table, need, outgoing))
+    held = pivot_spread(held, (2,), x, y, z)
+    held, window, bulk = tie((held, window, panel))
+    from_left1, from_right1 = right(bulk, (0, 1, 2)), left(bulk, (1, 2, 3))
+    held = pivot_spread(held, (3,), x, y, z)
+    window = window_x(window, x, 2)
+    held, from_left1, from_right1 = tie((held, from_left1, from_right1))
+    from_left2, from_right2 = right(from_left1, (1, 2)), left(from_right1, (1, 2))
+    held = join_y(held, y)
+    held, from_left2, from_right2, near, window = tie((held, from_left2, from_right2, near, window))
+    last = send(
+        jnp.where(zl == 2, from_left2, from_right2),
+        lambda x, c, y, z: {1: (x, c, y, z - 1), 2: (x, c, y, z + 1)}.get(z % 4),
+    )
+    held = pivot_spread(held, (4,), x, y, z)
+    window = window_x(window, x, 1)
+    held, last, window, outgoing = tie((held, last, window, outgoing))
+    slot1 = jnp.where(zl == 3, from_left1, from_right1)
+    slot2 = jnp.where(zl == 0, from_right2, jnp.where(zl == 3, from_left2, from_left1))
+    slot3 = jnp.where(zl == 1, from_right2, jnp.where(zl == 2, from_left2, last))
+    far = gather_y(jnp.concatenate([slot1, slot2, slot3], axis=0))
+    first = swap(outgoing[0])
+    main = swap(outgoing[1])
+    window = window_core(window, core)
+    held = pivot_spread(held, (5,), x, y, z)
+    parts = join_core(held, core)
     inverse = pivot_inverse(parts)
     factor, weight = solve(inverse, panel, window)
     done = update_near(table, near, weight, trailing, child[0])

time: 222 us -> 215 us (0.968)
  waiting for transfers between devices: 69.3 us -> 59.6 us
  starting transfers between devices: 50.4 us -> 59.1 us
  local copies, waits for them, and re-layouts: 9.71 us -> 6.22 us
    ppermute x21, waiting for transfers between devices: 69.3 us -> 58.8 us  [send(): return lax.ppermute(value, ALL, pairs_of(move))]
    ppermute x21, starting transfers between devices: 40.7 us -> 47.9 us  [send(): return lax.ppermute(value, ALL, pairs_of(move))]
    slice x2 -> x1, local copies, waits for them, and re-layouts: 4.32 us -> 0.59 us  [local(): order[low:high]]
    select_n x6, other arithmetic: 2.3 us -> 0.07 us  [kept(): return jnp.where(latest >= 0, latest % blocks, 0)]
  transfers between devices with their start and end apart: 24 -> 24, of which waited for: 11 -> 8; matrix products, arithmetic and copies ran while one was open for 10% -> 9% of each run, Pallas kernels for 17% -> 18%
where the time goes in v5:
time: 215 us; the launch traced here: 213 us
  waiting for transfers between devices  59.6 us (28%)
  starting transfers between devices  59.1 us (27%)
  Pallas kernels  54 us (25%)
  other arithmetic  17.8 us (8%)
  between operations  16 us (7%)
  local copies, waits for them, and re-layouts  6.22 us (3%)
    ppermute x21, waiting for transfers between devices, send(): return lax.ppermute(value, ALL, pairs_of(move))  58.8 us
    ppermute x21, starting transfers between devices, send(): return lax.ppermute(value, ALL, pairs_of(move))  47.9 us
    pallas_call x1, Pallas kernels, pivot_inverse(): pl.pallas_call(pivot_kernel, out_shape=jax.ShapeDtypeStruct((width, width...  26.9 us
    pallas_call x1, Pallas kernels, update_far(): pl.pallas_call(far_kernel, grid_spec=pltpu.PrefetchScalarGridSpec(num_sca...  15.1 us
    ppermute x1, starting transfers between devices, window_owned(): return lax.ppermute(panel, ALL, sorted(place.items()))  11.1 us
    pallas_call x1, Pallas kernels, update_near(): pl.pallas_call(near_kernel, grid_spec=pltpu.PrefetchScalarGridSpec(num_sc...  5.5 us
  transfers between devices with their start and end apart: 24, of which 8 were waited for; matrix products, arithmetic and copies ran while one was open for 9% of the time, Pallas kernels for 18%

profile of v5, /device:TPU:1, one launch (start us, length us, event | category | flops | bytes accessed | tf_op | source)
XLA Modules:
  0.0 212.7 jit_solution(8072221531224926305)
XLA Ops:
  8.0 11.1 %collective-permute-start.4 = (f32[256,512]{1,0:T(8,128)}, f32[256,512]{1,0:T(8,128)}, u32[]{:S(2)}, u32[]{:S(2)}) collective-permute-start(f32[256,512]{1,0:T(8,128)} %panel_ref.1), channel_id=1, source_target_pairs={{2,0},{3,1},{4,2},{5,3},{6,4},{7,5},{8,6},{9,7},{10,8},{11,9},{12,... | collective-permute-start | bytes 1572872 | tf_op jit(solution)/shard_map/ppermute | solution.py:326
  21.1 1.3 collective-permute-start.2
  26.8 2.9 %shard_map.78 = f32[1280,256]{1,0:T(8,128)} custom-call(s32[5]{0:T(128)} %slice.57.order, f32[2048,256]{1,0:T(8,128)S(1)} %bitcast.49), custom_call_target="tpu_custom_call" | custom-call | tf_op jit(solution)/shard_map/pallas_call | solution.py:149
  30.4 6.7 %collective-permute-start.3 = (f32[128,384]{1,0:T(8,128)S(1)}, f32[128,384]{1,0:T(8,128)S(1)}, u32[]{:S(2)}, u32[]{:S(2)}) collective-permute-start(f32[128,384]{1,0:T(8,128)S(1)} %slice_select_fusion), channel_id=1, source_target_pairs={{0,128},{1,129},{16,144},{17,145}} | collective-permute-start | bytes 589832 | tf_op jit(solution)/shard_map/ppermute | solution.py:32
  37.1 2.6 %collective-permute-done.3 = f32[128,384]{1,0:T(8,128)S(1)} collective-permute-done((f32[128,384]{1,0:T(8,128)S(1)}, f32[128,384]{1,0:T(8,128)S(1)}, u32[]{:S(2)}, u32[]{:S(2)}) %collective-permute-start.3) | collective-permute-done | bytes 196640 | tf_op jit(solution)/shard_map/ppermute | solution.py:32
  43.6 1.3 collective-permute-start.6
  44.9 1.5 collective-permute-start.8
  47.9 1.3 collective-permute-start.7
  49.2 3.9 %collective-permute-done.7 = f32[128,384]{1,0:T(8,128)S(1)} collective-permute-done((f32[128,384]{1,0:T(8,128)S(1)}, f32[128,384]{1,0:T(8,128)S(1)}, u32[]{:S(2)}, u32[]{:S(2)}) %collective-permute-start.7) | collective-permute-done | bytes 196640 | tf_op jit(solution)/shard_map/ppermute | solution.py:32
  54.3 1.3 collective-permute-start.11
  55.6 5.3 %collective-permute-start.10 = (f32[256,512]{1,0:T(8,128)S(1)}, f32[256,512]{1,0:T(8,128)}, u32[]{:S(2)}, u32[]{:S(2)}) collective-permute-start(f32[256,512]{1,0:T(8,128)S(1)} %copy-done), channel_id=1, source_target_pairs={{0,4},{4,8},{8,12},{128,132},{132,136},{136,140},{1,5},{5,9},{9,13... | collective-permute-start | bytes 1572872 | tf_op jit(solution)/shard_map/ppermute | solution.py:32
  60.9 1.5 collective-permute-start.15
  63.8 2.5 %collective-permute-done.9 = f32[128,384]{1,0:T(8,128)S(1)} collective-permute-done((f32[128,384]{1,0:T(8,128)S(1)}, f32[128,384]{1,0:T(8,128)S(1)}, u32[]{:S(2)}, u32[]{:S(2)}) %collective-permute-start.9) | collective-permute-done | bytes 196640 | tf_op jit(solution)/shard_map/ppermute | solution.py:32
  66.3 2.3 %collective-permute-start.12 = (f32[128,384]{1,0:T(8,128)S(1)}, f32[128,384]{1,0:T(8,128)S(1)}, u32[]{:S(2)}, u32[]{:S(2)}) collective-permute-start(f32[128,384]{1,0:T(8,128)S(1)} %broadcast_select_fusion.13), channel_id=1, source_target_pairs={{0,1},{4,5},{8,9},{12,13},{128,129},{132,133},{136,137},{140,141},... | collective-permute-start | bytes 589832 | tf_op jit(solution)/shard_map/ppermute | solution.py:32
  68.6 1.5 collective-permute-start.13
  72.8 21.4 %collective-permute-done.14 = f32[256,512]{1,0:T(8,128)} collective-permute-done((f32[256,512]{1,0:T(8,128)}, f32[256,512]{1,0:T(8,128)}, u32[]{:S(2)}, u32[]{:S(2)}) %collective-permute-start.14) | collective-permute-done | bytes 524320 | tf_op jit(solution)/shard_map/ppermute | solution.py:32
  94.3 2.0 collective-permute-start.16
  96.3 1.5 collective-permute-start.18
  97.8 1.9 broadcast_select_fusion.3
  102.7 8.7 %collective-permute-done.17 = f32[256,512]{1,0:T(8,128)} collective-permute-done((f32[256,512]{1,0:T(8,128)}, f32[256,512]{1,0:T(8,128)}, u32[]{:S(2)}, u32[]{:S(2)}) %collective-permute-start.17) | collective-permute-done | bytes 524320 | tf_op jit(solution)/shard_map/ppermute | solution.py:32
  111.4 2.0 select_select_fusion.1
  113.3 1.4 pad_maximum_fusion.1
  115.7 1.3 collective-permute-start.19
  117.0 5.5 %collective-permute-start.22 = (f32[1280,256]{1,0:T(8,128)}, f32[1280,256]{1,0:T(8,128)}, u32[]{:S(2)}, u32[]{:S(2)}) collective-permute-start(f32[1280,256]{1,0:T(8,128)} %shard_map.78), channel_id=1, source_target_pairs={{0,128},{4,132},{8,136},{12,140},{128,0},{132,4},{136,8},{140,12},... | collective-permute-start | bytes 3932168 | tf_op jit(solution)/shard_map/ppermute | solution.py:32
  124.6 5.7 %collective-permute-start.20 = (f32[2,128,384]{2,1,0:T(8,128)}, f32[2,128,384]{2,1,0:T(8,128)S(1)}, u32[]{:S(2)}, u32[]{:S(2)}) collective-permute-start(f32[2,128,384]{2,1,0:T(8,128)} %broadcast_select_fusion.7), channel_id=1, source_target_pairs={{0,16},{4,20},{8,24},{12,28},{128,144},{132,148},{136,152},{140,15... | collective-permute-start | bytes 1179656 | tf_op jit(solution)/shard_map/ppermute | solution.py:32
  130.3 2.8 %collective-permute-start.23 = (f32[256,256]{1,0:T(8,128)}, f32[256,256]{1,0:T(8,128)}, u32[]{:S(2)}, u32[]{:S(2)}) collective-permute-start(f32[256,256]{1,0:T(8,128)} %shard_map.77), channel_id=1, source_target_pairs={{0,128},{4,132},{8,136},{12,140},{128,0},{132,4},{136,8},{140,12},... | collective-permute-start | bytes 786440 | tf_op jit(solution)/shard_map/ppermute | solution.py:32
  135.4 26.9 %shard_map.79.inverse_ref = f32[512,512]{1,0:T(8,128)S(1)} custom-call(f32[2,256,384]{2,1,0:T(8,128)S(1)} %pad_maximum_fusion.2.parts_ref), custom_call_target="tpu_custom_call" | custom-call | tf_op jit(solution)/shard_map/pallas_call | solution.py:116
  162.3 2.8 %shard_map.80 = (f32[256,512]{1,0:T(8,128)}, f32[256,512]{1,0:T(8,128)S(1)}) custom-call(f32[512,512]{1,0:T(8,128)S(1)} %shard_map.79.inverse_ref, f32[256,512]{1,0:T(8,128)S(1)} %copy-done, f32[256,512]{1,0:T(8,128)S(1)} %broadcast_select_fusion.1.window_ref), custom_call_target="tpu_custom_call" | custom-call | tf_op jit(solution)/shard_map/pallas_call | solution.py:136
  166.0 5.5 %shard_map.81.done_ref = f32[4096,256]{1,0:T(8,128)} custom-call(s32[9,16]{1,0:T(8,128)} %stack.11.table, f32[1024,512]{1,0:T(8,128)} %all-gather.3.cloned.1.call-done.rows_ref, f32[256,512]{1,0:T(8,128)} %copy-done.1, f32[4096,256]{1,0:T(8,128)} %trailing_ref.3, f32[2048,256]{1,0:T(8,128)S(1)} %bitcast.50), custom_call_target="tpu_custom_call" | custom-call | tf_op jit(solution)/shard_map/pallas_call | solution.py:182
  171.5 13.7 %collective-permute-done.22.main_ref = f32[1280,256]{1,0:T(8,128)} collective-permute-done((f32[1280,256]{1,0:T(8,128)}, f32[1280,256]{1,0:T(8,128)}, u32[]{:S(2)}, u32[]{:S(2)}) %collective-permute-start.22) | collective-permute-done | bytes 1310752 | tf_op jit(solution)/shard_map/ppermute | solution.py:32
  185.2 5.6 %collective-permute-done.23.first_ref = f32[256,256]{1,0:T(8,128)} collective-permute-done((f32[256,256]{1,0:T(8,128)}, f32[256,256]{1,0:T(8,128)}, u32[]{:S(2)}, u32[]{:S(2)}) %collective-permute-start.23) | collective-permute-done | bytes 262176 | tf_op jit(solution)/shard_map/ppermute | solution.py:32
  190.8 15.1 %shard_map.82 = f32[4096,256]{1,0:T(8,128)} custom-call(s32[9,16]{1,0:T(8,128)} %stack.11.table, f32[4096,256]{1,0:T(8,128)} %shard_map.81.done_ref, f32[3072,512]{1,0:T(8,128)} %all-gather.5.cloned.1.call-done.rows_ref, f32[256,512]{1,0:T(8,128)} %copy-done.1, f32[4096,256]{1,0:T(8,128)} %trailing_ref.3, ...), custom_call_target="tpu_custom_call", output_to_operand_aliasing={{}: (1, {})} | custom-call | tf_op jit(solution)/shard_map/pallas_call | solution.py:230
  (105 shorter events, 26.0 us)
Async XLA Ops:
  7.2 13.8 %copy-start = (f32[256,512]{1,0:T(8,128)S(1)}, f32[256,512]{1,0:T(8,128)}, u32[]{:S(2)}) copy-start(f32[256,512]{1,0:T(8,128)} %panel_ref.1) | copy-start | bytes 1572868
  7.2 15.3 %copy-start.6 = (s32[1,8]{1,0:T(1,128)S(1)}, s32[1,8]{1,0:T(1,128)}, u32[]{:S(2)}) copy-start(s32[1,8]{1,0:T(1,128)} %param.13) | copy-start | bytes 100
  7.2 16.8 %copy-start.7 = (s32[16,1]{0,1:T(1,128)S(1)}, s32[16,1]{0,1:T(1,128)}, u32[]{:S(2)}) copy-start(s32[16,1]{0,1:T(1,128)} %param.14) | copy-start | bytes 196
  7.2 18.9 %copy-start.2 = (f32[1,2048,256]{2,1,0:T(8,128)S(1)}, f32[1,2048,256]{2,1,0:T(8,128)}, u32[]{:S(2)}) copy-start(f32[1,2048,256]{2,1,0:T(8,128)} %param.12) | copy-start | bytes 6291460
  7.2 87.1 %all-gather.3.cloned.1.call-start = ((), (), s32[]{:S(2)}) async-start(), calls=%async_computation | async-start | bytes 2621440 | tf_op jit(solution)/shard_map/all_gather | solution.py:348
  7.9 182.8 %all-gather.5.cloned.1.call-start = ((), (), s32[]{:S(2)}) async-start(), calls=%async_computation.1 | async-start | bytes 7864320 | tf_op jit(solution)/shard_map/all_gather | solution.py:348
  8.0 31.7 %collective-permute-start.4 = (f32[256,512]{1,0:T(8,128)}, f32[256,512]{1,0:T(8,128)}, u32[]{:S(2)}, u32[]{:S(2)}) collective-permute-start(f32[256,512]{1,0:T(8,128)} %panel_ref.1), channel_id=1, source_target_pairs={{2,0},{3,1},{4,2},{5,3},{6,4},{7,5},{8,6},{9,7},{10,8},{11,9},{12,... | collective-permute-start | bytes 1572872 | tf_op jit(solution)/shard_map/ppermute | solution.py:326
  19.1 20.6 %collective-permute-start.5 = (s32[1,8]{1,0:T(1,128)}, s32[1,8]{1,0:T(1,128)S(1)}, u32[]{:S(2)}, u32[]{:S(2)}) collective-permute-start(s32[1,8]{1,0:T(1,128)} %param.13), channel_id=1, source_target_pairs={{0,128},{4,132},{8,136},{12,140},{128,0},{132,4},{136,8},{140,12},... | collective-permute-start | bytes 104 | tf_op jit(solution)/shard_map/ppermute | solution.py:32
  21.1 9.3 %collective-permute-start.2 = (f32[128,384]{1,0:T(8,128)S(1)}, f32[128,384]{1,0:T(8,128)S(1)}, u32[]{:S(2)}, u32[]{:S(2)}) collective-permute-start(f32[128,384]{1,0:T(8,128)S(1)} %slice.59), channel_id=1, source_target_pairs={{0,16},{1,17}} | collective-permute-start | bytes 589832 | tf_op jit(solution)/shard_map/ppermute | solution.py:32
  30.4 9.3 %collective-permute-start.3 = (f32[128,384]{1,0:T(8,128)S(1)}, f32[128,384]{1,0:T(8,128)S(1)}, u32[]{:S(2)}, u32[]{:S(2)}) collective-permute-start(f32[128,384]{1,0:T(8,128)S(1)} %slice_select_fusion), channel_id=1, source_target_pairs={{0,128},{1,129},{16,144},{17,145}} | collective-permute-start | bytes 589832 | tf_op jit(solution)/shard_map/ppermute | solution.py:32
  43.6 4.2 %collective-permute-start.6 = (f32[128,384]{1,0:T(8,128)S(1)}, f32[128,384]{1,0:T(8,128)S(1)}, u32[]{:S(2)}, u32[]{:S(2)}) collective-permute-start(f32[128,384]{1,0:T(8,128)S(1)} %broadcast_select_fusion.10), channel_id=1, source_target_pairs={{0,8},{128,136},{1,9},{129,137},{16,24},{144,152},{17,25},{145,153}} | collective-permute-start | bytes 589832 | tf_op jit(solution)/shard_map/ppermute | solution.py:32
  44.9 8.2 %collective-permute-start.8 = (f32[256,512]{1,0:T(8,128)}, f32[256,512]{1,0:T(8,128)}, u32[]{:S(2)}, u32[]{:S(2)}) collective-permute-start(f32[256,512]{1,0:T(8,128)} %collective-permute-done.4), channel_id=1, source_target_pairs={{0,128},{4,132},{8,136},{12,140},{1,129},{5,133},{9,137},{13,141},... | collective-permute-start | bytes 1572872 | tf_op jit(solution)/shard_map/ppermute | solution.py:32
  47.9 5.3 %collective-permute-start.7 = (f32[128,384]{1,0:T(8,128)S(1)}, f32[128,384]{1,0:T(8,128)S(1)}, u32[]{:S(2)}, u32[]{:S(2)}) collective-permute-start(f32[128,384]{1,0:T(8,128)S(1)} %broadcast_select_fusion.11), channel_id=1, source_target_pairs={{0,4},{8,12},{128,132},{136,140},{1,5},{9,13},{129,133},{137,141},... | collective-permute-start | bytes 589832 | tf_op jit(solution)/shard_map/ppermute | solution.py:32
  54.3 12.0 %collective-permute-start.11 = (f32[256,512]{1,0:T(8,128)S(1)}, f32[256,512]{1,0:T(8,128)}, u32[]{:S(2)}, u32[]{:S(2)}) collective-permute-start(f32[256,512]{1,0:T(8,128)S(1)} %copy-done), channel_id=1, source_target_pairs={{4,0},{8,4},{12,8},{132,128},{136,132},{140,136},{5,1},{9,5},{13,9... | collective-permute-start | bytes 1572872 | tf_op jit(solution)/shard_map/ppermute | solution.py:32
  55.6 10.7 %collective-permute-start.10 = (f32[256,512]{1,0:T(8,128)S(1)}, f32[256,512]{1,0:T(8,128)}, u32[]{:S(2)}, u32[]{:S(2)}) collective-permute-start(f32[256,512]{1,0:T(8,128)S(1)} %copy-done), channel_id=1, source_target_pairs={{0,4},{4,8},{8,12},{128,132},{132,136},{136,140},{1,5},{5,9},{9,13... | collective-permute-start | bytes 1572872 | tf_op jit(solution)/shard_map/ppermute | solution.py:32
  60.9 10.5 %collective-permute-start.15 = (f32[256,512]{1,0:T(8,128)S(1)}, f32[256,512]{1,0:T(8,128)}, u32[]{:S(2)}, u32[]{:S(2)}) collective-permute-start(f32[256,512]{1,0:T(8,128)S(1)} %broadcast_select_fusion.5), channel_id=1, source_target_pairs={{0,64},{4,68},{8,72},{12,76},{128,192},{132,196},{136,200},{140,20... | collective-permute-start | bytes 1572872 | tf_op jit(solution)/shard_map/ppermute | solution.py:32
  62.4 3.9 %collective-permute-start.9 = (f32[128,384]{1,0:T(8,128)S(1)}, f32[128,384]{1,0:T(8,128)S(1)}, u32[]{:S(2)}, u32[]{:S(2)}) collective-permute-start(f32[128,384]{1,0:T(8,128)S(1)} %broadcast_select_fusion.12), channel_id=1, source_target_pairs={{0,2},{4,6},{8,10},{12,14},{128,130},{132,134},{136,138},{140,142}... | collective-permute-start | bytes 589832 | tf_op jit(solution)/shard_map/ppermute | solution.py:32
  66.3 6.4 %collective-permute-start.12 = (f32[128,384]{1,0:T(8,128)S(1)}, f32[128,384]{1,0:T(8,128)S(1)}, u32[]{:S(2)}, u32[]{:S(2)}) collective-permute-start(f32[128,384]{1,0:T(8,128)S(1)} %broadcast_select_fusion.13), channel_id=1, source_target_pairs={{0,1},{4,5},{8,9},{12,13},{128,129},{132,133},{136,137},{140,141},... | collective-permute-start | bytes 589832 | tf_op jit(solution)/shard_map/ppermute | solution.py:32
  68.6 4.2 %collective-permute-start.13 = (f32[256,512]{1,0:T(8,128)}, f32[256,512]{1,0:T(8,128)}, u32[]{:S(2)}, u32[]{:S(2)}) collective-permute-start(f32[256,512]{1,0:T(8,128)} %collective-permute-done.10), channel_id=1, source_target_pairs={{4,8},{8,12},{132,136},{136,140},{5,9},{9,13},{133,137},{137,141},... | collective-permute-start | bytes 1572872 | tf_op jit(solution)/shard_map/ppermute | solution.py:32
  70.1 24.2 %collective-permute-start.14 = (f32[256,512]{1,0:T(8,128)}, f32[256,512]{1,0:T(8,128)}, u32[]{:S(2)}, u32[]{:S(2)}) collective-permute-start(f32[256,512]{1,0:T(8,128)} %collective-permute-done.11), channel_id=1, source_target_pairs={{4,0},{8,4},{132,128},{136,132},{5,1},{9,5},{133,129},{137,133},{6... | collective-permute-start | bytes 1572872 | tf_op jit(solution)/shard_map/ppermute | solution.py:32
  72.3 24.0 %copy-start.3 = (f32[256,512]{1,0:T(8,128)S(1)}, f32[256,512]{1,0:T(8,128)}, u32[]{:S(2)}) copy-start(f32[256,512]{1,0:T(8,128)} %broadcast_select_fusion.4) | copy-start | bytes 1572868
  94.3 6.7 %collective-permute-start.16 = (f32[2,128,384]{2,1,0:T(8,128)S(1)}, f32[2,128,384]{2,1,0:T(8,128)}, u32[]{:S(2)}, u32[]{:S(2)}) collective-permute-start(f32[2,128,384]{2,1,0:T(8,128)S(1)} %pad_maximum_fusion.3), channel_id=1, source_target_pairs={{0,64},{4,68},{8,72},{12,76},{128,192},{132,196},{136,200},{140,20... | collective-permute-start | bytes 1179656 | tf_op jit(solution)/shard_map/ppermute | solution.py:32
  96.3 5.5 %collective-permute-start.18 = (f32[256,512]{1,0:T(8,128)S(1)}, f32[256,512]{1,0:T(8,128)}, u32[]{:S(2)}, u32[]{:S(2)}) collective-permute-start(f32[256,512]{1,0:T(8,128)S(1)} %copy-done.3), channel_id=1, source_target_pairs={{0,32},{4,36},{8,40},{12,44},{128,160},{132,164},{136,168},{140,17... | collective-permute-start | bytes 1572872 | tf_op jit(solution)/shard_map/ppermute | solution.py:32
  99.7 11.7 %collective-permute-start.17 = (f32[256,512]{1,0:T(8,128)}, f32[256,512]{1,0:T(8,128)}, u32[]{:S(2)}, u32[]{:S(2)}) collective-permute-start(f32[256,512]{1,0:T(8,128)} %broadcast_select_fusion.3), channel_id=1, source_target_pairs={{4,0},{8,12},{132,128},{136,140},{5,1},{9,13},{133,129},{137,141},... | collective-permute-start | bytes 1572872 | tf_op jit(solution)/shard_map/ppermute | solution.py:32
  114.7 1.0 copy-start.5
  114.7 7.8 %copy-start.4 = (f32[256,512]{1,0:T(8,128)S(1)}, f32[256,512]{1,0:T(8,128)}, u32[]{:S(2)}) copy-start(f32[256,512]{1,0:T(8,128)} %broadcast_select_fusion.2) | copy-start | bytes 1572868
  115.7 8.1 %collective-permute-start.19 = (f32[2,128,384]{2,1,0:T(8,128)S(1)}, f32[2,128,384]{2,1,0:T(8,128)S(1)}, u32[]{:S(2)}, u32[]{:S(2)}) collective-permute-start(f32[2,128,384]{2,1,0:T(8,128)S(1)} %copy-done.5), channel_id=1, source_target_pairs={{0,32},{4,36},{8,40},{12,44},{128,160},{132,164},{136,168},{140,17... | collective-permute-start | bytes 1179656 | tf_op jit(solution)/shard_map/ppermute | solution.py:32
  117.0 68.1 %collective-permute-start.22 = (f32[1280,256]{1,0:T(8,128)}, f32[1280,256]{1,0:T(8,128)}, u32[]{:S(2)}, u32[]{:S(2)}) collective-permute-start(f32[1280,256]{1,0:T(8,128)} %shard_map.78), channel_id=1, source_target_pairs={{0,128},{4,132},{8,136},{12,140},{128,0},{132,4},{136,8},{140,12},... | collective-permute-start | bytes 3932168 | tf_op jit(solution)/shard_map/ppermute | solution.py:32
  122.5 10.6 %collective-permute-start.21 = (f32[256,512]{1,0:T(8,128)S(1)}, f32[256,512]{1,0:T(8,128)}, u32[]{:S(2)}, u32[]{:S(2)}) collective-permute-start(f32[256,512]{1,0:T(8,128)S(1)} %copy-done.4), channel_id=1, source_target_pairs={{0,16},{4,20},{8,24},{12,28},{128,144},{132,148},{136,152},{140,15... | collective-permute-start | bytes 1572872 | tf_op jit(solution)/shard_map/ppermute | solution.py:32
  124.6 9.6 %collective-permute-start.20 = (f32[2,128,384]{2,1,0:T(8,128)}, f32[2,128,384]{2,1,0:T(8,128)S(1)}, u32[]{:S(2)}, u32[]{:S(2)}) collective-permute-start(f32[2,128,384]{2,1,0:T(8,128)} %broadcast_select_fusion.7), channel_id=1, source_target_pairs={{0,16},{4,20},{8,24},{12,28},{128,144},{132,148},{136,152},{140,15... | collective-permute-start | bytes 1179656 | tf_op jit(solution)/shard_map/ppermute | solution.py:32
  130.3 60.4 %collective-permute-start.23 = (f32[256,256]{1,0:T(8,128)}, f32[256,256]{1,0:T(8,128)}, u32[]{:S(2)}, u32[]{:S(2)}) collective-permute-start(f32[256,256]{1,0:T(8,128)} %shard_map.77), channel_id=1, source_target_pairs={{0,128},{4,132},{8,136},{12,140},{128,0},{132,4},{136,8},{140,12},... | collective-permute-start | bytes 786440 | tf_op jit(solution)/shard_map/ppermute | solution.py:32
  165.1 0.8 copy-start.1
Sparse Core Ops, SparseCore 0:
  9.8 37.2 all-gather.2
  114.8 69.3 all-gather.4

commit v6 on v5

--- a/solution.py
+++ b/solution.py
@@ -318,17 +318,12 @@
     return jnp.concatenate([top, bottom], axis=1)
 
 
-def window_owned(panel):
+def window_owned(panel, half):
     place = {}
     for col in range(16):
         block = 2 + col
-        place[(block // 16) * 16 + block % 16] = col
+        place[(block // 16) * 16 + block % 16] = half * 128 + col
     return lax.ppermute(panel, ALL, sorted(place.items()))
-
-
-def window_halves(held, z):
-    got = send(held, lambda x, c, y, z: (x, c, y, z + 4) if x == 0 and c == 0 and z < 4 else None)
-    return jnp.where(z >= 4, got, held)
 
 
 def window_x(held, x, stride):
@@ -367,23 +362,34 @@
     row = lax.axis_index("row")
     col = lax.axis_index("col")
     x, core, y, z = row // 2, row % 2, col % NY, sub * 4 + col // NY
-    own_slots = child_map[0]
-    own_count, own_place, order = crossing(own_slots, sub, blocks)
-    outgoing = [take_blocks(order[low:high], child[0], size) for low, high in ((0, FIRST), (FIRST, MAIN))]
-    other_slots = swap(child_map)
-
     tie = lax.optimization_barrier
     zl = z % 4
     right = lambda value, at: send(value, lambda x, c, y, z: (x, c, y, z + 1) if z % 4 in at else None)
     left = lambda value, at: send(value, lambda x, c, y, z: (x, c, y, z - 1) if z % 4 in at else None)
     near = gather_y(panel)
     held = pivot_split(panel, core, y)
-    window = window_owned(panel)
+    from_left1, from_right1 = right(panel, (0, 1, 2)), left(panel, (1, 2, 3))
+    held, owned = tie((held, panel))
+    windows = [window_owned(owned, half) for half in range(2)]
     held = pivot_spread(held, (0,), x, y, z)
-    held, window, other_slots = tie((held, window, other_slots))
+    held, from_left1, from_right1, child_map = tie((held, from_left1, from_right1, child_map))
+    own_slots = child_map[0]
+    own_count, own_place, order = crossing(own_slots, sub, blocks)
+    outgoing = [take_blocks(order[low:high], child[0], size) for low, high in ((0, FIRST), (FIRST, MAIN))]
+    other_slots = swap(child_map)
+    from_left2, from_right2 = right(from_left1, (1, 2)), left(from_right1, (1, 2))
+    held = pivot_spread(held, (1,), x, y, z)
+    held, from_left2, from_right2, other_slots = tie((held, from_left2, from_right2, other_slots))
     other_slots = other_slots[0]
-    window = window_halves(window, z)
-    held = pivot_spread(held, (1,), x, y, z)
+    last = send(
+        jnp.where(zl == 2, from_left2, from_right2),
+        lambda x, c, y, z: {1: (x, c, y, z - 1), 2: (x, c, y, z + 1)}.get(z % 4),
+    )
+    held = pivot_spread(held, (2,), x, y, z)
+    held, last, windows = tie((held, last, windows))
+    window = jnp.where(z >= 4, windows[1], windows[0])
+    window = window_x(window, x, 2)
+    held = pivot_spread(held, (3,), x, y, z)
 
     other_count, other_place, _ = crossing(other_slots, 1 - sub, blocks)
     need = jnp.maximum(own_count, other_count)
@@ -417,28 +423,18 @@
         ]
     ).astype(jnp.int32)
 
-    held, table, need, outgoing = tie((held, table, need, outgoing))
-    held = pivot_spread(held, (2,), x, y, z)
-    held, window, bulk = tie((held, window, panel))
-    from_left1, from_right1 = right(bulk, (0, 1, 2)), left(bulk, (1, 2, 3))
-    held = pivot_spread(held, (3,), x, y, z)
-    window = window_x(window, x, 2)
-    held, from_left1, from_right1 = tie((held, from_left1, from_right1))
-    from_left2, from_right2 = right(from_left1, (1, 2)), left(from_right1, (1, 2))
-    held = join_y(held, y)
-    held, from_left2, from_right2, near, window = tie((held, from_left2, from_right2, near, window))
-    last = send(
-        jnp.where(zl == 2, from_left2, from_right2),
-        lambda x, c, y, z: {1: (x, c, y, z - 1), 2: (x, c, y, z + 1)}.get(z % 4),
-    )
-    held = pivot_spread(held, (4,), x, y, z)
-    window = window_x(window, x, 1)
-    held, last, window, outgoing = tie((held, last, window, outgoing))
     slot1 = jnp.where(zl == 3, from_left1, from_right1)
     slot2 = jnp.where(zl == 0, from_right2, jnp.where(zl == 3, from_left2, from_left1))
     slot3 = jnp.where(zl == 1, from_right2, jnp.where(zl == 2, from_left2, last))
-    far = gather_y(jnp.concatenate([slot1, slot2, slot3], axis=0))
+    slots = jnp.concatenate([slot1, slot2, slot3], axis=0)
+    held, table, need, outgoing = tie((held, table, need, outgoing))
     first = swap(outgoing[0])
+    held = join_y(held, y)
+    held, near, window, slots = tie((held, near, window, slots))
+    far = gather_y(slots)
+    window = window_x(window, x, 1)
+    held = pivot_spread(held, (4,), x, y, z)
+    held, first, window, outgoing = tie((held, first, window, outgoing))
     main = swap(outgoing[1])
     window = window_core(window, core)
     held = pivot_spread(held, (5,), x, y, z)

time: 215 us -> 216 us (level); the launches traced: 213 us -> 220 us
  starting transfers between devices: 59.1 us -> 90.1 us
  waiting for transfers between devices: 59.6 us -> 28.7 us
  Pallas kernels: 54 us -> 57.7 us
    ppermute x21, starting transfers between devices: 47.9 us -> 79.1 us  [send(): return lax.ppermute(value, ALL, pairs_of(move))]
    ppermute x21, waiting for transfers between devices: 58.8 us -> 28 us  [send(): return lax.ppermute(value, ALL, pairs_of(move))]
    pallas_call x2 -> x3, Pallas kernels: 3.66 us -> 5.04 us  [take_blocks(): pl.pallas_call(take_kernel, grid_spec=pltpu.PrefetchScalarGridSpec(num_sc...]
    ppermute x1 -> x2, starting transfers between devices: 11.1 us -> 10.9 us  [window_owned(): return lax.ppermute(panel, ALL, sorted(place.items()))]
  transfers between devices with their start and end apart: 24 -> 25, of which waited for: 8 -> 9; matrix products, arithmetic and copies ran while one was open for 9% -> 12% of each run, Pallas kernels for 18% -> 19%
where the time goes in v6:
time: 216 us; the launch traced here: 220 us
  starting transfers between devices  90.1 us (42%)
  Pallas kernels  57.7 us (27%)
  waiting for transfers between devices  28.7 us (13%)
  other arithmetic  19.4 us (9%)
  between operations  15.9 us (7%)
  local copies, waits for them, and re-layouts  7.95 us (4%)
    ppermute x21, starting transfers between devices, send(): return lax.ppermute(value, ALL, pairs_of(move))  79.1 us
    ppermute x21, waiting for transfers between devices, send(): return lax.ppermute(value, ALL, pairs_of(move))  28 us
    pallas_call x1, Pallas kernels, pivot_inverse(): pl.pallas_call(pivot_kernel, out_shape=jax.ShapeDtypeStruct((width, width...  26.9 us
    pallas_call x1, Pallas kernels, update_far(): pl.pallas_call(far_kernel, grid_spec=pltpu.PrefetchScalarGridSpec(num_sca...  16.7 us
    ppermute x2, starting transfers between devices, window_owned(): return lax.ppermute(panel, ALL, sorted(place.items()))  10.9 us
    pallas_call x1, Pallas kernels, update_near(): pl.pallas_call(near_kernel, grid_spec=pltpu.PrefetchScalarGridSpec(num_sc...  6.2 us
    pallas_call x3, Pallas kernels, take_blocks(): pl.pallas_call(take_kernel, grid_spec=pltpu.PrefetchScalarGridSpec(num_sc...  5.04 us
  transfers between devices with their start and end apart: 25, of which 9 were waited for; matrix products, arithmetic and copies ran while one was open for 12% of the time, Pallas kernels for 19%

profile of v6, /device:TPU:1, one launch (start us, length us, event | category | flops | bytes accessed | tf_op | source)
XLA Modules:
  0.0 219.7 jit_solution(15982981453355312429)
XLA Ops:
  8.0 5.3 %collective-permute-start.4 = (f32[256,512]{1,0:T(8,128)}, f32[256,512]{1,0:T(8,128)}, u32[]{:S(2)}, u32[]{:S(2)}) collective-permute-start(f32[256,512]{1,0:T(8,128)} %panel_ref.1), channel_id=1, source_target_pairs={{0,4},{4,8},{8,12},{128,132},{132,136},{136,140},{1,5},{5,9},{9,13... | collective-permute-start | bytes 1572872 | tf_op jit(solution)/shard_map/ppermute | solution.py:32
  16.5 1.4 collective-permute-start.2
  20.3 7.3 %collective-permute-start.3 = (f32[128,384]{1,0:T(8,128)S(1)}, f32[128,384]{1,0:T(8,128)S(1)}, u32[]{:S(2)}, u32[]{:S(2)}) collective-permute-start(f32[128,384]{1,0:T(8,128)S(1)} %slice_select_fusion), channel_id=1, source_target_pairs={{0,128},{1,129},{16,144},{17,145}} | collective-permute-start | bytes 589832 | tf_op jit(solution)/shard_map/ppermute | solution.py:32
  28.1 5.2 %collective-permute-start.13 = (f32[256,512]{1,0:T(8,128)S(1)}, f32[256,512]{1,0:T(8,128)}, u32[]{:S(2)}, u32[]{:S(2)}) collective-permute-start(f32[256,512]{1,0:T(8,128)S(1)} %copy-done), channel_id=1, source_target_pairs={{2,128},{3,129},{4,130},{5,131},{6,132},{7,133},{8,134},{9,135},{1... | collective-permute-start | bytes 1572872 | tf_op jit(solution)/shard_map/ppermute | solution.py:326
  33.3 5.7 %collective-permute-start.12 = (f32[256,512]{1,0:T(8,128)S(1)}, f32[256,512]{1,0:T(8,128)}, u32[]{:S(2)}, u32[]{:S(2)}) collective-permute-start(f32[256,512]{1,0:T(8,128)S(1)} %copy-done), channel_id=1, source_target_pairs={{2,0},{3,1},{4,2},{5,3},{6,4},{7,5},{8,6},{9,7},{10,8},{11,9},{12,... | collective-permute-start | bytes 1572872 | tf_op jit(solution)/shard_map/ppermute | solution.py:326
  45.2 2.9 %shard_map.78 = f32[1280,256]{1,0:T(8,128)} custom-call(s32[5]{0:T(128)} %slice.57.order, f32[2048,256]{1,0:T(8,128)S(1)} %bitcast.49), custom_call_target="tpu_custom_call" | custom-call | tf_op jit(solution)/shard_map/pallas_call | solution.py:149
  48.7 4.2 %collective-permute-start.9 = (s32[1,8]{1,0:T(1,128)S(1)}, s32[1,8]{1,0:T(1,128)S(1)}, u32[]{:S(2)}, u32[]{:S(2)}) collective-permute-start(s32[1,8]{1,0:T(1,128)S(1)} %copy-done.6), channel_id=1, source_target_pairs={{0,128},{4,132},{8,136},{12,140},{128,0},{132,4},{136,8},{140,12},... | collective-permute-start | bytes 104 | tf_op jit(solution)/shard_map/ppermute | solution.py:32
  52.9 2.1 collective-permute-done.9
  55.0 1.4 collective-permute-done.8
  60.1 2.0 collective-permute-start.10
  62.0 1.9 broadcast_select_fusion.5
  67.7 2.6 %stack.11.table = s32[9,16]{1,0:T(8,128)} concatenate(s32[1,16]{1,0:T(1,128)} %fusion.13, s32[1,16]{1,0:T(1,128)} %compare_select_fusion.16, s32[1,16]{1,0:T(1,128)} %convert_bitcast_fusion.1, s32[1,16]{1,0:T(1,128)} %compare_select_fusion.15, s32[1,16]{1,0:T(1,128)S(1)} %compare_select_fusion.14, s32[1,16]{1,0:T(1,128)} %compare_select_fusion.13, ...), dimensions={0} | concatenate | bytes 1152 | tf_op jit(solution)/shard_map/stack | solution.py:414
  70.3 4.6 %collective-permute-done.11 = f32[256,512]{1,0:T(8,128)} collective-permute-done((f32[256,512]{1,0:T(8,128)}, f32[256,512]{1,0:T(8,128)}, u32[]{:S(2)}, u32[]{:S(2)}) %collective-permute-start.11) | collective-permute-done | bytes 524320 | tf_op jit(solution)/shard_map/ppermute | solution.py:32
  77.4 1.5 collective-permute-start.16
  78.9 3.3 %collective-permute-start.15 = (f32[128,384]{1,0:T(8,128)S(1)}, f32[128,384]{1,0:T(8,128)S(1)}, u32[]{:S(2)}, u32[]{:S(2)}) collective-permute-start(f32[128,384]{1,0:T(8,128)S(1)} %broadcast_select_fusion.13), channel_id=1, source_target_pairs={{0,1},{4,5},{8,9},{12,13},{128,129},{132,133},{136,137},{140,141},... | collective-permute-start | bytes 589832 | tf_op jit(solution)/shard_map/ppermute | solution.py:32
  82.3 1.8 select_select_fusion.1
  84.1 1.4 pad_maximum_fusion.1
  87.7 2.2 collective-permute-start.17
  89.8 1.5 collective-permute-start.19
  91.3 6.9 %collective-permute-start.18 = (f32[256,256]{1,0:T(8,128)}, f32[256,256]{1,0:T(8,128)}, u32[]{:S(2)}, u32[]{:S(2)}) collective-permute-start(f32[256,256]{1,0:T(8,128)} %shard_map.77), channel_id=1, source_target_pairs={{0,128},{4,132},{8,136},{12,140},{128,0},{132,4},{136,8},{140,12},... | collective-permute-start | bytes 786440 | tf_op jit(solution)/shard_map/ppermute | solution.py:32
  99.2 5.9 %collective-permute-done.18.first_ref = f32[256,256]{1,0:T(8,128)} collective-permute-done((f32[256,256]{1,0:T(8,128)}, f32[256,256]{1,0:T(8,128)}, u32[]{:S(2)}, u32[]{:S(2)}) %collective-permute-start.18) | collective-permute-done | bytes 262176 | tf_op jit(solution)/shard_map/ppermute | solution.py:32
  106.4 2.6 %collective-permute-start.23 = (f32[1280,256]{1,0:T(8,128)}, f32[1280,256]{1,0:T(8,128)}, u32[]{:S(2)}, u32[]{:S(2)}) collective-permute-start(f32[1280,256]{1,0:T(8,128)} %shard_map.78), channel_id=1, source_target_pairs={{0,128},{4,132},{8,136},{12,140},{128,0},{132,4},{136,8},{140,12},... | collective-permute-start | bytes 3932168 | tf_op jit(solution)/shard_map/ppermute | solution.py:32
  110.3 4.4 %collective-permute-done.20 = f32[2,128,384]{2,1,0:T(8,128)S(1)} collective-permute-done((f32[2,128,384]{2,1,0:T(8,128)S(1)}, f32[2,128,384]{2,1,0:T(8,128)S(1)}, u32[]{:S(2)}, u32[]{:S(2)}) %collective-permute-start.20) | collective-permute-done | bytes 393248 | tf_op jit(solution)/shard_map/ppermute | solution.py:32
  114.8 29.3 %collective-permute-start.21 = (f32[2,128,384]{2,1,0:T(8,128)S(1)}, f32[2,128,384]{2,1,0:T(8,128)}, u32[]{:S(2)}, u32[]{:S(2)}) collective-permute-start(f32[2,128,384]{2,1,0:T(8,128)S(1)} %broadcast_select_fusion.7), channel_id=1, source_target_pairs={{0,16},{4,20},{8,24},{12,28},{128,144},{132,148},{136,152},{140,15... | collective-permute-start | bytes 1179656 | tf_op jit(solution)/shard_map/ppermute | solution.py:32
  147.0 26.9 %shard_map.79.inverse_ref = f32[512,512]{1,0:T(8,128)S(1)} custom-call(f32[2,256,384]{2,1,0:T(8,128)S(1)} %pad_maximum_fusion.2.parts_ref), custom_call_target="tpu_custom_call" | custom-call | tf_op jit(solution)/shard_map/pallas_call | solution.py:116
  173.9 2.8 %shard_map.80 = (f32[256,512]{1,0:T(8,128)}, f32[256,512]{1,0:T(8,128)S(1)}) custom-call(f32[512,512]{1,0:T(8,128)S(1)} %shard_map.79.inverse_ref, f32[256,512]{1,0:T(8,128)S(1)} %copy-done, f32[256,512]{1,0:T(8,128)S(1)} %broadcast_select_fusion.window_ref), custom_call_target="tpu_custom_call" | custom-call | tf_op jit(solution)/shard_map/pallas_call | solution.py:136
  177.5 6.2 %shard_map.81.done_ref = f32[4096,256]{1,0:T(8,128)} custom-call(s32[9,16]{1,0:T(8,128)} %stack.11.table, f32[1024,512]{1,0:T(8,128)} %all-gather.3.cloned.1.call-done.rows_ref, f32[256,512]{1,0:T(8,128)} %copy-done.1, f32[4096,256]{1,0:T(8,128)} %trailing_ref.3, f32[2048,256]{1,0:T(8,128)S(1)} %bitcast.50), custom_call_target="tpu_custom_call" | custom-call | tf_op jit(solution)/shard_map/pallas_call | solution.py:182
  183.8 12.4 %conditional.2 = (f32[512,256]{1,0:T(8,128)S(1)}) conditional(s32[]{:T(128)} %convert_element_type.69, () %tuple.39, (s32[8]{0:T(128)S(1)}, f32[1,2048,256]{2,1,0:T(8,128)S(1)}, s32[]{:T(128)}) %tuple.64), branch_computations={%region_18.19_spmd, %region_19.22_spmd} | conditional | flops 131074 | bytes 3145870 | solution.py:446
  184.4 1.4 branch_1_fun.3
  185.8 2.0 collective-permute-start.1
  188.5 6.6 %collective-permute-done.1 = f32[256,256]{1,0:T(8,128)S(1)} collective-permute-done((f32[256,256]{1,0:T(8,128)}, f32[256,256]{1,0:T(8,128)S(1)}, u32[]{:S(2)}, u32[]{:S(2)}) %collective-permute-start.1) | collective-permute-done | bytes 262176 | tf_op jit(solution)/shard_map/cond/branch_1_fun/ppermute | solution.py:32
  196.2 16.7 %shard_map.82 = f32[4096,256]{1,0:T(8,128)} custom-call(s32[9,16]{1,0:T(8,128)} %stack.11.table, f32[4096,256]{1,0:T(8,128)} %shard_map.81.done_ref, f32[3072,512]{1,0:T(8,128)} %all-gather.5.cloned.1.call-done.rows_ref, f32[256,512]{1,0:T(8,128)} %copy-done.1, f32[4096,256]{1,0:T(8,128)} %trailing_ref.3, ...), custom_call_target="tpu_custom_call", output_to_operand_aliasing={{}: (1, {})} | custom-call | tf_op jit(solution)/shard_map/pallas_call | solution.py:230
  (111 shorter events, 34.5 us)
Async XLA Ops:
  7.2 9.3 %copy-start = (f32[256,512]{1,0:T(8,128)S(1)}, f32[256,512]{1,0:T(8,128)}, u32[]{:S(2)}) copy-start(f32[256,512]{1,0:T(8,128)} %panel_ref.1) | copy-start | bytes 1572868
  7.2 11.6 %copy-start.7 = (s32[16,1]{0,1:T(1,128)S(1)}, s32[16,1]{0,1:T(1,128)}, u32[]{:S(2)}) copy-start(s32[16,1]{0,1:T(1,128)} %param.14) | copy-start | bytes 196
  7.2 80.5 %all-gather.3.cloned.1.call-start = ((), (), s32[]{:S(2)}) async-start(), calls=%async_computation | async-start | bytes 2621440 | tf_op jit(solution)/shard_map/all_gather | solution.py:343
  7.9 188.2 %all-gather.5.cloned.1.call-start = ((), (), s32[]{:S(2)}) async-start(), calls=%async_computation.1 | async-start | bytes 7864320 | tf_op jit(solution)/shard_map/all_gather | solution.py:343
  8.0 31.1 %collective-permute-start.4 = (f32[256,512]{1,0:T(8,128)}, f32[256,512]{1,0:T(8,128)}, u32[]{:S(2)}, u32[]{:S(2)}) collective-permute-start(f32[256,512]{1,0:T(8,128)} %panel_ref.1), channel_id=1, source_target_pairs={{0,4},{4,8},{8,12},{128,132},{132,136},{136,140},{1,5},{5,9},{9,13... | collective-permute-start | bytes 1572872 | tf_op jit(solution)/shard_map/ppermute | solution.py:32
  13.2 25.9 %collective-permute-start.5 = (f32[256,512]{1,0:T(8,128)}, f32[256,512]{1,0:T(8,128)}, u32[]{:S(2)}, u32[]{:S(2)}) collective-permute-start(f32[256,512]{1,0:T(8,128)} %panel_ref.1), channel_id=1, source_target_pairs={{4,0},{8,4},{12,8},{132,128},{136,132},{140,136},{5,1},{9,5},{13,9... | collective-permute-start | bytes 1572872 | tf_op jit(solution)/shard_map/ppermute | solution.py:32
  16.4 22.7 %copy-start.6 = (s32[1,8]{1,0:T(1,128)S(1)}, s32[1,8]{1,0:T(1,128)}, u32[]{:S(2)}) copy-start(s32[1,8]{1,0:T(1,128)} %param.13) | copy-start | bytes 100
  16.4 28.1 %copy-start.2 = (f32[1,2048,256]{2,1,0:T(8,128)S(1)}, f32[1,2048,256]{2,1,0:T(8,128)}, u32[]{:S(2)}) copy-start(f32[1,2048,256]{2,1,0:T(8,128)} %param.12) | copy-start | bytes 6291460
  16.5 3.7 %collective-permute-start.2 = (f32[128,384]{1,0:T(8,128)S(1)}, f32[128,384]{1,0:T(8,128)S(1)}, u32[]{:S(2)}, u32[]{:S(2)}) collective-permute-start(f32[128,384]{1,0:T(8,128)S(1)} %slice.59), channel_id=1, source_target_pairs={{0,16},{1,17}} | collective-permute-start | bytes 589832 | tf_op jit(solution)/shard_map/ppermute | solution.py:32
  20.3 18.8 %collective-permute-start.3 = (f32[128,384]{1,0:T(8,128)S(1)}, f32[128,384]{1,0:T(8,128)S(1)}, u32[]{:S(2)}, u32[]{:S(2)}) collective-permute-start(f32[128,384]{1,0:T(8,128)S(1)} %slice_select_fusion), channel_id=1, source_target_pairs={{0,128},{1,129},{16,144},{17,145}} | collective-permute-start | bytes 589832 | tf_op jit(solution)/shard_map/ppermute | solution.py:32
  28.1 42.2 %collective-permute-start.13 = (f32[256,512]{1,0:T(8,128)S(1)}, f32[256,512]{1,0:T(8,128)}, u32[]{:S(2)}, u32[]{:S(2)}) collective-permute-start(f32[256,512]{1,0:T(8,128)S(1)} %copy-done), channel_id=1, source_target_pairs={{2,128},{3,129},{4,130},{5,131},{6,132},{7,133},{8,134},{9,135},{1... | collective-permute-start | bytes 1572872 | tf_op jit(solution)/shard_map/ppermute | solution.py:326
  33.3 37.0 %collective-permute-start.12 = (f32[256,512]{1,0:T(8,128)S(1)}, f32[256,512]{1,0:T(8,128)}, u32[]{:S(2)}, u32[]{:S(2)}) collective-permute-start(f32[256,512]{1,0:T(8,128)S(1)} %copy-done), channel_id=1, source_target_pairs={{2,0},{3,1},{4,2},{5,3},{6,4},{7,5},{8,6},{9,7},{10,8},{11,9},{12,... | collective-permute-start | bytes 1572872 | tf_op jit(solution)/shard_map/ppermute | solution.py:326
  39.9 15.1 %collective-permute-start.7 = (f32[256,512]{1,0:T(8,128)}, f32[256,512]{1,0:T(8,128)S(1)}, u32[]{:S(2)}, u32[]{:S(2)}) collective-permute-start(f32[256,512]{1,0:T(8,128)} %collective-permute-done.4), channel_id=1, source_target_pairs={{4,8},{8,12},{132,136},{136,140},{5,9},{9,13},{133,137},{137,141},... | collective-permute-start | bytes 1572872 | tf_op jit(solution)/shard_map/ppermute | solution.py:32
  40.6 15.8 %collective-permute-start.8 = (f32[256,512]{1,0:T(8,128)}, f32[256,512]{1,0:T(8,128)}, u32[]{:S(2)}, u32[]{:S(2)}) collective-permute-start(f32[256,512]{1,0:T(8,128)} %collective-permute-done.5), channel_id=1, source_target_pairs={{4,0},{8,4},{132,128},{136,132},{5,1},{9,5},{133,129},{137,133},{6... | collective-permute-start | bytes 1572872 | tf_op jit(solution)/shard_map/ppermute | solution.py:32
  43.2 5.5 %collective-permute-start.6 = (f32[128,384]{1,0:T(8,128)S(1)}, f32[128,384]{1,0:T(8,128)S(1)}, u32[]{:S(2)}, u32[]{:S(2)}) collective-permute-start(f32[128,384]{1,0:T(8,128)S(1)} %broadcast_select_fusion.10), channel_id=1, source_target_pairs={{0,8},{128,136},{1,9},{129,137},{16,24},{144,152},{17,25},{145,153}} | collective-permute-start | bytes 589832 | tf_op jit(solution)/shard_map/ppermute | solution.py:32
  48.7 6.3 %collective-permute-start.9 = (s32[1,8]{1,0:T(1,128)S(1)}, s32[1,8]{1,0:T(1,128)S(1)}, u32[]{:S(2)}, u32[]{:S(2)}) collective-permute-start(s32[1,8]{1,0:T(1,128)S(1)} %copy-done.6), channel_id=1, source_target_pairs={{0,128},{4,132},{8,136},{12,140},{128,0},{132,4},{136,8},{140,12},... | collective-permute-start | bytes 104 | tf_op jit(solution)/shard_map/ppermute | solution.py:32
  55.0 19.9 %copy-start.4 = (f32[256,512]{1,0:T(8,128)}, f32[256,512]{1,0:T(8,128)S(1)}, u32[]{:S(2)}) copy-start(f32[256,512]{1,0:T(8,128)S(1)} %collective-permute-done.7) | copy-start | bytes 1572868
  60.1 10.2 %collective-permute-start.10 = (f32[128,384]{1,0:T(8,128)S(1)}, f32[128,384]{1,0:T(8,128)S(1)}, u32[]{:S(2)}, u32[]{:S(2)}) collective-permute-start(f32[128,384]{1,0:T(8,128)S(1)} %broadcast_select_fusion.11), channel_id=1, source_target_pairs={{0,4},{8,12},{128,132},{136,140},{1,5},{9,13},{129,133},{137,141},... | collective-permute-start | bytes 589832 | tf_op jit(solution)/shard_map/ppermute | solution.py:32
  64.0 11.0 %collective-permute-start.11 = (f32[256,512]{1,0:T(8,128)}, f32[256,512]{1,0:T(8,128)}, u32[]{:S(2)}, u32[]{:S(2)}) collective-permute-start(f32[256,512]{1,0:T(8,128)} %broadcast_select_fusion.5), channel_id=1, source_target_pairs={{4,0},{8,12},{132,128},{136,140},{5,1},{9,13},{133,129},{137,141},... | collective-permute-start | bytes 1572872 | tf_op jit(solution)/shard_map/ppermute | solution.py:32
  74.9 4.0 %collective-permute-start.14 = (f32[128,384]{1,0:T(8,128)S(1)}, f32[128,384]{1,0:T(8,128)S(1)}, u32[]{:S(2)}, u32[]{:S(2)}) collective-permute-start(f32[128,384]{1,0:T(8,128)S(1)} %broadcast_select_fusion.12), channel_id=1, source_target_pairs={{0,2},{4,6},{8,10},{12,14},{128,130},{132,134},{136,138},{140,142}... | collective-permute-start | bytes 589832 | tf_op jit(solution)/shard_map/ppermute | solution.py:32
  76.2 6.0 %copy-start.5 = (f32[256,512]{1,0:T(8,128)S(1)}, f32[256,512]{1,0:T(8,128)}, u32[]{:S(2)}) copy-start(f32[256,512]{1,0:T(8,128)} %copy-done.4) | copy-start | bytes 1572868
  77.4 9.3 %collective-permute-start.16 = (f32[256,512]{1,0:T(8,128)S(1)}, f32[256,512]{1,0:T(8,128)}, u32[]{:S(2)}, u32[]{:S(2)}) collective-permute-start(f32[256,512]{1,0:T(8,128)S(1)} %broadcast_select_fusion.3), channel_id=1, source_target_pairs={{0,64},{4,68},{8,72},{12,76},{128,192},{132,196},{136,200},{140,20... | collective-permute-start | bytes 1572872 | tf_op jit(solution)/shard_map/ppermute | solution.py:32
  78.9 7.7 %collective-permute-start.15 = (f32[128,384]{1,0:T(8,128)S(1)}, f32[128,384]{1,0:T(8,128)S(1)}, u32[]{:S(2)}, u32[]{:S(2)}) collective-permute-start(f32[128,384]{1,0:T(8,128)S(1)} %broadcast_select_fusion.13), channel_id=1, source_target_pairs={{0,1},{4,5},{8,9},{12,13},{128,129},{132,133},{136,137},{140,141},... | collective-permute-start | bytes 589832 | tf_op jit(solution)/shard_map/ppermute | solution.py:32
  87.6 2.2 %copy-start.3 = (f32[256,512]{1,0:T(8,128)S(1)}, f32[256,512]{1,0:T(8,128)}, u32[]{:S(2)}) copy-start(f32[256,512]{1,0:T(8,128)} %broadcast_select_fusion.4) | copy-start | bytes 1572868
  87.7 10.5 %collective-permute-start.17 = (f32[2,128,384]{2,1,0:T(8,128)S(1)}, f32[2,128,384]{2,1,0:T(8,128)}, u32[]{:S(2)}, u32[]{:S(2)}) collective-permute-start(f32[2,128,384]{2,1,0:T(8,128)S(1)} %pad_maximum_fusion.3), channel_id=1, source_target_pairs={{0,64},{4,68},{8,72},{12,76},{128,192},{132,196},{136,200},{140,20... | collective-permute-start | bytes 1179656 | tf_op jit(solution)/shard_map/ppermute | solution.py:32
  89.8 8.4 %collective-permute-start.19 = (f32[256,512]{1,0:T(8,128)S(1)}, f32[256,512]{1,0:T(8,128)}, u32[]{:S(2)}, u32[]{:S(2)}) collective-permute-start(f32[256,512]{1,0:T(8,128)S(1)} %copy-done.3), channel_id=1, source_target_pairs={{0,32},{4,36},{8,40},{12,44},{128,160},{132,164},{136,168},{140,17... | collective-permute-start | bytes 1572872 | tf_op jit(solution)/shard_map/ppermute | solution.py:32
  91.3 13.8 %collective-permute-start.18 = (f32[256,256]{1,0:T(8,128)}, f32[256,256]{1,0:T(8,128)}, u32[]{:S(2)}, u32[]{:S(2)}) collective-permute-start(f32[256,256]{1,0:T(8,128)} %shard_map.77), channel_id=1, source_target_pairs={{0,128},{4,132},{8,136},{12,140},{128,0},{132,4},{136,8},{140,12},... | collective-permute-start | bytes 786440 | tf_op jit(solution)/shard_map/ppermute | solution.py:32
  105.1 9.6 %collective-permute-start.20 = (f32[2,128,384]{2,1,0:T(8,128)S(1)}, f32[2,128,384]{2,1,0:T(8,128)S(1)}, u32[]{:S(2)}, u32[]{:S(2)}) collective-permute-start(f32[2,128,384]{2,1,0:T(8,128)S(1)} %broadcast_select_fusion.6), channel_id=1, source_target_pairs={{0,32},{4,36},{8,40},{12,44},{128,160},{132,164},{136,168},{140,17... | collective-permute-start | bytes 1179656 | tf_op jit(solution)/shard_map/ppermute | solution.py:32
  106.4 77.4 %collective-permute-start.23 = (f32[1280,256]{1,0:T(8,128)}, f32[1280,256]{1,0:T(8,128)}, u32[]{:S(2)}, u32[]{:S(2)}) collective-permute-start(f32[1280,256]{1,0:T(8,128)} %shard_map.78), channel_id=1, source_target_pairs={{0,128},{4,132},{8,136},{12,140},{128,0},{132,4},{136,8},{140,12},... | collective-permute-start | bytes 3932168 | tf_op jit(solution)/shard_map/ppermute | solution.py:32
  109.0 36.3 %collective-permute-start.22 = (f32[256,512]{1,0:T(8,128)}, f32[256,512]{1,0:T(8,128)S(1)}, u32[]{:S(2)}, u32[]{:S(2)}) collective-permute-start(f32[256,512]{1,0:T(8,128)} %broadcast_select_fusion.1), channel_id=1, source_target_pairs={{0,16},{4,20},{8,24},{12,28},{128,144},{132,148},{136,152},{140,15... | collective-permute-start | bytes 1572872 | tf_op jit(solution)/shard_map/ppermute | solution.py:32
  114.8 31.1 %collective-permute-start.21 = (f32[2,128,384]{2,1,0:T(8,128)S(1)}, f32[2,128,384]{2,1,0:T(8,128)}, u32[]{:S(2)}, u32[]{:S(2)}) collective-permute-start(f32[2,128,384]{2,1,0:T(8,128)S(1)} %broadcast_select_fusion.7), channel_id=1, source_target_pairs={{0,16},{4,20},{8,24},{12,28},{128,144},{132,148},{136,152},{140,15... | collective-permute-start | bytes 1179656 | tf_op jit(solution)/shard_map/ppermute | solution.py:32
  185.8 9.3 %collective-permute-start.1 = (f32[256,256]{1,0:T(8,128)}, f32[256,256]{1,0:T(8,128)S(1)}, u32[]{:S(2)}, u32[]{:S(2)}) collective-permute-start(f32[256,256]{1,0:T(8,128)} %branch_1_fun.3), channel_id=1, source_target_pairs={{0,128},{4,132},{8,136},{12,140},{128,0},{132,4},{136,8},{140,12},... | collective-permute-start | bytes 786440 | tf_op jit(solution)/shard_map/cond/branch_1_fun/ppermute | solution.py:32
  (1 other events, 0.8 us)
Sparse Core Ops, SparseCore 0:
  9.8 41.8 all-gather.2
  87.8 73.4 all-gather.4

commit v7 on v6

--- a/solution.py
+++ b/solution.py
@@ -9,7 +9,7 @@
 ALL = ("sub", "row", "col")
 SB = 128
 NX, NY, NZ = 4, 4, 8
-FIRST, MAIN = 1, 6
+MAIN = 6
 
 
 def linear(x, core, y, z):
@@ -125,19 +125,35 @@
     )(parts)
 
 
-def solve_kernel(inverse_ref, panel_ref, window_ref, factor_ref, weight_ref):
+def thirds(value):
+    first = value.astype(jnp.bfloat16)
+    left = value - first.astype(jnp.float32)
+    second = left.astype(jnp.bfloat16)
+    return first, second, (left - second.astype(jnp.float32)).astype(jnp.bfloat16)
+
+
+def product(rows, weights):
+    a, b = thirds(rows), weights
+    dot = lambda i, j: jnp.dot(a[i], b[j], preferred_element_type=jnp.float32)
+    return dot(0, 0) + ((dot(0, 1) + dot(1, 0)) + ((dot(0, 2) + dot(1, 1)) + dot(2, 0)))
+
+
+def solve_kernel(inverse_ref, panel_ref, window_ref, factor_ref, *weight_refs):
     inverse = inverse_ref[...]
     factor_ref[...] = contract(panel_ref[...], inverse, 1, 1)
-    weight_ref[...] = contract(contract(window_ref[...], inverse, 1, 1), inverse, 1, 0)
+    weight = contract(contract(window_ref[...], inverse, 1, 1), inverse, 1, 0)
+    for weight_ref, value in zip(weight_refs, thirds(weight.T)):
+        weight_ref[...] = value
 
 
 def solve(inverse, panel, window):
-    shape = jax.ShapeDtypeStruct(panel.shape, jnp.float32)
-    return pl.pallas_call(
+    weight = jax.ShapeDtypeStruct((window.shape[1], window.shape[0]), jnp.bfloat16)
+    factor, *weights = pl.pallas_call(
         solve_kernel,
-        out_shape=(shape, jax.ShapeDtypeStruct(window.shape, jnp.float32)),
+        out_shape=(jax.ShapeDtypeStruct(panel.shape, jnp.float32), weight, weight, weight),
         compiler_params=pltpu.CompilerParams(vmem_limit_bytes=32 << 20),
     )(inverse, panel, window)
+    return factor, weights
 
 
 def take_kernel(order, block_ref, out_ref):
@@ -159,11 +175,11 @@
     )(order, blocks)
 
 
-BLOCK, OWN, OWN_HAS, FROM, FROM_HAS, PRESENT, ROWS = 0, 1, 2, (3, 4, 5), 6, 7, 8
+BLOCK, OWN, OWN_HAS, FROM, FROM_HAS, PRESENT, ROWS = 0, 1, 2, (3, 4), 5, 6, 7
 NEAR = 4
 
 
-def near_kernel(table, rows_ref, weight_ref, trailing_ref, own_ref, out_ref):
+def near_kernel(table, rows_ref, w0_ref, w1_ref, w2_ref, trailing_ref, own_ref, out_ref):
     i = pl.program_id(0)
     out_ref[...] = trailing_ref[...]
 
@@ -173,11 +189,11 @@
 
     @pl.when(table[PRESENT, i] == 1)
     def _():
-        out_ref[...] -= contract(rows_ref[...], weight_ref[...], 1, 1)
-
-
-def update_near(table, near, weight, trailing, own):
-    size, width = weight.shape
+        out_ref[...] -= product(rows_ref[...], (w0_ref[...], w1_ref[...], w2_ref[...]))
+
+
+def update_near(table, near, weights, trailing, own):
+    width, size = weights[0].shape
     square = lambda pick: pl.BlockSpec((size, size), pick)
     return pl.pallas_call(
         near_kernel,
@@ -186,7 +202,7 @@
             grid=(NEAR,),
             in_specs=[
                 pl.BlockSpec((size, width), lambda i, t: (t[ROWS, i], 0)),
-                pl.BlockSpec((size, width), lambda i, t: (0, 0)),
+                *[pl.BlockSpec((width, size), lambda i, t: (0, 0)) for _ in weights],
                 square(lambda i, t: (t[BLOCK, i], 0)),
                 square(lambda i, t: (t[OWN, i], 0)),
             ],
@@ -194,10 +210,10 @@
         ),
         out_shape=jax.ShapeDtypeStruct(trailing.shape, jnp.float32),
         compiler_params=pltpu.CompilerParams(vmem_limit_bytes=56 << 20),
-    )(table, near, weight, trailing, own)
-
-
-def far_kernel(table, done_ref, rows_ref, weight_ref, trailing_ref, own_ref, first_ref, main_ref, rest_ref, out_ref):
+    )(table, near, *weights, trailing, own)
+
+
+def far_kernel(table, done_ref, rows_ref, w0_ref, w1_ref, w2_ref, trailing_ref, own_ref, main_ref, rest_ref, out_ref):
     i = pl.program_id(0)
 
     @pl.when(i < NEAR)
@@ -214,17 +230,17 @@
 
         @pl.when(table[PRESENT, i] == 1)
         def _():
-            out_ref[...] -= contract(rows_ref[...], weight_ref[...], 1, 1)
-
-    for number, other_ref in enumerate((first_ref, main_ref, rest_ref)):
+            out_ref[...] -= product(rows_ref[...], (w0_ref[...], w1_ref[...], w2_ref[...]))
+
+    for number, other_ref in enumerate((main_ref, rest_ref)):
 
         @pl.when(table[FROM_HAS, i] == number + 1)
         def _():
             out_ref[...] += other_ref[...]
 
 
-def update_far(table, done, far, weight, trailing, own, others):
-    size, width = weight.shape
+def update_far(table, done, far, weights, trailing, own, others):
+    width, size = weights[0].shape
     last = NEAR - 1
     square = lambda pick: pl.BlockSpec((size, size), pick)
     return pl.pallas_call(
@@ -235,7 +251,7 @@
             in_specs=[
                 square(lambda i, t: (t[BLOCK, jnp.minimum(i, last)], 0)),
                 pl.BlockSpec((size, width), lambda i, t: (t[ROWS, jnp.maximum(i, NEAR)], 0)),
-                pl.BlockSpec((size, width), lambda i, t: (0, 0)),
+                *[pl.BlockSpec((width, size), lambda i, t: (0, 0)) for _ in weights],
                 square(lambda i, t: (t[BLOCK, jnp.maximum(i, NEAR)], 0)),
                 square(lambda i, t: (t[OWN, jnp.maximum(i, NEAR)], 0)),
                 *[square(lambda i, t, at=at: (t[at, i], 0)) for at in FROM],
@@ -245,7 +261,7 @@
         out_shape=jax.ShapeDtypeStruct(trailing.shape, jnp.float32),
         input_output_aliases={1: 0},
         compiler_params=pltpu.CompilerParams(vmem_limit_bytes=56 << 20),
-    )(table, done, far, weight, trailing, own, *others)
+    )(table, done, far, *weights, trailing, own, *others)
 
 
 def kept(has, index):
@@ -375,7 +391,7 @@
     held, from_left1, from_right1, child_map = tie((held, from_left1, from_right1, child_map))
     own_slots = child_map[0]
     own_count, own_place, order = crossing(own_slots, sub, blocks)
-    outgoing = [take_blocks(order[low:high], child[0], size) for low, high in ((0, FIRST), (FIRST, MAIN))]
+    outgoing = take_blocks(order[:MAIN], child[0], size)
     other_slots = swap(child_map)
     from_left2, from_right2 = right(from_left1, (1, 2)), left(from_right1, (1, 2))
     held = pivot_spread(held, (1,), x, y, z)
@@ -406,8 +422,8 @@
         jnp.where(other_index[:, None] == jnp.arange(other_place.shape[0])[None, :], other_place[None, :], 0),
         axis=1,
     )
-    starts = (0, FIRST, MAIN)
-    ends = (FIRST, MAIN, other_place.shape[0])
+    starts = (0, MAIN)
+    ends = (MAIN, other_place.shape[0])
     inside = [other_has & (place >= low) & (place < high) for low, high in zip(starts, ends)]
     present = jnp.sum(jnp.where(block[:, None] == step[None, :], pattern[:, 0][None, :], 0), axis=1) == 1
     rows = jnp.concatenate([kept(present[:NEAR], step[:NEAR]), kept(present[NEAR:], later[NEAR:])])
@@ -428,27 +444,26 @@
     slot3 = jnp.where(zl == 1, from_right2, jnp.where(zl == 2, from_left2, last))
     slots = jnp.concatenate([slot1, slot2, slot3], axis=0)
     held, table, need, outgoing = tie((held, table, need, outgoing))
-    first = swap(outgoing[0])
+    main = swap(outgoing)
     held = join_y(held, y)
     held, near, window, slots = tie((held, near, window, slots))
     far = gather_y(slots)
     window = window_x(window, x, 1)
     held = pivot_spread(held, (4,), x, y, z)
-    held, first, window, outgoing = tie((held, first, window, outgoing))
-    main = swap(outgoing[1])
+    held, window = tie((held, window))
     window = window_core(window, core)
     held = pivot_spread(held, (5,), x, y, z)
     parts = join_core(held, core)
     inverse = pivot_inverse(parts)
-    factor, weight = solve(inverse, panel, window)
-    done = update_near(table, near, weight, trailing, child[0])
+    factor, weights = solve(inverse, panel, window)
+    done = update_near(table, near, weights, trailing, child[0])
     done, main, need = tie((done, main, need))
     rest = lax.cond(
         need > MAIN,
         lambda: send_rest(order[MAIN:], child[0], size, need > MAIN + 1),
         lambda: jnp.zeros((2 * size, size), jnp.float32),
     )
-    updated = update_far(table, done, far, weight, trailing, child[0], (first, main, rest))
+    updated = update_far(table, done, far, weights, trailing, child[0], (main, rest))
     return (factor, updated)
 
 

time: 216 us -> 191 us (0.88); the launches traced: 220 us -> 189 us
  starting transfers between devices: 90.1 us -> 69.3 us
  Pallas kernels: 57.7 us -> 54.2 us
    ppermute x21 -> x19, starting transfers between devices: 79.1 us -> 58.3 us  [send(): return lax.ppermute(value, ALL, pairs_of(move))]
    pallas_call x3 -> x1, Pallas kernels: 5.04 us -> 2.86 us  [take_blocks(): pl.pallas_call(take_kernel, grid_spec=pltpu.PrefetchScalarGridSpec(num_sc...]
    ppermute x21 -> x19, waiting for transfers between devices: 28 us -> 25.9 us  [send(): return lax.ppermute(value, ALL, pairs_of(move))]
  transfers between devices with their start and end apart: 25 -> 23, of which waited for: 9 -> 7; matrix products, arithmetic and copies ran while one was open for 12% -> 11% of each run, Pallas kernels for 19% -> 20%
where the time goes in v7:
time: 191 us; the launch traced here: 189 us
  starting transfers between devices  69.3 us (36%)
  Pallas kernels  54.2 us (28%)
  waiting for transfers between devices  26.6 us (14%)
  other arithmetic  17.4 us (9%)
  between operations  15.9 us (8%)
  local copies, waits for them, and re-layouts  6.04 us (3%)
    ppermute x19, starting transfers between devices, send(): return lax.ppermute(value, ALL, pairs_of(move))  58.3 us
    pallas_call x1, Pallas kernels, pivot_inverse(): pl.pallas_call(pivot_kernel, out_shape=jax.ShapeDtypeStruct((width, width...  27.1 us
    ppermute x19, waiting for transfers between devices, send(): return lax.ppermute(value, ALL, pairs_of(move))  25.9 us
    pallas_call x1, Pallas kernels, update_far(): pl.pallas_call(far_kernel, grid_spec=pltpu.PrefetchScalarGridSpec(num_sca...  15.7 us
    ppermute x2, starting transfers between devices, window_owned(): return lax.ppermute(panel, ALL, sorted(place.items()))  10.9 us
    pallas_call x1, Pallas kernels, update_near(): pl.pallas_call(near_kernel, grid_spec=pltpu.PrefetchScalarGridSpec(num_sc...  5.54 us
  transfers between devices with their start and end apart: 23, of which 7 were waited for; matrix products, arithmetic and copies ran while one was open for 11% of the time, Pallas kernels for 20%

profile of v7, /device:TPU:1, one launch (start us, length us, event | category | flops | bytes accessed | tf_op | source)
XLA Modules:
  0.0 189.5 jit_solution(9512210593861232975)
XLA Ops:
  8.0 5.3 %collective-permute-start.4 = (f32[256,512]{1,0:T(8,128)}, f32[256,512]{1,0:T(8,128)}, u32[]{:S(2)}, u32[]{:S(2)}) collective-permute-start(f32[256,512]{1,0:T(8,128)} %panel_ref.1), channel_id=1, source_target_pairs={{0,4},{4,8},{8,12},{128,132},{132,136},{136,140},{1,5},{5,9},{9,13... | collective-permute-start | bytes 1572872 | tf_op jit(solution)/shard_map/ppermute | solution.py:32
  13.2 1.3 collective-permute-start.5
  16.5 1.4 collective-permute-start.2
  20.8 7.3 %collective-permute-start.3 = (f32[128,384]{1,0:T(8,128)S(1)}, f32[128,384]{1,0:T(8,128)S(1)}, u32[]{:S(2)}, u32[]{:S(2)}) collective-permute-start(f32[128,384]{1,0:T(8,128)S(1)} %slice_select_fusion), channel_id=1, source_target_pairs={{0,128},{1,129},{16,144},{17,145}} | collective-permute-start | bytes 589832 | tf_op jit(solution)/shard_map/ppermute | solution.py:32
  28.7 5.2 %collective-permute-start.13 = (f32[256,512]{1,0:T(8,128)S(1)}, f32[256,512]{1,0:T(8,128)}, u32[]{:S(2)}, u32[]{:S(2)}) collective-permute-start(f32[256,512]{1,0:T(8,128)S(1)} %copy-done), channel_id=1, source_target_pairs={{2,128},{3,129},{4,130},{5,131},{6,132},{7,133},{8,134},{9,135},{1... | collective-permute-start | bytes 1572872 | tf_op jit(solution)/shard_map/ppermute | solution.py:342
  33.9 5.7 %collective-permute-start.12 = (f32[256,512]{1,0:T(8,128)S(1)}, f32[256,512]{1,0:T(8,128)}, u32[]{:S(2)}, u32[]{:S(2)}) collective-permute-start(f32[256,512]{1,0:T(8,128)S(1)} %copy-done), channel_id=1, source_target_pairs={{2,0},{3,1},{4,2},{5,3},{6,4},{7,5},{8,6},{9,7},{10,8},{11,9},{12,... | collective-permute-start | bytes 1572872 | tf_op jit(solution)/shard_map/ppermute | solution.py:342
  40.4 1.3 collective-permute-start.6
  42.4 1.3 collective-permute-start.8
  44.4 2.9 %shard_map.77 = f32[1536,256]{1,0:T(8,128)} custom-call(s32[6]{0:T(128)S(1)} %bitcast.55, f32[2048,256]{1,0:T(8,128)S(1)} %bitcast.46), custom_call_target="tpu_custom_call" | custom-call | tf_op jit(solution)/shard_map/pallas_call | solution.py:165
  49.5 6.0 %collective-permute-done.9 = s32[1,8]{1,0:T(1,128)S(1)} collective-permute-done((s32[1,8]{1,0:T(1,128)S(1)}, s32[1,8]{1,0:T(1,128)S(1)}, u32[]{:S(2)}, u32[]{:S(2)}) %collective-permute-start.9) | collective-permute-done | bytes 64 | tf_op jit(solution)/shard_map/ppermute | solution.py:32
  55.5 1.8 collective-permute-done.8
  60.0 1.3 collective-permute-start.10
  61.3 1.9 %broadcast_select_fusion.5 = f32[256,512]{1,0:T(8,128)} fusion(f32[256,512]{1,0:T(8,128)S(1)} %collective-permute-done.7, f32[256,512]{1,0:T(8,128)} %collective-permute-done.8, pred[]{:T(512)S(6)} %eq.173), kind=kLoop, calls=%fused_computation.12 | loop fusion | flops 131072 | bytes 1572865 | tf_op jit(solution)/shard_map/jit(_where)/select_n | solution.py:401
  67.6 6.3 %collective-permute-done.11 = f32[256,512]{1,0:T(8,128)} collective-permute-done((f32[256,512]{1,0:T(8,128)}, f32[256,512]{1,0:T(8,128)}, u32[]{:S(2)}, u32[]{:S(2)}) %collective-permute-start.11) | collective-permute-done | bytes 524320 | tf_op jit(solution)/shard_map/ppermute | solution.py:32
  73.9 1.3 collective-permute-start.14
  76.4 1.5 collective-permute-start.16
  77.9 3.4 %collective-permute-start.15 = (f32[128,384]{1,0:T(8,128)S(1)}, f32[128,384]{1,0:T(8,128)S(1)}, u32[]{:S(2)}, u32[]{:S(2)}) collective-permute-start(f32[128,384]{1,0:T(8,128)S(1)} %broadcast_select_fusion.13), channel_id=1, source_target_pairs={{0,1},{4,5},{8,9},{12,13},{128,129},{132,133},{136,137},{140,141},... | collective-permute-start | bytes 589832 | tf_op jit(solution)/shard_map/ppermute | solution.py:32
  81.3 1.8 select_select_fusion.1
  83.1 1.4 pad_maximum_fusion.1
  84.5 1.6 collective-permute-done.15
  87.0 2.2 %collective-permute-start.17 = (f32[2,128,384]{2,1,0:T(8,128)S(1)}, f32[2,128,384]{2,1,0:T(8,128)}, u32[]{:S(2)}, u32[]{:S(2)}) collective-permute-start(f32[2,128,384]{2,1,0:T(8,128)S(1)} %pad_maximum_fusion.3), channel_id=1, source_target_pairs={{0,64},{4,68},{8,72},{12,76},{128,192},{132,196},{136,200},{140,20... | collective-permute-start | bytes 1179656 | tf_op jit(solution)/shard_map/ppermute | solution.py:32
  89.2 1.5 collective-permute-start.18
  90.7 7.3 %collective-permute-start.22 = (f32[1536,256]{1,0:T(8,128)}, f32[1536,256]{1,0:T(8,128)}, u32[]{:S(2)}, u32[]{:S(2)}) collective-permute-start(f32[1536,256]{1,0:T(8,128)} %shard_map.77), channel_id=1, source_target_pairs={{0,128},{4,132},{8,136},{12,140},{128,0},{132,4},{136,8},{140,12},... | collective-permute-start | bytes 4718600 | tf_op jit(solution)/shard_map/ppermute | solution.py:32
  99.0 1.3 collective-permute-start.19
  100.3 1.3 collective-permute-start.21
  101.6 7.6 %collective-permute-done.19 = f32[2,128,384]{2,1,0:T(8,128)S(1)} collective-permute-done((f32[2,128,384]{2,1,0:T(8,128)S(1)}, f32[2,128,384]{2,1,0:T(8,128)S(1)}, u32[]{:S(2)}, u32[]{:S(2)}) %collective-permute-start.19) | collective-permute-done | bytes 393248 | tf_op jit(solution)/shard_map/ppermute | solution.py:32
  109.2 17.2 %collective-permute-start.20 = (f32[2,128,384]{2,1,0:T(8,128)S(1)}, f32[2,128,384]{2,1,0:T(8,128)}, u32[]{:S(2)}, u32[]{:S(2)}) collective-permute-start(f32[2,128,384]{2,1,0:T(8,128)S(1)} %broadcast_select_fusion.7), channel_id=1, source_target_pairs={{0,16},{4,20},{8,24},{12,28},{128,144},{132,148},{136,152},{140,15... | collective-permute-start | bytes 1179656 | tf_op jit(solution)/shard_map/ppermute | solution.py:32
  126.6 1.4 collective-permute-done.20
  129.1 27.1 %shard_map.78.inverse_ref = f32[512,512]{1,0:T(8,128)S(1)} custom-call(f32[2,256,384]{2,1,0:T(8,128)S(1)} %pad_maximum_fusion.2.parts_ref), custom_call_target="tpu_custom_call" | custom-call | tf_op jit(solution)/shard_map/pallas_call | solution.py:116
  156.1 3.0 %shard_map.79 = (f32[256,512]{1,0:T(8,128)}, bf16[512,256]{1,0:T(8,128)(2,1)S(1)}, bf16[512,256]{1,0:T(8,128)(2,1)S(1)}, bf16[512,256]{1,0:T(8,128)(2,1)S(1)}) custom-call(f32[512,512]{1,0:T(8,128)S(1)} %shard_map.78.inverse_ref, f32[256,512]{1,0:T(8,128)S(1)} %copy-done, f32[256,512]{1,0:T(8,128)S(1)} %broadcast_select_fusion.window_ref), custom_call_target="tpu_custom_call" | custom-call | tf_op jit(solution)/shard_map/pallas_call | solution.py:151
  161.3 5.5 %shard_map.80.done_ref = f32[4096,256]{1,0:T(8,128)} custom-call(s32[8,16]{1,0:T(8,128)} %stack.11.table, f32[1024,512]{1,0:T(8,128)} %all-gather.3.cloned.1.call-done.rows_ref, bf16[512,256]{1,0:T(8,128)(2,1)} %copy-done.1, bf16[512,256]{1,0:T(8,128)(2,1)} %copy-done.2, bf16[512,256]{1,0:T(8,128)(2,1)} %copy-done.3, f32[4096,256]{1,0:T(8,128)} %trailing_ref.3, ...), custom_call_target="tpu_custom_call" | custom-call | tf_op jit(solution)/shard_map/pallas_call | solution.py:198
  166.9 15.7 %shard_map.81 = f32[4096,256]{1,0:T(8,128)} custom-call(s32[8,16]{1,0:T(8,128)} %stack.11.table, f32[4096,256]{1,0:T(8,128)} %shard_map.80.done_ref, f32[3072,512]{1,0:T(8,128)} %all-gather.5.cloned.1.call-done.rows_ref, bf16[512,256]{1,0:T(8,128)(2,1)} %copy-done.1, bf16[512,256]{1,0:T(8,128)(2,1)} %copy-done.2, ...), custom_call_target="tpu_custom_call", output_to_operand_aliasing={{}: (1, {})} | custom-call | tf_op jit(solution)/shard_map/pallas_call | solution.py:246
  (109 shorter events, 22.7 us)
Async XLA Ops:
  7.2 9.3 %copy-start = (f32[256,512]{1,0:T(8,128)S(1)}, f32[256,512]{1,0:T(8,128)}, u32[]{:S(2)}) copy-start(f32[256,512]{1,0:T(8,128)} %panel_ref.1) | copy-start | bytes 1572868
  7.2 11.7 %copy-start.12 = (s32[16,1]{0,1:T(1,128)S(1)}, s32[16,1]{0,1:T(1,128)}, u32[]{:S(2)}) copy-start(s32[16,1]{0,1:T(1,128)} %param.14) | copy-start | bytes 196
  7.2 79.8 %all-gather.3.cloned.1.call-start = ((), (), s32[]{:S(2)}) async-start(), calls=%async_computation | async-start | bytes 2621440 | tf_op jit(solution)/shard_map/all_gather | solution.py:359
  7.9 159.0 %all-gather.5.cloned.1.call-start = ((), (), s32[]{:S(2)}) async-start(), calls=%async_computation.1 | async-start | bytes 7864320 | tf_op jit(solution)/shard_map/all_gather | solution.py:359
  8.0 31.7 %collective-permute-start.4 = (f32[256,512]{1,0:T(8,128)}, f32[256,512]{1,0:T(8,128)}, u32[]{:S(2)}, u32[]{:S(2)}) collective-permute-start(f32[256,512]{1,0:T(8,128)} %panel_ref.1), channel_id=1, source_target_pairs={{0,4},{4,8},{8,12},{128,132},{132,136},{136,140},{1,5},{5,9},{9,13... | collective-permute-start | bytes 1572872 | tf_op jit(solution)/shard_map/ppermute | solution.py:32
  13.2 26.4 %collective-permute-start.5 = (f32[256,512]{1,0:T(8,128)}, f32[256,512]{1,0:T(8,128)}, u32[]{:S(2)}, u32[]{:S(2)}) collective-permute-start(f32[256,512]{1,0:T(8,128)} %panel_ref.1), channel_id=1, source_target_pairs={{4,0},{8,4},{12,8},{132,128},{136,132},{140,136},{5,1},{9,5},{13,9... | collective-permute-start | bytes 1572872 | tf_op jit(solution)/shard_map/ppermute | solution.py:32
  16.4 23.3 %copy-start.8 = (s32[1,8]{1,0:T(1,128)S(1)}, s32[1,8]{1,0:T(1,128)}, u32[]{:S(2)}) copy-start(s32[1,8]{1,0:T(1,128)} %param.13) | copy-start | bytes 100
  16.4 28.0 %copy-start.4 = (f32[1,2048,256]{2,1,0:T(8,128)S(1)}, f32[1,2048,256]{2,1,0:T(8,128)}, u32[]{:S(2)}) copy-start(f32[1,2048,256]{2,1,0:T(8,128)} %param.12) | copy-start | bytes 6291460
  16.5 4.2 %collective-permute-start.2 = (f32[128,384]{1,0:T(8,128)S(1)}, f32[128,384]{1,0:T(8,128)S(1)}, u32[]{:S(2)}, u32[]{:S(2)}) collective-permute-start(f32[128,384]{1,0:T(8,128)S(1)} %slice.55), channel_id=1, source_target_pairs={{0,16},{1,17}} | collective-permute-start | bytes 589832 | tf_op jit(solution)/shard_map/ppermute | solution.py:32
  20.8 18.8 %collective-permute-start.3 = (f32[128,384]{1,0:T(8,128)S(1)}, f32[128,384]{1,0:T(8,128)S(1)}, u32[]{:S(2)}, u32[]{:S(2)}) collective-permute-start(f32[128,384]{1,0:T(8,128)S(1)} %slice_select_fusion), channel_id=1, source_target_pairs={{0,128},{1,129},{16,144},{17,145}} | collective-permute-start | bytes 589832 | tf_op jit(solution)/shard_map/ppermute | solution.py:32
  28.7 38.9 %collective-permute-start.13 = (f32[256,512]{1,0:T(8,128)S(1)}, f32[256,512]{1,0:T(8,128)}, u32[]{:S(2)}, u32[]{:S(2)}) collective-permute-start(f32[256,512]{1,0:T(8,128)S(1)} %copy-done), channel_id=1, source_target_pairs={{2,128},{3,129},{4,130},{5,131},{6,132},{7,133},{8,134},{9,135},{1... | collective-permute-start | bytes 1572872 | tf_op jit(solution)/shard_map/ppermute | solution.py:342
  33.9 33.8 %collective-permute-start.12 = (f32[256,512]{1,0:T(8,128)S(1)}, f32[256,512]{1,0:T(8,128)}, u32[]{:S(2)}, u32[]{:S(2)}) collective-permute-start(f32[256,512]{1,0:T(8,128)S(1)} %copy-done), channel_id=1, source_target_pairs={{2,0},{3,1},{4,2},{5,3},{6,4},{7,5},{8,6},{9,7},{10,8},{11,9},{12,... | collective-permute-start | bytes 1572872 | tf_op jit(solution)/shard_map/ppermute | solution.py:342
  40.4 8.7 %collective-permute-start.6 = (f32[128,384]{1,0:T(8,128)S(1)}, f32[128,384]{1,0:T(8,128)S(1)}, u32[]{:S(2)}, u32[]{:S(2)}) collective-permute-start(f32[128,384]{1,0:T(8,128)S(1)} %broadcast_select_fusion.10), channel_id=1, source_target_pairs={{0,8},{128,136},{1,9},{129,137},{16,24},{144,152},{17,25},{145,153}} | collective-permute-start | bytes 589832 | tf_op jit(solution)/shard_map/ppermute | solution.py:32
  41.7 13.7 %collective-permute-start.7 = (f32[256,512]{1,0:T(8,128)}, f32[256,512]{1,0:T(8,128)S(1)}, u32[]{:S(2)}, u32[]{:S(2)}) collective-permute-start(f32[256,512]{1,0:T(8,128)} %collective-permute-done.4), channel_id=1, source_target_pairs={{4,8},{8,12},{132,136},{136,140},{5,9},{9,13},{133,137},{137,141},... | collective-permute-start | bytes 1572872 | tf_op jit(solution)/shard_map/ppermute | solution.py:32
  42.4 14.9 %collective-permute-start.8 = (f32[256,512]{1,0:T(8,128)}, f32[256,512]{1,0:T(8,128)}, u32[]{:S(2)}, u32[]{:S(2)}) collective-permute-start(f32[256,512]{1,0:T(8,128)} %collective-permute-done.5), channel_id=1, source_target_pairs={{4,0},{8,4},{132,128},{136,132},{5,1},{9,5},{133,129},{137,133},{6... | collective-permute-start | bytes 1572872 | tf_op jit(solution)/shard_map/ppermute | solution.py:32
  44.4 2.9 %copy-start.10 = (s32[8]{0:T(128)}, s32[8]{0:T(128)S(1)}, u32[]{:S(2)}) copy-start(s32[8]{0:T(128)S(1)} %select_reduce_fusion.5) | copy-start | bytes 100
  49.2 6.3 %collective-permute-start.9 = (s32[1,8]{1,0:T(1,128)S(1)}, s32[1,8]{1,0:T(1,128)S(1)}, u32[]{:S(2)}, u32[]{:S(2)}) collective-permute-start(s32[1,8]{1,0:T(1,128)S(1)} %copy-done.8), channel_id=1, source_target_pairs={{0,128},{4,132},{8,136},{12,140},{128,0},{132,4},{136,8},{140,12},... | collective-permute-start | bytes 104 | tf_op jit(solution)/shard_map/ppermute | solution.py:32
  55.5 18.5 %copy-start.6 = (f32[256,512]{1,0:T(8,128)}, f32[256,512]{1,0:T(8,128)S(1)}, u32[]{:S(2)}) copy-start(f32[256,512]{1,0:T(8,128)S(1)} %collective-permute-done.7) | copy-start | bytes 1572868
  59.9 5.3 %copy-start.9 = (s32[16]{0:T(128)S(1)}, s32[16]{0:T(128)}, u32[]{:S(2)}) copy-start(s32[16]{0:T(128)} %get-tuple-element.69) | copy-start | bytes 196
  60.0 7.5 %collective-permute-start.10 = (f32[128,384]{1,0:T(8,128)S(1)}, f32[128,384]{1,0:T(8,128)S(1)}, u32[]{:S(2)}, u32[]{:S(2)}) collective-permute-start(f32[128,384]{1,0:T(8,128)S(1)} %broadcast_select_fusion.11), channel_id=1, source_target_pairs={{0,4},{8,12},{128,132},{136,140},{1,5},{9,13},{129,133},{137,141},... | collective-permute-start | bytes 589832 | tf_op jit(solution)/shard_map/ppermute | solution.py:32
  63.3 10.7 %collective-permute-start.11 = (f32[256,512]{1,0:T(8,128)}, f32[256,512]{1,0:T(8,128)}, u32[]{:S(2)}, u32[]{:S(2)}) collective-permute-start(f32[256,512]{1,0:T(8,128)} %broadcast_select_fusion.5), channel_id=1, source_target_pairs={{4,0},{8,12},{132,128},{136,140},{5,1},{9,13},{133,129},{137,141},... | collective-permute-start | bytes 1572872 | tf_op jit(solution)/shard_map/ppermute | solution.py:32
  73.9 4.0 %collective-permute-start.14 = (f32[128,384]{1,0:T(8,128)S(1)}, f32[128,384]{1,0:T(8,128)S(1)}, u32[]{:S(2)}, u32[]{:S(2)}) collective-permute-start(f32[128,384]{1,0:T(8,128)S(1)} %broadcast_select_fusion.12), channel_id=1, source_target_pairs={{0,2},{4,6},{8,10},{12,14},{128,130},{132,134},{136,138},{140,142}... | collective-permute-start | bytes 589832 | tf_op jit(solution)/shard_map/ppermute | solution.py:32
  75.2 6.1 %copy-start.7 = (f32[256,512]{1,0:T(8,128)S(1)}, f32[256,512]{1,0:T(8,128)}, u32[]{:S(2)}) copy-start(f32[256,512]{1,0:T(8,128)} %copy-done.6) | copy-start | bytes 1572868
  76.4 9.6 %collective-permute-start.16 = (f32[256,512]{1,0:T(8,128)S(1)}, f32[256,512]{1,0:T(8,128)}, u32[]{:S(2)}, u32[]{:S(2)}) collective-permute-start(f32[256,512]{1,0:T(8,128)S(1)} %broadcast_select_fusion.3), channel_id=1, source_target_pairs={{0,64},{4,68},{8,72},{12,76},{128,192},{132,196},{136,200},{140,20... | collective-permute-start | bytes 1572872 | tf_op jit(solution)/shard_map/ppermute | solution.py:32
  77.9 8.1 %collective-permute-start.15 = (f32[128,384]{1,0:T(8,128)S(1)}, f32[128,384]{1,0:T(8,128)S(1)}, u32[]{:S(2)}, u32[]{:S(2)}) collective-permute-start(f32[128,384]{1,0:T(8,128)S(1)} %broadcast_select_fusion.13), channel_id=1, source_target_pairs={{0,1},{4,5},{8,9},{12,13},{128,129},{132,133},{136,137},{140,141},... | collective-permute-start | bytes 589832 | tf_op jit(solution)/shard_map/ppermute | solution.py:32
  87.0 11.0 %collective-permute-start.17 = (f32[2,128,384]{2,1,0:T(8,128)S(1)}, f32[2,128,384]{2,1,0:T(8,128)}, u32[]{:S(2)}, u32[]{:S(2)}) collective-permute-start(f32[2,128,384]{2,1,0:T(8,128)S(1)} %pad_maximum_fusion.3), channel_id=1, source_target_pairs={{0,64},{4,68},{8,72},{12,76},{128,192},{132,196},{136,200},{140,20... | collective-permute-start | bytes 1179656 | tf_op jit(solution)/shard_map/ppermute | solution.py:32
  89.2 8.9 %collective-permute-start.18 = (f32[256,512]{1,0:T(8,128)S(1)}, f32[256,512]{1,0:T(8,128)}, u32[]{:S(2)}, u32[]{:S(2)}) collective-permute-start(f32[256,512]{1,0:T(8,128)S(1)} %copy-done.5), channel_id=1, source_target_pairs={{0,32},{4,36},{8,40},{12,44},{128,160},{132,164},{136,168},{140,17... | collective-permute-start | bytes 1572872 | tf_op jit(solution)/shard_map/ppermute | solution.py:32
  90.7 76.1 %collective-permute-start.22 = (f32[1536,256]{1,0:T(8,128)}, f32[1536,256]{1,0:T(8,128)}, u32[]{:S(2)}, u32[]{:S(2)}) collective-permute-start(f32[1536,256]{1,0:T(8,128)} %shard_map.77), channel_id=1, source_target_pairs={{0,128},{4,132},{8,136},{12,140},{128,0},{132,4},{136,8},{140,12},... | collective-permute-start | bytes 4718600 | tf_op jit(solution)/shard_map/ppermute | solution.py:32
  99.0 10.2 %collective-permute-start.19 = (f32[2,128,384]{2,1,0:T(8,128)S(1)}, f32[2,128,384]{2,1,0:T(8,128)S(1)}, u32[]{:S(2)}, u32[]{:S(2)}) collective-permute-start(f32[2,128,384]{2,1,0:T(8,128)S(1)} %broadcast_select_fusion.6), channel_id=1, source_target_pairs={{0,32},{4,36},{8,40},{12,44},{128,160},{132,164},{136,168},{140,17... | collective-permute-start | bytes 1179656 | tf_op jit(solution)/shard_map/ppermute | solution.py:32
  100.3 26.1 %collective-permute-start.21 = (f32[256,512]{1,0:T(8,128)}, f32[256,512]{1,0:T(8,128)S(1)}, u32[]{:S(2)}, u32[]{:S(2)}) collective-permute-start(f32[256,512]{1,0:T(8,128)} %broadcast_select_fusion.1), channel_id=1, source_target_pairs={{0,16},{4,20},{8,24},{12,28},{128,144},{132,148},{136,152},{140,15... | collective-permute-start | bytes 1572872 | tf_op jit(solution)/shard_map/ppermute | solution.py:32
  109.2 18.7 %collective-permute-start.20 = (f32[2,128,384]{2,1,0:T(8,128)S(1)}, f32[2,128,384]{2,1,0:T(8,128)}, u32[]{:S(2)}, u32[]{:S(2)}) collective-permute-start(f32[2,128,384]{2,1,0:T(8,128)S(1)} %broadcast_select_fusion.7), channel_id=1, source_target_pairs={{0,16},{4,20},{8,24},{12,28},{128,144},{132,148},{136,152},{140,15... | collective-permute-start | bytes 1179656 | tf_op jit(solution)/shard_map/ppermute | solution.py:32
  161.3 5.6 %copy-start.11 = (s32[8]{0:T(128)S(1)}, s32[8]{0:T(128)}, u32[]{:S(2)}) copy-start(s32[8]{0:T(128)} %copy-done.10) | copy-start | bytes 100
  (4 other events, 4.3 us)
Sparse Core Ops, SparseCore 0:
  9.8 41.8 all-gather.2
  87.1 74.7 all-gather.4

commit v8 on v7

--- a/solution.py
+++ b/solution.py
@@ -179,89 +179,79 @@
 NEAR = 4
 
 
-def near_kernel(table, rows_ref, w0_ref, w1_ref, w2_ref, trailing_ref, own_ref, out_ref):
-    i = pl.program_id(0)
-    out_ref[...] = trailing_ref[...]
-
-    @pl.when(table[OWN_HAS, i] == 1)
-    def _():
-        out_ref[...] += own_ref[...]
-
-    @pl.when(table[PRESENT, i] == 1)
-    def _():
-        out_ref[...] -= product(rows_ref[...], (w0_ref[...], w1_ref[...], w2_ref[...]))
-
-
-def update_near(table, near, weights, trailing, own):
+def update_kernel(
+    table, w0_ref, w1_ref, w2_ref, near, far, trailing, own, main, rest, out,
+    rows, base, own_held, main_held, rest_held, rows_sem, base_sem, child_sem, out_sem,
+):
+    blocks, size = base.shape[:2]
+    place = lambda i: pl.ds(pl.multiple_of(table[BLOCK, i] * size, size), size)
+    children = [
+        pltpu.make_async_copy(source, held, child_sem.at[k])
+        for k, (source, held) in enumerate(((own, own_held), (main, main_held), (rest, rest_held)))
+    ]
+    rows_in = lambda i: pltpu.make_async_copy(
+        near.at[pl.ds(i * size, size)] if i < NEAR else far.at[pl.ds((i - NEAR) * size, size)],
+        rows.at[i],
+        rows_sem.at[i],
+    )
+    base_in = lambda i: pltpu.make_async_copy(trailing.at[place(i)], base.at[i], base_sem.at[i])
+    base_out = lambda i: pltpu.make_async_copy(base.at[i], out.at[place(i)], out_sem.at[i])
+    for copy in children:
+        copy.start()
+    for i in range(blocks):
+        base_in(i).start()
+
+        @pl.when(table[PRESENT, i] == 1)
+        def _(i=i):
+            rows_in(i).start()
+
+    for copy in children:
+        copy.wait()
+    for i in range(blocks):
+        base_in(i).wait()
+        for has, at, held in (
+            (table[OWN_HAS, i] == 1, OWN, own_held),
+            (table[FROM_HAS, i] == 1, FROM[0], main_held),
+            (table[FROM_HAS, i] == 2, FROM[1], rest_held),
+        ):
+
+            @pl.when(has)
+            def _(at=at, held=held):
+                base[i] += held[pl.ds(pl.multiple_of(table[at, i] * size, size), size), :]
+
+        @pl.when(table[PRESENT, i] == 1)
+        def _(i=i):
+            rows_in(i).wait()
+            base[i] -= product(rows[i], (w0_ref[...], w1_ref[...], w2_ref[...]))
+
+        base_out(i).start()
+    for i in range(blocks):
+        base_out(i).wait()
+
+
+def update(table, near, far, weights, trailing, own, main, rest):
     width, size = weights[0].shape
-    square = lambda pick: pl.BlockSpec((size, size), pick)
+    blocks = trailing.shape[0] // size
+    anywhere = pl.BlockSpec(memory_space=pl.ANY)
+    inside = pl.BlockSpec(memory_space=pltpu.VMEM)
     return pl.pallas_call(
-        near_kernel,
-        grid_spec=pltpu.PrefetchScalarGridSpec(
-            num_scalar_prefetch=1,
-            grid=(NEAR,),
-            in_specs=[
-                pl.BlockSpec((size, width), lambda i, t: (t[ROWS, i], 0)),
-                *[pl.BlockSpec((width, size), lambda i, t: (0, 0)) for _ in weights],
-                square(lambda i, t: (t[BLOCK, i], 0)),
-                square(lambda i, t: (t[OWN, i], 0)),
-            ],
-            out_specs=square(lambda i, t: (t[BLOCK, i], 0)),
-        ),
+        update_kernel,
+        in_specs=[pl.BlockSpec(memory_space=pltpu.SMEM), inside, inside, inside] + [anywhere] * 6,
+        out_specs=anywhere,
         out_shape=jax.ShapeDtypeStruct(trailing.shape, jnp.float32),
+        scratch_shapes=[
+            pltpu.VMEM((blocks, size, width), jnp.float32),
+            pltpu.VMEM((blocks, size, size), jnp.float32),
+            pltpu.VMEM(own.shape, jnp.float32),
+            pltpu.VMEM(main.shape, jnp.float32),
+            pltpu.VMEM(rest.shape, jnp.float32),
+            pltpu.SemaphoreType.DMA((blocks,)),
+            pltpu.SemaphoreType.DMA((blocks,)),
+            pltpu.SemaphoreType.DMA((3,)),
+            pltpu.SemaphoreType.DMA((blocks,)),
+        ],
         compiler_params=pltpu.CompilerParams(vmem_limit_bytes=56 << 20),
-    )(table, near, *weights, trailing, own)
-
-
-def far_kernel(table, done_ref, rows_ref, w0_ref, w1_ref, w2_ref, trailing_ref, own_ref, main_ref, rest_ref, out_ref):
-    i = pl.program_id(0)
-
-    @pl.when(i < NEAR)
-    def _():
-        out_ref[...] = done_ref[...]
-
-    @pl.when(i >= NEAR)
-    def _():
-        out_ref[...] = trailing_ref[...]
-
-        @pl.when(table[OWN_HAS, i] == 1)
-        def _():
-            out_ref[...] += own_ref[...]
-
-        @pl.when(table[PRESENT, i] == 1)
-        def _():
-            out_ref[...] -= product(rows_ref[...], (w0_ref[...], w1_ref[...], w2_ref[...]))
-
-    for number, other_ref in enumerate((main_ref, rest_ref)):
-
-        @pl.when(table[FROM_HAS, i] == number + 1)
-        def _():
-            out_ref[...] += other_ref[...]
-
-
-def update_far(table, done, far, weights, trailing, own, others):
-    width, size = weights[0].shape
-    last = NEAR - 1
-    square = lambda pick: pl.BlockSpec((size, size), pick)
-    return pl.pallas_call(
-        far_kernel,
-        grid_spec=pltpu.PrefetchScalarGridSpec(
-            num_scalar_prefetch=1,
-            grid=(trailing.shape[0] // size,),
-            in_specs=[
-                square(lambda i, t: (t[BLOCK, jnp.minimum(i, last)], 0)),
-                pl.BlockSpec((size, width), lambda i, t: (t[ROWS, jnp.maximum(i, NEAR)], 0)),
-                *[pl.BlockSpec((width, size), lambda i, t: (0, 0)) for _ in weights],
-                square(lambda i, t: (t[BLOCK, jnp.maximum(i, NEAR)], 0)),
-                square(lambda i, t: (t[OWN, jnp.maximum(i, NEAR)], 0)),
-                *[square(lambda i, t, at=at: (t[at, i], 0)) for at in FROM],
-            ],
-            out_specs=square(lambda i, t: (t[BLOCK, i], 0)),
-        ),
-        out_shape=jax.ShapeDtypeStruct(trailing.shape, jnp.float32),
-        input_output_aliases={1: 0},
-        compiler_params=pltpu.CompilerParams(vmem_limit_bytes=56 << 20),
-    )(table, done, far, *weights, trailing, own, *others)
+    )(table, *weights, near, far, trailing, own, main, rest)
 
 
 def kept(has, index):
@@ -456,14 +446,13 @@
     parts = join_core(held, core)
     inverse = pivot_inverse(parts)
     factor, weights = solve(inverse, panel, window)
-    done = update_near(table, near, weights, trailing, child[0])
-    done, main, need = tie((done, main, need))
+    weights, main, need = tie((weights, main, need))
     rest = lax.cond(
         need > MAIN,
         lambda: send_rest(order[MAIN:], child[0], size, need > MAIN + 1),
         lambda: jnp.zeros((2 * size, size), jnp.float32),
     )
-    updated = update_far(table, done, far, weights, trailing, child[0], (main, rest))
+    updated = update(table, near, far, weights, trailing, child[0], main, rest)
     return (factor, updated)
 
 

time: 191 us -> 185 us (0.969)
  Pallas kernels: 54.2 us -> 43.7 us
  waiting for transfers between devices: 26.6 us -> 30 us
    pallas_call x2 -> x1, Pallas kernels: 21.3 us -> 10.7 us  [update(): pl.pallas_call(update_kernel, in_specs=[pl.BlockSpec(memory_space=pltpu.S...]
    ppermute x19, waiting for transfers between devices: 25.9 us -> 29.3 us  [send(): return lax.ppermute(value, ALL, pairs_of(move))]
  transfers between devices with their start and end apart: 23 -> 23, of which waited for: 7 -> 8; matrix products, arithmetic and copies ran while one was open for 11% -> 12% of each run, Pallas kernels for 20% -> 18%
where the time goes in v8:
time: 185 us; the launch traced here: 183 us
  starting transfers between devices  69.5 us (38%)
  Pallas kernels  43.7 us (24%)
  waiting for transfers between devices  30 us (16%)
  other arithmetic  17.2 us (9%)
  between operations  16.1 us (9%)
  local copies, waits for them, and re-layouts  6.02 us (3%)
    ppermute x19, starting transfers between devices, send(): return lax.ppermute(value, ALL, pairs_of(move))  58.5 us
    ppermute x19, waiting for transfers between devices, send(): return lax.ppermute(value, ALL, pairs_of(move))  29.3 us
    pallas_call x1, Pallas kernels, pivot_inverse(): pl.pallas_call(pivot_kernel, out_shape=jax.ShapeDtypeStruct((width, width...  27.1 us
    ppermute x2, starting transfers between devices, window_owned(): return lax.ppermute(panel, ALL, sorted(place.items()))  10.9 us
    pallas_call x1, Pallas kernels, update(): pl.pallas_call(update_kernel, in_specs=[pl.BlockSpec(memory_space=pltpu.S...  10.7 us
  transfers between devices with their start and end apart: 23, of which 8 were waited for; matrix products, arithmetic and copies ran while one was open for 12% of the time, Pallas kernels for 18%

profile of v8, /device:TPU:1, one launch (start us, length us, event | category | flops | bytes accessed | tf_op | source)
XLA Modules:
  0.0 182.6 jit_solution(15608614823634425641)
XLA Ops:
  8.0 5.2 %collective-permute-start.4 = (f32[256,512]{1,0:T(8,128)}, f32[256,512]{1,0:T(8,128)}, u32[]{:S(2)}, u32[]{:S(2)}) collective-permute-start(f32[256,512]{1,0:T(8,128)} %panel_ref.1), channel_id=1, source_target_pairs={{0,4},{4,8},{8,12},{128,132},{132,136},{136,140},{1,5},{5,9},{9,13... | collective-permute-start | bytes 1572872 | tf_op jit(solution)/shard_map/ppermute | solution.py:32
  13.2 1.3 collective-permute-start.5
  16.5 1.4 collective-permute-start.2
  20.7 7.3 %collective-permute-start.3 = (f32[128,384]{1,0:T(8,128)S(1)}, f32[128,384]{1,0:T(8,128)S(1)}, u32[]{:S(2)}, u32[]{:S(2)}) collective-permute-start(f32[128,384]{1,0:T(8,128)S(1)} %slice_select_fusion), channel_id=1, source_target_pairs={{0,128},{1,129},{16,144},{17,145}} | collective-permute-start | bytes 589832 | tf_op jit(solution)/shard_map/ppermute | solution.py:32
  28.5 5.2 %collective-permute-start.13 = (f32[256,512]{1,0:T(8,128)S(1)}, f32[256,512]{1,0:T(8,128)}, u32[]{:S(2)}, u32[]{:S(2)}) collective-permute-start(f32[256,512]{1,0:T(8,128)S(1)} %copy-done), channel_id=1, source_target_pairs={{2,128},{3,129},{4,130},{5,131},{6,132},{7,133},{8,134},{9,135},{1... | collective-permute-start | bytes 1572872 | tf_op jit(solution)/shard_map/ppermute | solution.py:332
  33.7 5.7 %collective-permute-start.12 = (f32[256,512]{1,0:T(8,128)S(1)}, f32[256,512]{1,0:T(8,128)}, u32[]{:S(2)}, u32[]{:S(2)}) collective-permute-start(f32[256,512]{1,0:T(8,128)S(1)} %copy-done), channel_id=1, source_target_pairs={{2,0},{3,1},{4,2},{5,3},{6,4},{7,5},{8,6},{9,7},{10,8},{11,9},{12,... | collective-permute-start | bytes 1572872 | tf_op jit(solution)/shard_map/ppermute | solution.py:332
  40.3 1.3 collective-permute-start.6
  42.3 1.3 collective-permute-start.8
  44.4 2.9 %shard_map.77 = f32[1536,256]{1,0:T(8,128)} custom-call(s32[6]{0:T(128)S(1)} %bitcast.54, f32[2048,256]{1,0:T(8,128)S(1)} %bitcast.46), custom_call_target="tpu_custom_call" | custom-call | tf_op jit(solution)/shard_map/pallas_call | solution.py:165
  49.6 5.8 %collective-permute-done.9 = s32[1,8]{1,0:T(1,128)S(1)} collective-permute-done((s32[1,8]{1,0:T(1,128)S(1)}, s32[1,8]{1,0:T(1,128)S(1)}, u32[]{:S(2)}, u32[]{:S(2)}) %collective-permute-start.9) | collective-permute-done | bytes 64 | tf_op jit(solution)/shard_map/ppermute | solution.py:32
  55.4 1.8 collective-permute-done.8
  60.0 1.3 collective-permute-start.10
  61.3 1.9 %broadcast_select_fusion.5 = f32[256,512]{1,0:T(8,128)} fusion(f32[256,512]{1,0:T(8,128)S(1)} %collective-permute-done.7, f32[256,512]{1,0:T(8,128)} %collective-permute-done.8, pred[]{:T(512)S(6)} %eq.173), kind=kLoop, calls=%fused_computation.12 | loop fusion | flops 131072 | bytes 1572865 | tf_op jit(solution)/shard_map/jit(_where)/select_n | solution.py:391
  66.3 1.3 stack.11.table
  67.6 6.3 %collective-permute-done.11 = f32[256,512]{1,0:T(8,128)} collective-permute-done((f32[256,512]{1,0:T(8,128)}, f32[256,512]{1,0:T(8,128)}, u32[]{:S(2)}, u32[]{:S(2)}) %collective-permute-start.11) | collective-permute-done | bytes 524320 | tf_op jit(solution)/shard_map/ppermute | solution.py:32
  73.9 1.3 collective-permute-start.14
  76.5 1.5 collective-permute-start.16
  78.0 3.3 %collective-permute-start.15 = (f32[128,384]{1,0:T(8,128)S(1)}, f32[128,384]{1,0:T(8,128)S(1)}, u32[]{:S(2)}, u32[]{:S(2)}) collective-permute-start(f32[128,384]{1,0:T(8,128)S(1)} %broadcast_select_fusion.13), channel_id=1, source_target_pairs={{0,1},{4,5},{8,9},{12,13},{128,129},{132,133},{136,137},{140,141},... | collective-permute-start | bytes 589832 | tf_op jit(solution)/shard_map/ppermute | solution.py:32
  81.3 1.8 select_select_fusion.1
  84.3 1.6 collective-permute-done.15
  87.0 2.2 %collective-permute-start.17 = (f32[2,128,384]{2,1,0:T(8,128)S(1)}, f32[2,128,384]{2,1,0:T(8,128)}, u32[]{:S(2)}, u32[]{:S(2)}) collective-permute-start(f32[2,128,384]{2,1,0:T(8,128)S(1)} %pad_maximum_fusion.3), channel_id=1, source_target_pairs={{0,64},{4,68},{8,72},{12,76},{128,192},{132,196},{136,200},{140,20... | collective-permute-start | bytes 1179656 | tf_op jit(solution)/shard_map/ppermute | solution.py:32
  89.1 1.5 collective-permute-start.18
  90.6 7.3 %collective-permute-start.22 = (f32[1536,256]{1,0:T(8,128)}, f32[1536,256]{1,0:T(8,128)}, u32[]{:S(2)}, u32[]{:S(2)}) collective-permute-start(f32[1536,256]{1,0:T(8,128)} %shard_map.77), channel_id=1, source_target_pairs={{0,128},{4,132},{8,136},{12,140},{128,0},{132,4},{136,8},{140,12},... | collective-permute-start | bytes 4718600 | tf_op jit(solution)/shard_map/ppermute | solution.py:32
  98.9 1.3 collective-permute-start.19
  100.2 1.3 collective-permute-start.21
  101.5 7.5 %collective-permute-done.19 = f32[2,128,384]{2,1,0:T(8,128)S(1)} collective-permute-done((f32[2,128,384]{2,1,0:T(8,128)S(1)}, f32[2,128,384]{2,1,0:T(8,128)S(1)}, u32[]{:S(2)}, u32[]{:S(2)}) %collective-permute-start.19) | collective-permute-done | bytes 393248 | tf_op jit(solution)/shard_map/ppermute | solution.py:32
  109.1 17.3 %collective-permute-start.20 = (f32[2,128,384]{2,1,0:T(8,128)S(1)}, f32[2,128,384]{2,1,0:T(8,128)}, u32[]{:S(2)}, u32[]{:S(2)}) collective-permute-start(f32[2,128,384]{2,1,0:T(8,128)S(1)} %broadcast_select_fusion.7), channel_id=1, source_target_pairs={{0,16},{4,20},{8,24},{12,28},{128,144},{132,148},{136,152},{140,15... | collective-permute-start | bytes 1179656 | tf_op jit(solution)/shard_map/ppermute | solution.py:32
  126.6 1.4 collective-permute-done.20
  129.1 27.1 %shard_map.78.inverse_ref = f32[512,512]{1,0:T(8,128)S(1)} custom-call(f32[2,256,384]{2,1,0:T(8,128)S(1)} %pad_maximum_fusion.2.parts_ref), custom_call_target="tpu_custom_call" | custom-call | tf_op jit(solution)/shard_map/pallas_call | solution.py:116
  156.2 3.0 %shard_map.79 = (f32[256,512]{1,0:T(8,128)}, bf16[512,256]{1,0:T(8,128)(2,1)S(1)}, bf16[512,256]{1,0:T(8,128)(2,1)S(1)}, bf16[512,256]{1,0:T(8,128)(2,1)S(1)}) custom-call(f32[512,512]{1,0:T(8,128)S(1)} %shard_map.78.inverse_ref, f32[256,512]{1,0:T(8,128)S(1)} %copy-done, f32[256,512]{1,0:T(8,128)S(1)} %broadcast_select_fusion.window_ref), custom_call_target="tpu_custom_call" | custom-call | tf_op jit(solution)/shard_map/pallas_call | solution.py:151
  161.3 3.7 %collective-permute-done.22.main = f32[1536,256]{1,0:T(8,128)} collective-permute-done((f32[1536,256]{1,0:T(8,128)}, f32[1536,256]{1,0:T(8,128)}, u32[]{:S(2)}, u32[]{:S(2)}) %collective-permute-start.22) | collective-permute-done | bytes 1572896 | tf_op jit(solution)/shard_map/ppermute | solution.py:32
  165.0 10.7 %shard_map.80 = f32[4096,256]{1,0:T(8,128)} custom-call(s32[8,16]{1,0:T(8,128)} %stack.11.table, bf16[512,256]{1,0:T(8,128)(2,1)} %copy-done.1, bf16[512,256]{1,0:T(8,128)(2,1)} %copy-done.2, bf16[512,256]{1,0:T(8,128)(2,1)} %copy-done.3, f32[1024,512]{1,0:T(8,128)} %all-gather.3.cloned.1.call-done.near, f32[3072,512]{1,0:T(8,128)} %all-gather.5.cloned.1.call-done.far, ...), custom_call_target="tpu_custom_call" | custom-call | tf_op jit(solution)/shard_map/pallas_call | solution.py:237
  (108 shorter events, 22.8 us)
Async XLA Ops:
  7.2 9.2 %copy-start = (f32[256,512]{1,0:T(8,128)S(1)}, f32[256,512]{1,0:T(8,128)}, u32[]{:S(2)}) copy-start(f32[256,512]{1,0:T(8,128)} %panel_ref.1) | copy-start | bytes 1572868
  7.2 11.6 %copy-start.12 = (s32[16,1]{0,1:T(1,128)S(1)}, s32[16,1]{0,1:T(1,128)}, u32[]{:S(2)}) copy-start(s32[16,1]{0,1:T(1,128)} %param.14) | copy-start | bytes 196
  7.2 79.8 %all-gather.3.cloned.1.call-start = ((), (), s32[]{:S(2)}) async-start(), calls=%async_computation | async-start | bytes 2621440 | tf_op jit(solution)/shard_map/all_gather | solution.py:349
  7.9 157.1 %all-gather.5.cloned.1.call-start = ((), (), s32[]{:S(2)}) async-start(), calls=%async_computation.1 | async-start | bytes 7864320 | tf_op jit(solution)/shard_map/all_gather | solution.py:349
  8.0 31.5 %collective-permute-start.4 = (f32[256,512]{1,0:T(8,128)}, f32[256,512]{1,0:T(8,128)}, u32[]{:S(2)}, u32[]{:S(2)}) collective-permute-start(f32[256,512]{1,0:T(8,128)} %panel_ref.1), channel_id=1, source_target_pairs={{0,4},{4,8},{8,12},{128,132},{132,136},{136,140},{1,5},{5,9},{9,13... | collective-permute-start | bytes 1572872 | tf_op jit(solution)/shard_map/ppermute | solution.py:32
  13.2 26.4 %collective-permute-start.5 = (f32[256,512]{1,0:T(8,128)}, f32[256,512]{1,0:T(8,128)}, u32[]{:S(2)}, u32[]{:S(2)}) collective-permute-start(f32[256,512]{1,0:T(8,128)} %panel_ref.1), channel_id=1, source_target_pairs={{4,0},{8,4},{12,8},{132,128},{136,132},{140,136},{5,1},{9,5},{13,9... | collective-permute-start | bytes 1572872 | tf_op jit(solution)/shard_map/ppermute | solution.py:32
  16.3 23.2 %copy-start.8 = (s32[1,8]{1,0:T(1,128)S(1)}, s32[1,8]{1,0:T(1,128)}, u32[]{:S(2)}) copy-start(s32[1,8]{1,0:T(1,128)} %param.13) | copy-start | bytes 100
  16.3 28.0 %copy-start.4 = (f32[1,2048,256]{2,1,0:T(8,128)S(1)}, f32[1,2048,256]{2,1,0:T(8,128)}, u32[]{:S(2)}) copy-start(f32[1,2048,256]{2,1,0:T(8,128)} %param.12) | copy-start | bytes 6291460
  16.5 4.2 %collective-permute-start.2 = (f32[128,384]{1,0:T(8,128)S(1)}, f32[128,384]{1,0:T(8,128)S(1)}, u32[]{:S(2)}, u32[]{:S(2)}) collective-permute-start(f32[128,384]{1,0:T(8,128)S(1)} %slice.55), channel_id=1, source_target_pairs={{0,16},{1,17}} | collective-permute-start | bytes 589832 | tf_op jit(solution)/shard_map/ppermute | solution.py:32
  20.7 18.8 %collective-permute-start.3 = (f32[128,384]{1,0:T(8,128)S(1)}, f32[128,384]{1,0:T(8,128)S(1)}, u32[]{:S(2)}, u32[]{:S(2)}) collective-permute-start(f32[128,384]{1,0:T(8,128)S(1)} %slice_select_fusion), channel_id=1, source_target_pairs={{0,128},{1,129},{16,144},{17,145}} | collective-permute-start | bytes 589832 | tf_op jit(solution)/shard_map/ppermute | solution.py:32
  28.5 39.0 %collective-permute-start.13 = (f32[256,512]{1,0:T(8,128)S(1)}, f32[256,512]{1,0:T(8,128)}, u32[]{:S(2)}, u32[]{:S(2)}) collective-permute-start(f32[256,512]{1,0:T(8,128)S(1)} %copy-done), channel_id=1, source_target_pairs={{2,128},{3,129},{4,130},{5,131},{6,132},{7,133},{8,134},{9,135},{1... | collective-permute-start | bytes 1572872 | tf_op jit(solution)/shard_map/ppermute | solution.py:332
  33.7 33.8 %collective-permute-start.12 = (f32[256,512]{1,0:T(8,128)S(1)}, f32[256,512]{1,0:T(8,128)}, u32[]{:S(2)}, u32[]{:S(2)}) collective-permute-start(f32[256,512]{1,0:T(8,128)S(1)} %copy-done), channel_id=1, source_target_pairs={{2,0},{3,1},{4,2},{5,3},{6,4},{7,5},{8,6},{9,7},{10,8},{11,9},{12,... | collective-permute-start | bytes 1572872 | tf_op jit(solution)/shard_map/ppermute | solution.py:332
  40.3 8.7 %collective-permute-start.6 = (f32[128,384]{1,0:T(8,128)S(1)}, f32[128,384]{1,0:T(8,128)S(1)}, u32[]{:S(2)}, u32[]{:S(2)}) collective-permute-start(f32[128,384]{1,0:T(8,128)S(1)} %broadcast_select_fusion.10), channel_id=1, source_target_pairs={{0,8},{128,136},{1,9},{129,137},{16,24},{144,152},{17,25},{145,153}} | collective-permute-start | bytes 589832 | tf_op jit(solution)/shard_map/ppermute | solution.py:32
  41.6 13.7 %collective-permute-start.7 = (f32[256,512]{1,0:T(8,128)}, f32[256,512]{1,0:T(8,128)S(1)}, u32[]{:S(2)}, u32[]{:S(2)}) collective-permute-start(f32[256,512]{1,0:T(8,128)} %collective-permute-done.4), channel_id=1, source_target_pairs={{4,8},{8,12},{132,136},{136,140},{5,9},{9,13},{133,137},{137,141},... | collective-permute-start | bytes 1572872 | tf_op jit(solution)/shard_map/ppermute | solution.py:32
  42.3 14.9 %collective-permute-start.8 = (f32[256,512]{1,0:T(8,128)}, f32[256,512]{1,0:T(8,128)}, u32[]{:S(2)}, u32[]{:S(2)}) collective-permute-start(f32[256,512]{1,0:T(8,128)} %collective-permute-done.5), channel_id=1, source_target_pairs={{4,0},{8,4},{132,128},{136,132},{5,1},{9,5},{133,129},{137,133},{6... | collective-permute-start | bytes 1572872 | tf_op jit(solution)/shard_map/ppermute | solution.py:32
  44.4 2.9 %copy-start.10 = (s32[8]{0:T(128)}, s32[8]{0:T(128)S(1)}, u32[]{:S(2)}) copy-start(s32[8]{0:T(128)S(1)} %select_reduce_fusion.5) | copy-start | bytes 100
  49.1 6.3 %collective-permute-start.9 = (s32[1,8]{1,0:T(1,128)S(1)}, s32[1,8]{1,0:T(1,128)S(1)}, u32[]{:S(2)}, u32[]{:S(2)}) collective-permute-start(s32[1,8]{1,0:T(1,128)S(1)} %copy-done.8), channel_id=1, source_target_pairs={{0,128},{4,132},{8,136},{12,140},{128,0},{132,4},{136,8},{140,12},... | collective-permute-start | bytes 104 | tf_op jit(solution)/shard_map/ppermute | solution.py:32
  55.4 18.6 %copy-start.6 = (f32[256,512]{1,0:T(8,128)}, f32[256,512]{1,0:T(8,128)S(1)}, u32[]{:S(2)}) copy-start(f32[256,512]{1,0:T(8,128)S(1)} %collective-permute-done.7) | copy-start | bytes 1572868
  59.9 5.3 %copy-start.9 = (s32[16]{0:T(128)S(1)}, s32[16]{0:T(128)}, u32[]{:S(2)}) copy-start(s32[16]{0:T(128)} %get-tuple-element.71) | copy-start | bytes 196
  60.0 7.5 %collective-permute-start.10 = (f32[128,384]{1,0:T(8,128)S(1)}, f32[128,384]{1,0:T(8,128)S(1)}, u32[]{:S(2)}, u32[]{:S(2)}) collective-permute-start(f32[128,384]{1,0:T(8,128)S(1)} %broadcast_select_fusion.11), channel_id=1, source_target_pairs={{0,4},{8,12},{128,132},{136,140},{1,5},{9,13},{129,133},{137,141},... | collective-permute-start | bytes 589832 | tf_op jit(solution)/shard_map/ppermute | solution.py:32
  63.3 10.7 %collective-permute-start.11 = (f32[256,512]{1,0:T(8,128)}, f32[256,512]{1,0:T(8,128)}, u32[]{:S(2)}, u32[]{:S(2)}) collective-permute-start(f32[256,512]{1,0:T(8,128)} %broadcast_select_fusion.5), channel_id=1, source_target_pairs={{4,0},{8,12},{132,128},{136,140},{5,1},{9,13},{133,129},{137,141},... | collective-permute-start | bytes 1572872 | tf_op jit(solution)/shard_map/ppermute | solution.py:32
  73.9 4.0 %collective-permute-start.14 = (f32[128,384]{1,0:T(8,128)S(1)}, f32[128,384]{1,0:T(8,128)S(1)}, u32[]{:S(2)}, u32[]{:S(2)}) collective-permute-start(f32[128,384]{1,0:T(8,128)S(1)} %broadcast_select_fusion.12), channel_id=1, source_target_pairs={{0,2},{4,6},{8,10},{12,14},{128,130},{132,134},{136,138},{140,142}... | collective-permute-start | bytes 589832 | tf_op jit(solution)/shard_map/ppermute | solution.py:32
  75.2 6.0 %copy-start.7 = (f32[256,512]{1,0:T(8,128)S(1)}, f32[256,512]{1,0:T(8,128)}, u32[]{:S(2)}) copy-start(f32[256,512]{1,0:T(8,128)} %copy-done.6) | copy-start | bytes 1572868
  76.5 9.6 %collective-permute-start.16 = (f32[256,512]{1,0:T(8,128)S(1)}, f32[256,512]{1,0:T(8,128)}, u32[]{:S(2)}, u32[]{:S(2)}) collective-permute-start(f32[256,512]{1,0:T(8,128)S(1)} %broadcast_select_fusion.3), channel_id=1, source_target_pairs={{0,64},{4,68},{8,72},{12,76},{128,192},{132,196},{136,200},{140,20... | collective-permute-start | bytes 1572872 | tf_op jit(solution)/shard_map/ppermute | solution.py:32
  78.0 8.0 %collective-permute-start.15 = (f32[128,384]{1,0:T(8,128)S(1)}, f32[128,384]{1,0:T(8,128)S(1)}, u32[]{:S(2)}, u32[]{:S(2)}) collective-permute-start(f32[128,384]{1,0:T(8,128)S(1)} %broadcast_select_fusion.13), channel_id=1, source_target_pairs={{0,1},{4,5},{8,9},{12,13},{128,129},{132,133},{136,137},{140,141},... | collective-permute-start | bytes 589832 | tf_op jit(solution)/shard_map/ppermute | solution.py:32
  87.0 11.0 %collective-permute-start.17 = (f32[2,128,384]{2,1,0:T(8,128)S(1)}, f32[2,128,384]{2,1,0:T(8,128)}, u32[]{:S(2)}, u32[]{:S(2)}) collective-permute-start(f32[2,128,384]{2,1,0:T(8,128)S(1)} %pad_maximum_fusion.3), channel_id=1, source_target_pairs={{0,64},{4,68},{8,72},{12,76},{128,192},{132,196},{136,200},{140,20... | collective-permute-start | bytes 1179656 | tf_op jit(solution)/shard_map/ppermute | solution.py:32
  89.1 8.9 %collective-permute-start.18 = (f32[256,512]{1,0:T(8,128)S(1)}, f32[256,512]{1,0:T(8,128)}, u32[]{:S(2)}, u32[]{:S(2)}) collective-permute-start(f32[256,512]{1,0:T(8,128)S(1)} %copy-done.5), channel_id=1, source_target_pairs={{0,32},{4,36},{8,40},{12,44},{128,160},{132,164},{136,168},{140,17... | collective-permute-start | bytes 1572872 | tf_op jit(solution)/shard_map/ppermute | solution.py:32
  90.6 74.3 %collective-permute-start.22 = (f32[1536,256]{1,0:T(8,128)}, f32[1536,256]{1,0:T(8,128)}, u32[]{:S(2)}, u32[]{:S(2)}) collective-permute-start(f32[1536,256]{1,0:T(8,128)} %shard_map.77), channel_id=1, source_target_pairs={{0,128},{4,132},{8,136},{12,140},{128,0},{132,4},{136,8},{140,12},... | collective-permute-start | bytes 4718600 | tf_op jit(solution)/shard_map/ppermute | solution.py:32
  98.9 10.2 %collective-permute-start.19 = (f32[2,128,384]{2,1,0:T(8,128)S(1)}, f32[2,128,384]{2,1,0:T(8,128)S(1)}, u32[]{:S(2)}, u32[]{:S(2)}) collective-permute-start(f32[2,128,384]{2,1,0:T(8,128)S(1)} %broadcast_select_fusion.6), channel_id=1, source_target_pairs={{0,32},{4,36},{8,40},{12,44},{128,160},{132,164},{136,168},{140,17... | collective-permute-start | bytes 1179656 | tf_op jit(solution)/shard_map/ppermute | solution.py:32
  100.2 26.2 %collective-permute-start.21 = (f32[256,512]{1,0:T(8,128)}, f32[256,512]{1,0:T(8,128)S(1)}, u32[]{:S(2)}, u32[]{:S(2)}) collective-permute-start(f32[256,512]{1,0:T(8,128)} %broadcast_select_fusion.1), channel_id=1, source_target_pairs={{0,16},{4,20},{8,24},{12,28},{128,144},{132,148},{136,152},{140,15... | collective-permute-start | bytes 1572872 | tf_op jit(solution)/shard_map/ppermute | solution.py:32
  109.1 18.8 %collective-permute-start.20 = (f32[2,128,384]{2,1,0:T(8,128)S(1)}, f32[2,128,384]{2,1,0:T(8,128)}, u32[]{:S(2)}, u32[]{:S(2)}) collective-permute-start(f32[2,128,384]{2,1,0:T(8,128)S(1)} %broadcast_select_fusion.7), channel_id=1, source_target_pairs={{0,16},{4,20},{8,24},{12,28},{128,144},{132,148},{136,152},{140,15... | collective-permute-start | bytes 1179656 | tf_op jit(solution)/shard_map/ppermute | solution.py:32
  129.1 35.9 %copy-start.11 = (s32[8]{0:T(128)S(1)}, s32[8]{0:T(128)}, u32[]{:S(2)}) copy-start(s32[8]{0:T(128)} %copy-done.10) | copy-start | bytes 100
  (4 other events, 4.3 us)
Sparse Core Ops, SparseCore 0:
  9.8 41.8 all-gather.2
  87.1 74.7 all-gather.4

commit v9 on v8

--- a/solution.py
+++ b/solution.py
@@ -440,9 +440,8 @@
     far = gather_y(slots)
     window = window_x(window, x, 1)
     held = pivot_spread(held, (4,), x, y, z)
-    held, window = tie((held, window))
+    held = pivot_spread(held, (5,), x, y, z)
     window = window_core(window, core)
-    held = pivot_spread(held, (5,), x, y, z)
     parts = join_core(held, core)
     inverse = pivot_inverse(parts)
     factor, weights = solve(inverse, panel, window)

time: 185 us -> 188 us (1.016)
  starting transfers between devices: 69.5 us -> 62.9 us
  waiting for transfers between devices: 30 us -> 36.6 us
  Pallas kernels: 43.7 us -> 45.9 us
    ppermute x19, starting transfers between devices: 58.5 us -> 51.9 us  [send(): return lax.ppermute(value, ALL, pairs_of(move))]
    ppermute x19, waiting for transfers between devices: 29.3 us -> 35.9 us  [send(): return lax.ppermute(value, ALL, pairs_of(move))]
    pallas_call x1, Pallas kernels: 10.7 us -> 12.9 us  [update(): pl.pallas_call(update_kernel, in_specs=[pl.BlockSpec(memory_space=pltpu.S...]
  transfers between devices with their start and end apart: 23 -> 23, of which waited for: 8 -> 8; matrix products, arithmetic and copies ran while one was open for 12% -> 11% of each run, Pallas kernels for 18% -> 18%
where the time goes in v9:
time: 188 us; the launch traced here: 185 us
  starting transfers between devices  62.9 us (33%)
  Pallas kernels  45.9 us (24%)
  waiting for transfers between devices  36.6 us (19%)
  other arithmetic  17.3 us (9%)
  between operations  16.1 us (9%)
  local copies, waits for them, and re-layouts  6.02 us (3%)
    ppermute x19, starting transfers between devices, send(): return lax.ppermute(value, ALL, pairs_of(move))  51.9 us
    ppermute x19, waiting for transfers between devices, send(): return lax.ppermute(value, ALL, pairs_of(move))  35.9 us
    pallas_call x1, Pallas kernels, pivot_inverse(): pl.pallas_call(pivot_kernel, out_shape=jax.ShapeDtypeStruct((width, width...  27.1 us
    pallas_call x1, Pallas kernels, update(): pl.pallas_call(update_kernel, in_specs=[pl.BlockSpec(memory_space=pltpu.S...  12.9 us
    ppermute x2, starting transfers between devices, window_owned(): return lax.ppermute(panel, ALL, sorted(place.items()))  10.9 us
  transfers between devices with their start and end apart: 23, of which 8 were waited for; matrix products, arithmetic and copies ran while one was open for 11% of the time, Pallas kernels for 18%

profile of v9, /device:TPU:1, one launch (start us, length us, event | category | flops | bytes accessed | tf_op | source)
XLA Modules:
  0.0 184.8 jit_solution(8422316904848410508)
XLA Ops:
  8.0 5.2 %collective-permute-start.4 = (f32[256,512]{1,0:T(8,128)}, f32[256,512]{1,0:T(8,128)}, u32[]{:S(2)}, u32[]{:S(2)}) collective-permute-start(f32[256,512]{1,0:T(8,128)} %panel_ref.1), channel_id=1, source_target_pairs={{0,4},{4,8},{8,12},{128,132},{132,136},{136,140},{1,5},{5,9},{9,13... | collective-permute-start | bytes 1572872 | tf_op jit(solution)/shard_map/ppermute | solution.py:32
  13.2 1.3 collective-permute-start.5
  16.5 1.4 collective-permute-start.2
  20.7 7.3 %collective-permute-start.3 = (f32[128,384]{1,0:T(8,128)S(1)}, f32[128,384]{1,0:T(8,128)S(1)}, u32[]{:S(2)}, u32[]{:S(2)}) collective-permute-start(f32[128,384]{1,0:T(8,128)S(1)} %slice_select_fusion), channel_id=1, source_target_pairs={{0,128},{1,129},{16,144},{17,145}} | collective-permute-start | bytes 589832 | tf_op jit(solution)/shard_map/ppermute | solution.py:32
  28.5 5.2 %collective-permute-start.13 = (f32[256,512]{1,0:T(8,128)S(1)}, f32[256,512]{1,0:T(8,128)}, u32[]{:S(2)}, u32[]{:S(2)}) collective-permute-start(f32[256,512]{1,0:T(8,128)S(1)} %copy-done), channel_id=1, source_target_pairs={{2,128},{3,129},{4,130},{5,131},{6,132},{7,133},{8,134},{9,135},{1... | collective-permute-start | bytes 1572872 | tf_op jit(solution)/shard_map/ppermute | solution.py:332
  33.7 5.7 %collective-permute-start.12 = (f32[256,512]{1,0:T(8,128)S(1)}, f32[256,512]{1,0:T(8,128)}, u32[]{:S(2)}, u32[]{:S(2)}) collective-permute-start(f32[256,512]{1,0:T(8,128)S(1)} %copy-done), channel_id=1, source_target_pairs={{2,0},{3,1},{4,2},{5,3},{6,4},{7,5},{8,6},{9,7},{10,8},{11,9},{12,... | collective-permute-start | bytes 1572872 | tf_op jit(solution)/shard_map/ppermute | solution.py:332
  40.3 1.3 collective-permute-start.6
  42.3 1.3 collective-permute-start.8
  44.4 2.9 %shard_map.77 = f32[1536,256]{1,0:T(8,128)} custom-call(s32[6]{0:T(128)S(1)} %bitcast.54, f32[2048,256]{1,0:T(8,128)S(1)} %bitcast.46), custom_call_target="tpu_custom_call" | custom-call | tf_op jit(solution)/shard_map/pallas_call | solution.py:165
  49.6 5.8 %collective-permute-done.9 = s32[1,8]{1,0:T(1,128)S(1)} collective-permute-done((s32[1,8]{1,0:T(1,128)S(1)}, s32[1,8]{1,0:T(1,128)S(1)}, u32[]{:S(2)}, u32[]{:S(2)}) %collective-permute-start.9) | collective-permute-done | bytes 64 | tf_op jit(solution)/shard_map/ppermute | solution.py:32
  55.4 1.8 collective-permute-done.8
  60.0 1.3 collective-permute-start.10
  61.3 1.9 %broadcast_select_fusion.5 = f32[256,512]{1,0:T(8,128)} fusion(f32[256,512]{1,0:T(8,128)S(1)} %collective-permute-done.7, f32[256,512]{1,0:T(8,128)} %collective-permute-done.8, pred[]{:T(512)S(6)} %eq.173), kind=kLoop, calls=%fused_computation.12 | loop fusion | flops 131072 | bytes 1572865 | tf_op jit(solution)/shard_map/jit(_where)/select_n | solution.py:391
  63.3 1.3 collective-permute-start.11
  66.3 1.3 stack.11.table
  67.6 6.3 %collective-permute-done.11 = f32[256,512]{1,0:T(8,128)} collective-permute-done((f32[256,512]{1,0:T(8,128)}, f32[256,512]{1,0:T(8,128)}, u32[]{:S(2)}, u32[]{:S(2)}) %collective-permute-start.11) | collective-permute-done | bytes 524320 | tf_op jit(solution)/shard_map/ppermute | solution.py:32
  73.9 1.3 collective-permute-start.14
  76.5 1.5 collective-permute-start.16
  78.0 3.3 %collective-permute-start.15 = (f32[128,384]{1,0:T(8,128)S(1)}, f32[128,384]{1,0:T(8,128)S(1)}, u32[]{:S(2)}, u32[]{:S(2)}) collective-permute-start(f32[128,384]{1,0:T(8,128)S(1)} %broadcast_select_fusion.13), channel_id=1, source_target_pairs={{0,1},{4,5},{8,9},{12,13},{128,129},{132,133},{136,137},{140,141},... | collective-permute-start | bytes 589832 | tf_op jit(solution)/shard_map/ppermute | solution.py:32
  81.3 1.8 select_select_fusion.1
  84.3 1.6 collective-permute-done.15
  87.0 2.2 %collective-permute-start.17 = (f32[2,128,384]{2,1,0:T(8,128)S(1)}, f32[2,128,384]{2,1,0:T(8,128)}, u32[]{:S(2)}, u32[]{:S(2)}) collective-permute-start(f32[2,128,384]{2,1,0:T(8,128)S(1)} %pad_maximum_fusion.3), channel_id=1, source_target_pairs={{0,64},{4,68},{8,72},{12,76},{128,192},{132,196},{136,200},{140,20... | collective-permute-start | bytes 1179656 | tf_op jit(solution)/shard_map/ppermute | solution.py:32
  89.1 1.5 collective-permute-start.20
  90.6 7.3 %collective-permute-start.22 = (f32[1536,256]{1,0:T(8,128)}, f32[1536,256]{1,0:T(8,128)}, u32[]{:S(2)}, u32[]{:S(2)}) collective-permute-start(f32[1536,256]{1,0:T(8,128)} %shard_map.77), channel_id=1, source_target_pairs={{0,128},{4,132},{8,136},{12,140},{128,0},{132,4},{136,8},{140,12},... | collective-permute-start | bytes 4718600 | tf_op jit(solution)/shard_map/ppermute | solution.py:32
  98.0 1.3 collective-permute-start.18
  101.5 6.5 %collective-permute-done.18 = f32[2,128,384]{2,1,0:T(8,128)S(1)} collective-permute-done((f32[2,128,384]{2,1,0:T(8,128)S(1)}, f32[2,128,384]{2,1,0:T(8,128)S(1)}, u32[]{:S(2)}, u32[]{:S(2)}) %collective-permute-start.18) | collective-permute-done | bytes 393248 | tf_op jit(solution)/shard_map/ppermute | solution.py:32
  108.1 10.7 %collective-permute-start.19 = (f32[2,128,384]{2,1,0:T(8,128)S(1)}, f32[2,128,384]{2,1,0:T(8,128)}, u32[]{:S(2)}, u32[]{:S(2)}) collective-permute-start(f32[2,128,384]{2,1,0:T(8,128)S(1)} %broadcast_select_fusion.7), channel_id=1, source_target_pairs={{0,16},{4,20},{8,24},{12,28},{128,144},{132,148},{136,152},{140,15... | collective-permute-start | bytes 1179656 | tf_op jit(solution)/shard_map/ppermute | solution.py:32
  118.9 1.4 collective-permute-done.19
  121.4 27.1 %shard_map.78.inverse_ref = f32[512,512]{1,0:T(8,128)S(1)} custom-call(f32[2,256,384]{2,1,0:T(8,128)S(1)} %pad_maximum_fusion.2.parts_ref), custom_call_target="tpu_custom_call" | custom-call | tf_op jit(solution)/shard_map/pallas_call | solution.py:116
  148.5 3.0 %shard_map.79 = (f32[256,512]{1,0:T(8,128)}, bf16[512,256]{1,0:T(8,128)(2,1)S(1)}, bf16[512,256]{1,0:T(8,128)(2,1)S(1)}, bf16[512,256]{1,0:T(8,128)(2,1)S(1)}) custom-call(f32[512,512]{1,0:T(8,128)S(1)} %shard_map.78.inverse_ref, f32[256,512]{1,0:T(8,128)S(1)} %copy-done, f32[256,512]{1,0:T(8,128)S(1)} %broadcast_select_fusion.1.window_ref), custom_call_target="tpu_custom_call" | custom-call | tf_op jit(solution)/shard_map/pallas_call | solution.py:151
  153.6 11.3 %collective-permute-done.22.main = f32[1536,256]{1,0:T(8,128)} collective-permute-done((f32[1536,256]{1,0:T(8,128)}, f32[1536,256]{1,0:T(8,128)}, u32[]{:S(2)}, u32[]{:S(2)}) %collective-permute-start.22) | collective-permute-done | bytes 1572896 | tf_op jit(solution)/shard_map/ppermute | solution.py:32
  165.0 12.9 %shard_map.80 = f32[4096,256]{1,0:T(8,128)} custom-call(s32[8,16]{1,0:T(8,128)} %stack.11.table, bf16[512,256]{1,0:T(8,128)(2,1)} %copy-done.1, bf16[512,256]{1,0:T(8,128)(2,1)} %copy-done.2, bf16[512,256]{1,0:T(8,128)(2,1)} %copy-done.3, f32[1024,512]{1,0:T(8,128)} %all-gather.3.cloned.1.call-done.near, f32[3072,512]{1,0:T(8,128)} %all-gather.5.cloned.1.call-done.far, ...), custom_call_target="tpu_custom_call" | custom-call | tf_op jit(solution)/shard_map/pallas_call | solution.py:237
  (108 shorter events, 22.8 us)
Async XLA Ops:
  7.2 9.2 %copy-start = (f32[256,512]{1,0:T(8,128)S(1)}, f32[256,512]{1,0:T(8,128)}, u32[]{:S(2)}) copy-start(f32[256,512]{1,0:T(8,128)} %panel_ref.1) | copy-start | bytes 1572868
  7.2 11.6 %copy-start.12 = (s32[16,1]{0,1:T(1,128)S(1)}, s32[16,1]{0,1:T(1,128)}, u32[]{:S(2)}) copy-start(s32[16,1]{0,1:T(1,128)} %param.14) | copy-start | bytes 196
  7.2 79.8 %all-gather.3.cloned.1.call-start = ((), (), s32[]{:S(2)}) async-start(), calls=%async_computation | async-start | bytes 2621440 | tf_op jit(solution)/shard_map/all_gather | solution.py:349
  7.9 157.1 %all-gather.5.cloned.1.call-start = ((), (), s32[]{:S(2)}) async-start(), calls=%async_computation.1 | async-start | bytes 7864320 | tf_op jit(solution)/shard_map/all_gather | solution.py:349
  8.0 31.5 %collective-permute-start.4 = (f32[256,512]{1,0:T(8,128)}, f32[256,512]{1,0:T(8,128)}, u32[]{:S(2)}, u32[]{:S(2)}) collective-permute-start(f32[256,512]{1,0:T(8,128)} %panel_ref.1), channel_id=1, source_target_pairs={{0,4},{4,8},{8,12},{128,132},{132,136},{136,140},{1,5},{5,9},{9,13... | collective-permute-start | bytes 1572872 | tf_op jit(solution)/shard_map/ppermute | solution.py:32
  13.2 26.4 %collective-permute-start.5 = (f32[256,512]{1,0:T(8,128)}, f32[256,512]{1,0:T(8,128)}, u32[]{:S(2)}, u32[]{:S(2)}) collective-permute-start(f32[256,512]{1,0:T(8,128)} %panel_ref.1), channel_id=1, source_target_pairs={{4,0},{8,4},{12,8},{132,128},{136,132},{140,136},{5,1},{9,5},{13,9... | collective-permute-start | bytes 1572872 | tf_op jit(solution)/shard_map/ppermute | solution.py:32
  16.3 23.2 %copy-start.8 = (s32[1,8]{1,0:T(1,128)S(1)}, s32[1,8]{1,0:T(1,128)}, u32[]{:S(2)}) copy-start(s32[1,8]{1,0:T(1,128)} %param.13) | copy-start | bytes 100
  16.3 28.0 %copy-start.4 = (f32[1,2048,256]{2,1,0:T(8,128)S(1)}, f32[1,2048,256]{2,1,0:T(8,128)}, u32[]{:S(2)}) copy-start(f32[1,2048,256]{2,1,0:T(8,128)} %param.12) | copy-start | bytes 6291460
  16.5 4.2 %collective-permute-start.2 = (f32[128,384]{1,0:T(8,128)S(1)}, f32[128,384]{1,0:T(8,128)S(1)}, u32[]{:S(2)}, u32[]{:S(2)}) collective-permute-start(f32[128,384]{1,0:T(8,128)S(1)} %slice.55), channel_id=1, source_target_pairs={{0,16},{1,17}} | collective-permute-start | bytes 589832 | tf_op jit(solution)/shard_map/ppermute | solution.py:32
  20.7 18.8 %collective-permute-start.3 = (f32[128,384]{1,0:T(8,128)S(1)}, f32[128,384]{1,0:T(8,128)S(1)}, u32[]{:S(2)}, u32[]{:S(2)}) collective-permute-start(f32[128,384]{1,0:T(8,128)S(1)} %slice_select_fusion), channel_id=1, source_target_pairs={{0,128},{1,129},{16,144},{17,145}} | collective-permute-start | bytes 589832 | tf_op jit(solution)/shard_map/ppermute | solution.py:32
  28.5 39.0 %collective-permute-start.13 = (f32[256,512]{1,0:T(8,128)S(1)}, f32[256,512]{1,0:T(8,128)}, u32[]{:S(2)}, u32[]{:S(2)}) collective-permute-start(f32[256,512]{1,0:T(8,128)S(1)} %copy-done), channel_id=1, source_target_pairs={{2,128},{3,129},{4,130},{5,131},{6,132},{7,133},{8,134},{9,135},{1... | collective-permute-start | bytes 1572872 | tf_op jit(solution)/shard_map/ppermute | solution.py:332
  33.7 33.8 %collective-permute-start.12 = (f32[256,512]{1,0:T(8,128)S(1)}, f32[256,512]{1,0:T(8,128)}, u32[]{:S(2)}, u32[]{:S(2)}) collective-permute-start(f32[256,512]{1,0:T(8,128)S(1)} %copy-done), channel_id=1, source_target_pairs={{2,0},{3,1},{4,2},{5,3},{6,4},{7,5},{8,6},{9,7},{10,8},{11,9},{12,... | collective-permute-start | bytes 1572872 | tf_op jit(solution)/shard_map/ppermute | solution.py:332
  40.3 8.7 %collective-permute-start.6 = (f32[128,384]{1,0:T(8,128)S(1)}, f32[128,384]{1,0:T(8,128)S(1)}, u32[]{:S(2)}, u32[]{:S(2)}) collective-permute-start(f32[128,384]{1,0:T(8,128)S(1)} %broadcast_select_fusion.10), channel_id=1, source_target_pairs={{0,8},{128,136},{1,9},{129,137},{16,24},{144,152},{17,25},{145,153}} | collective-permute-start | bytes 589832 | tf_op jit(solution)/shard_map/ppermute | solution.py:32
  41.6 13.7 %collective-permute-start.7 = (f32[256,512]{1,0:T(8,128)}, f32[256,512]{1,0:T(8,128)S(1)}, u32[]{:S(2)}, u32[]{:S(2)}) collective-permute-start(f32[256,512]{1,0:T(8,128)} %collective-permute-done.4), channel_id=1, source_target_pairs={{4,8},{8,12},{132,136},{136,140},{5,9},{9,13},{133,137},{137,141},... | collective-permute-start | bytes 1572872 | tf_op jit(solution)/shard_map/ppermute | solution.py:32
  42.3 14.9 %collective-permute-start.8 = (f32[256,512]{1,0:T(8,128)}, f32[256,512]{1,0:T(8,128)}, u32[]{:S(2)}, u32[]{:S(2)}) collective-permute-start(f32[256,512]{1,0:T(8,128)} %collective-permute-done.5), channel_id=1, source_target_pairs={{4,0},{8,4},{132,128},{136,132},{5,1},{9,5},{133,129},{137,133},{6... | collective-permute-start | bytes 1572872 | tf_op jit(solution)/shard_map/ppermute | solution.py:32
  44.4 2.9 %copy-start.10 = (s32[8]{0:T(128)}, s32[8]{0:T(128)S(1)}, u32[]{:S(2)}) copy-start(s32[8]{0:T(128)S(1)} %select_reduce_fusion.5) | copy-start | bytes 100
  49.1 6.3 %collective-permute-start.9 = (s32[1,8]{1,0:T(1,128)S(1)}, s32[1,8]{1,0:T(1,128)S(1)}, u32[]{:S(2)}, u32[]{:S(2)}) collective-permute-start(s32[1,8]{1,0:T(1,128)S(1)} %copy-done.8), channel_id=1, source_target_pairs={{0,128},{4,132},{8,136},{12,140},{128,0},{132,4},{136,8},{140,12},... | collective-permute-start | bytes 104 | tf_op jit(solution)/shard_map/ppermute | solution.py:32
  55.4 18.6 %copy-start.6 = (f32[256,512]{1,0:T(8,128)}, f32[256,512]{1,0:T(8,128)S(1)}, u32[]{:S(2)}) copy-start(f32[256,512]{1,0:T(8,128)S(1)} %collective-permute-done.7) | copy-start | bytes 1572868
  59.9 5.3 %copy-start.9 = (s32[16]{0:T(128)S(1)}, s32[16]{0:T(128)}, u32[]{:S(2)}) copy-start(s32[16]{0:T(128)} %get-tuple-element.69) | copy-start | bytes 196
  60.0 7.5 %collective-permute-start.10 = (f32[128,384]{1,0:T(8,128)S(1)}, f32[128,384]{1,0:T(8,128)S(1)}, u32[]{:S(2)}, u32[]{:S(2)}) collective-permute-start(f32[128,384]{1,0:T(8,128)S(1)} %broadcast_select_fusion.11), channel_id=1, source_target_pairs={{0,4},{8,12},{128,132},{136,140},{1,5},{9,13},{129,133},{137,141},... | collective-permute-start | bytes 589832 | tf_op jit(solution)/shard_map/ppermute | solution.py:32
  63.3 10.7 %collective-permute-start.11 = (f32[256,512]{1,0:T(8,128)}, f32[256,512]{1,0:T(8,128)}, u32[]{:S(2)}, u32[]{:S(2)}) collective-permute-start(f32[256,512]{1,0:T(8,128)} %broadcast_select_fusion.5), channel_id=1, source_target_pairs={{4,0},{8,12},{132,128},{136,140},{5,1},{9,13},{133,129},{137,141},... | collective-permute-start | bytes 1572872 | tf_op jit(solution)/shard_map/ppermute | solution.py:32
  73.9 4.0 %collective-permute-start.14 = (f32[128,384]{1,0:T(8,128)S(1)}, f32[128,384]{1,0:T(8,128)S(1)}, u32[]{:S(2)}, u32[]{:S(2)}) collective-permute-start(f32[128,384]{1,0:T(8,128)S(1)} %broadcast_select_fusion.12), channel_id=1, source_target_pairs={{0,2},{4,6},{8,10},{12,14},{128,130},{132,134},{136,138},{140,142}... | collective-permute-start | bytes 589832 | tf_op jit(solution)/shard_map/ppermute | solution.py:32
  75.2 6.0 %copy-start.7 = (f32[256,512]{1,0:T(8,128)S(1)}, f32[256,512]{1,0:T(8,128)}, u32[]{:S(2)}) copy-start(f32[256,512]{1,0:T(8,128)} %copy-done.6) | copy-start | bytes 1572868
  76.5 9.6 %collective-permute-start.16 = (f32[256,512]{1,0:T(8,128)S(1)}, f32[256,512]{1,0:T(8,128)}, u32[]{:S(2)}, u32[]{:S(2)}) collective-permute-start(f32[256,512]{1,0:T(8,128)S(1)} %broadcast_select_fusion.3), channel_id=1, source_target_pairs={{0,64},{4,68},{8,72},{12,76},{128,192},{132,196},{136,200},{140,20... | collective-permute-start | bytes 1572872 | tf_op jit(solution)/shard_map/ppermute | solution.py:32
  78.0 8.0 %collective-permute-start.15 = (f32[128,384]{1,0:T(8,128)S(1)}, f32[128,384]{1,0:T(8,128)S(1)}, u32[]{:S(2)}, u32[]{:S(2)}) collective-permute-start(f32[128,384]{1,0:T(8,128)S(1)} %broadcast_select_fusion.13), channel_id=1, source_target_pairs={{0,1},{4,5},{8,9},{12,13},{128,129},{132,133},{136,137},{140,141},... | collective-permute-start | bytes 589832 | tf_op jit(solution)/shard_map/ppermute | solution.py:32
  87.0 11.0 %collective-permute-start.17 = (f32[2,128,384]{2,1,0:T(8,128)S(1)}, f32[2,128,384]{2,1,0:T(8,128)}, u32[]{:S(2)}, u32[]{:S(2)}) collective-permute-start(f32[2,128,384]{2,1,0:T(8,128)S(1)} %pad_maximum_fusion.3), channel_id=1, source_target_pairs={{0,64},{4,68},{8,72},{12,76},{128,192},{132,196},{136,200},{140,20... | collective-permute-start | bytes 1179656 | tf_op jit(solution)/shard_map/ppermute | solution.py:32
  89.1 10.2 %collective-permute-start.20 = (f32[256,512]{1,0:T(8,128)S(1)}, f32[256,512]{1,0:T(8,128)}, u32[]{:S(2)}, u32[]{:S(2)}) collective-permute-start(f32[256,512]{1,0:T(8,128)S(1)} %copy-done.5), channel_id=1, source_target_pairs={{0,32},{4,36},{8,40},{12,44},{128,160},{132,164},{136,168},{140,17... | collective-permute-start | bytes 1572872 | tf_op jit(solution)/shard_map/ppermute | solution.py:32
  90.6 74.3 %collective-permute-start.22 = (f32[1536,256]{1,0:T(8,128)}, f32[1536,256]{1,0:T(8,128)}, u32[]{:S(2)}, u32[]{:S(2)}) collective-permute-start(f32[1536,256]{1,0:T(8,128)} %shard_map.77), channel_id=1, source_target_pairs={{0,128},{4,132},{8,136},{12,140},{128,0},{132,4},{136,8},{140,12},... | collective-permute-start | bytes 4718600 | tf_op jit(solution)/shard_map/ppermute | solution.py:32
  98.0 10.0 %collective-permute-start.18 = (f32[2,128,384]{2,1,0:T(8,128)S(1)}, f32[2,128,384]{2,1,0:T(8,128)S(1)}, u32[]{:S(2)}, u32[]{:S(2)}) collective-permute-start(f32[2,128,384]{2,1,0:T(8,128)S(1)} %broadcast_select_fusion.6), channel_id=1, source_target_pairs={{0,32},{4,36},{8,40},{12,44},{128,160},{132,164},{136,168},{140,17... | collective-permute-start | bytes 1179656 | tf_op jit(solution)/shard_map/ppermute | solution.py:32
  100.3 18.5 %collective-permute-start.21 = (f32[256,512]{1,0:T(8,128)}, f32[256,512]{1,0:T(8,128)S(1)}, u32[]{:S(2)}, u32[]{:S(2)}) collective-permute-start(f32[256,512]{1,0:T(8,128)} %broadcast_select_fusion), channel_id=1, source_target_pairs={{0,16},{4,20},{8,24},{12,28},{128,144},{132,148},{136,152},{140,15... | collective-permute-start | bytes 1572872 | tf_op jit(solution)/shard_map/ppermute | solution.py:32
  108.1 12.2 %collective-permute-start.19 = (f32[2,128,384]{2,1,0:T(8,128)S(1)}, f32[2,128,384]{2,1,0:T(8,128)}, u32[]{:S(2)}, u32[]{:S(2)}) collective-permute-start(f32[2,128,384]{2,1,0:T(8,128)S(1)} %broadcast_select_fusion.7), channel_id=1, source_target_pairs={{0,16},{4,20},{8,24},{12,28},{128,144},{132,148},{136,152},{140,15... | collective-permute-start | bytes 1179656 | tf_op jit(solution)/shard_map/ppermute | solution.py:32
  121.4 43.5 %copy-start.11 = (s32[8]{0:T(128)S(1)}, s32[8]{0:T(128)}, u32[]{:S(2)}) copy-start(s32[8]{0:T(128)} %copy-done.10) | copy-start | bytes 100
  (4 other events, 4.3 us)
Sparse Core Ops, SparseCore 0:
  9.8 41.8 all-gather.2
  87.1 74.7 all-gather.4
